TPU v7x, 128 devices: a whole 4x4x4 slice. The times are simulated.
128 devices in a mesh: ctx: 16 (over x_hi, y, core), exp: 8 (over z, x_lo).
Axes of the slice: x: 4 (x_hi: 2, x_lo: 2; x = x_hi * 2 + x_lo), y: 4, z: 4, core: 2. Of those that a mesh axis runs over, the one named last changes fastest.
Arguments:
- latent: bfloat16 [2048, 576], P('ctx'), may hold values from -8 to 8
- query: bfloat16 [2048, 12288], P('ctx', 'exp'), may hold values from -8 to 8
- w_uk: bfloat16 [64, 512, 128], P('exp'), may hold values from -0.5 to 0.5
- w_uv: bfloat16 [64, 512, 128], P('exp'), may hold values from -0.25 to 0.25
- w_o: bfloat16 [8192, 4096], P('exp'), may hold values from -0.0625 to 0.0625
- residual: bfloat16 [2048, 4096], P('ctx', 'exp'), may hold values from -16 to 16
- norm_gain: float32 [4096], P('exp'), may hold values from 0.1 to 1.9
- w_in: bfloat16 [32, 4096, 2, 2048], P('ctx', None, None, 'exp'), may hold values from -0.09375 to 0.09375
- w_out: bfloat16 [32, 2048, 4096], P('ctx', 'exp'), may hold values from -0.125 to 0.125
- routes: int32 [2048, 8], P('ctx'), may hold values from 0 to 31, all different within a row; in each aligned block of 128 rows (0 to 127, 128 to 255, ...) at most 48 rows name the same one
- gate_weights: float32 [2048, 8], P('ctx'), may hold values from 0.05 to 0.5
- doc_lengths: int32 [12], replicated, may hold values from 1 to 1152, 2048 in all
Outputs:
- mixed: bfloat16 [2048, 4096], P('ctx', 'exp')
Inputs may be any that keep to these rules, and one draw needn't show every extreme that they name: `routes`: the 128 rows of one index of ctx name each expert at most 48 times in all, a bound that some block reaches.
All inputs are finite; a program needn't handle non-finite values.
Results may differ from a plain program's by a relative error of at most 0.009.
Values may be sent and summed in bfloat16 or wider, within the bound.
No kernel may reach another device: no remote copies, remote signals or barrier semaphores. Data moves between devices by JAX's collectives and lax.ppermute only.
A program may use at most 128 MiB of HBM per device.

v0:
```python
import math

import jax
import jax.numpy as jnp
from jax import lax
from jax.sharding import PartitionSpec as P

D = 4096
NOPE = 128
ROPE = 64
LAT = 512
VDIM = 128
TOP = 8


epsilon = 1e-06


def document(positions, doc_ends):
    return jnp.sum((positions[:, None] >= doc_ends[None, :]).astype(jnp.int32), axis=1)


def expert_mlp(arrived, w_in, w_out, local_experts, capacity):
    sources = arrived.shape[0]
    grouped = arrived.reshape(sources, local_experts, capacity, arrived.shape[2])
    hidden_pre = jnp.einsum("secd,edgf->secgf", grouped, w_in, preferred_element_type=jnp.float32)
    activated = (jax.nn.silu(hidden_pre[:, :, :, 0, :]) * hidden_pre[:, :, :, 1, :]).astype(
        jnp.bfloat16
    )
    partials = jnp.einsum(
        "secf,efd->secd", activated, w_out, preferred_element_type=jnp.float32
    ).astype(jnp.bfloat16)
    return partials.reshape(sources, local_experts * capacity, w_out.shape[2])


def body(
    latent,
    query,
    w_uk,
    w_uv,
    w_o,
    residual,
    norm_gain,
    w_in,
    w_out,
    routes,
    gate_weights,
    doc_lengths,
):
    count_ctx = lax.axis_size("ctx")
    tokens = latent.shape[0]
    heads = w_uk.shape[0]
    qk_width = NOPE + ROPE
    score_scale = 1.0 / math.sqrt(qk_width)
    doc_ends = jnp.cumsum(doc_lengths)
    first_pos = lax.axis_index("ctx") * tokens
    q_pos = first_pos + jnp.arange(tokens, dtype=jnp.int32)
    q_doc = document(q_pos, doc_ends)
    q_rows = query.reshape(tokens, heads, qk_width)
    q_lat = jnp.einsum(
        "thn,hln->htl", q_rows[:, :, :NOPE], w_uk, preferred_element_type=jnp.float32
    ).astype(jnp.bfloat16)
    q_full = jnp.concatenate(
        [q_lat, jnp.transpose(q_rows[:, :, NOPE:], (1, 0, 2))], axis=2
    ).reshape(heads * tokens, LAT + ROPE)
    row_pos = jnp.tile(q_pos, heads)
    row_doc = jnp.tile(q_doc, heads)
    row_count = heads * tokens
    piece = lax.all_gather(latent, "ctx", axis=0, tiled=True)
    key_pos = jnp.arange(piece.shape[0], dtype=jnp.int32)
    key_doc = document(key_pos, doc_ends)
    allowed = (row_doc[:, None] == key_doc[None, :]) & (row_pos[:, None] >= key_pos[None, :])
    row_max = jnp.full((row_count,), -1e30, jnp.float32)
    scores = jnp.dot(q_full, piece.T, preferred_element_type=jnp.float32) * score_scale
    scores = jnp.where(allowed, scores, -1e30)
    new_max = jnp.maximum(row_max, jnp.max(scores, axis=1))
    weights = jnp.where(allowed, jnp.exp(scores - new_max[:, None]), 0.0)
    row_total = jnp.sum(weights, axis=1)
    accumulated = jnp.dot(
        weights.astype(jnp.bfloat16), piece[:, :LAT], preferred_element_type=jnp.float32
    )
    row_max, row_total, accumulated = (new_max, row_total, accumulated)
    o_lat = (accumulated / row_total[:, None]).astype(jnp.bfloat16).reshape(heads, tokens, LAT)
    head_out = (
        jnp.einsum("htl,hlv->thv", o_lat, w_uv, preferred_element_type=jnp.float32)
        .astype(jnp.bfloat16)
        .reshape(tokens, heads * VDIM)
    )
    local_width = residual.shape[1]
    attn_t = lax.psum_scatter(
        lax.dot_general(
            w_o, head_out, (((0,), (1,)), ((), ())), preferred_element_type=jnp.float32
        ).astype(jnp.bfloat16),
        "exp",
        scatter_dimension=0,
        tiled=True,
    ).astype(jnp.float32)
    hidden = residual.astype(jnp.float32) + attn_t.T
    squares = lax.psum(jnp.sum(hidden * hidden, axis=1), "exp")
    normed = (hidden * lax.rsqrt(squares[:, None] / D + epsilon) * norm_gain[None, :]).astype(
        jnp.bfloat16
    )
    local_experts = w_in.shape[0]
    experts = local_experts * count_ctx
    capacity = tokens * TOP * 3 // (2 * experts)
    flat_routes = routes.reshape(-1)
    onehot = (flat_routes[:, None] == jnp.arange(experts, dtype=jnp.int32)[None, :]).astype(
        jnp.int32
    )
    slot_rank = jnp.sum((jnp.cumsum(onehot, axis=0) - onehot) * onehot, axis=1)
    slot_index = flat_routes * capacity + slot_rank
    owner_row = (
        jnp.zeros((experts * capacity,), jnp.int32)
        .at[slot_index]
        .set(jnp.arange(tokens * TOP, dtype=jnp.int32) // TOP)
    )
    filled = jnp.zeros((experts * capacity,), jnp.bool_).at[slot_index].set(True)
    gate_flat = gate_weights.reshape(-1)
    outgoing = jnp.where(filled[:, None], normed[owner_row], jnp.zeros((), jnp.bfloat16)).reshape(
        count_ctx, local_experts * capacity, local_width
    )
    arrived = lax.all_to_all(outgoing, "ctx", split_axis=0, concat_axis=0, tiled=True)
    rows_full = lax.all_gather(arrived, "exp", axis=2, tiled=True)
    partials = expert_mlp(rows_full, w_in, w_out, local_experts, capacity)
    summed = lax.psum_scatter(partials, "exp", scatter_dimension=2, tiled=True).astype(jnp.float32)
    returned = (
        lax.all_to_all(summed.astype(jnp.bfloat16), "ctx", split_axis=0, concat_axis=0, tiled=True)
        .astype(summed.dtype)
        .reshape(experts * capacity, local_width)
    )
    picked = returned[slot_index] * gate_flat[:, None]
    moe_out = jnp.sum(picked.reshape(tokens, TOP, local_width), axis=1)
    return (hidden + moe_out).astype(jnp.bfloat16)


def solution(mesh):
    placed = (
        P("ctx", None),
        P("ctx", "exp"),
        P("exp", None, None),
        P("exp", None, None),
        P("exp", None),
        P("ctx", "exp"),
        P("exp"),
        P("ctx", None, None, "exp"),
        P("ctx", "exp", None),
        P("ctx", None),
        P("ctx", None),
        P(),
    )
    return jax.shard_map(
        body, mesh=mesh, in_specs=placed, out_specs=P("ctx", "exp"), check_vma=False
    )
```

profile of v0, /device:TPU:0, one launch (start us, length us, event | category | flops | bytes accessed | tf_op | source)
XLA Modules:
  0.0 739.5 jit_solution(3180911814520054930)
XLA Ops:
  7.3 1.2 copy.31
  10.4 49.8 %all-gather.3.cloned.1.call-done = bf16[2048,576]{0,1:T(8,128)(2,1)} async-done(((bf16[128,576]{0,1:T(8,128)(2,1)}), bf16[2048,576]{0,1:T(8,128)(2,1)}) %all-gather.3.cloned.1.call-update) | async-done | bytes 2359312 | tf_op jit(solution)/shard_map/all_gather | solution.py:69
  60.2 5.9 fusion.4
  66.1 3.5 fusion.6
  69.6 3.6 divide_convert_fusion
  73.8 2.3 fusion.5
  76.6 9.0 %reduce-window.19 = s32[32,8,128]{2,1,0:T(8,128)S(1)} reduce-window(s32[32,8,128]{2,1,0:T(8,128)S(1)} %fusion.30, s32[]{:T(128)} %constant.24.clone.1), window={size=1x1x128 pad=0_0x0_0x127_0}, to_apply=%region_6.7 | reduce-window | flops 4161536 | bytes 262148 | tf_op jit(solution)/shard_map/reduce-window.1
  86.4 4.3 scatter_custom_fusion.1
  90.7 4.3 scatter_custom_fusion
  95.2 20.4 %reduce-scatter.3.cloned.1.call-done = bf16[512,128]{0,1:T(8,128)(2,1)} async-done(((bf16[4096,128]{0,1:T(8,128)(2,1)}), bf16[512,128]{0,1:T(8,128)(2,1)}) %reduce-scatter.3.cloned.1.call-update) | async-done | bytes 131088 | tf_op jit(solution)/shard_map/reduce_scatter | solution.py:90
  115.6 1.0 multiply_reduce_fusion
  116.7 16.8 %psum.7 = f32[128]{0:T(128)S(1)} all-reduce(f32[128]{0:T(128)S(1)} %multiply_reduce_fusion), channel_id=1, replica_groups=mesh['ctx'=16,'exp'=8] {'exp'}, use_global_device_ids=true, to_apply=%region_11.12 | all-reduce | flops 128 | bytes 1024 | tf_op jit(solution)/shard_map/psum | solution.py:99
  133.4 1.0 multiply_convert_fusion
  134.4 4.8 gather_fusion
  139.5 30.3 %all_to_all.10 = bf16[16,96,512]{2,1,0:T(8,128)(2,1)} all-to-all(bf16[16,96,512]{2,1,0:T(8,128)(2,1)S(1)} %broadcast_select_fusion), channel_id=1, replica_groups=mesh['ctx'=16,'exp'=8] {'ctx'}, dimensions={0} | all-to-all | bytes 3145728 | tf_op jit(solution)/shard_map/all_to_all | solution.py:122
  169.9 241.7 %all-gather.5.cloned.1.call-done = bf16[16,96,4096]{2,1,0:T(8,128)(2,1)} async-done(((bf16[16,96,512]{2,1,0:T(8,128)(2,1)}), bf16[16,96,4096]{2,1,0:T(8,128)(2,1)}) %all-gather.5.cloned.1.call-update) | async-done | bytes 12582928 | tf_op jit(solution)/shard_map/all_gather | solution.py:123
  411.6 13.3 %fusion.13 = f32[16,2,48,2,256]{4,2,3,0,1:T(8,128)} fusion(bf16[2,4096,2,256,1]{3,2,1,0,4:T(2,128)(2,1)} %bitcast.105, bf16[16,2,48,4096,1]{3,2,1,0,4:T(8,128)(2,1)} %bitcast.104), kind=kOutput, calls=%fused_computation.23 | convolution fusion | flops 6442450944 | bytes 24117248 | tf_op jit(solution)/shard_map/secd,edgf->secgf/dot_general | solution.py:26
  424.9 8.3 %convert_bitcast_fusion = bf16[16,2,48,4096]{3,2,0,1:T(8,128)(2,1)} fusion(bf16[2,256,4096]{2,1,0:T(8,128)(2,1)S(1)} %copy-done.8, f32[16,2,48,2,256]{4,2,3,0,1:T(8,128)} %fusion.13), kind=kOutput, calls=%fused_computation.6 | convolution fusion | flops 3229876224 | bytes 19922944 | tf_op jit(solution)/shard_map/secf,efd->secd/dot_general | solution.py:30
  433.3 10.6 %copy.43 = bf16[16,2,48,4096]{3,2,1,0:T(8,128)(2,1)} copy(bf16[16,2,48,4096]{3,2,0,1:T(8,128)(2,1)} %convert_bitcast_fusion) | data formatting | bytes 25165824 | tf_op jit(solution)/shard_map/convert_element_type | solution.py:32
  443.9 249.3 %reduce-scatter.5.cloned.1.call-done = bf16[16,96,512]{2,1,0:T(8,128)(2,1)} async-done(((bf16[16,96,4096]{2,1,0:T(8,128)(2,1)}), bf16[16,96,512]{2,1,0:T(8,128)(2,1)}) %reduce-scatter.5.cloned.1.call-update) | async-done | bytes 1572880 | tf_op jit(solution)/shard_map/reduce_scatter | solution.py:125
  693.2 6.5 all-to-all-start.1
  699.8 23.6 %all-to-all-done.1 = bf16[16,96,512]{2,1,0:T(8,128)(2,1)S(1)} async-done(((bf16[16,96,512]{2,1,0:T(8,128)(2,1)}), bf16[16,96,512]{2,1,0:T(8,128)(2,1)S(1)}, u32[]{:S(2)}, u32[]{:S(2)}) %all-to-all-start.1) | async-done | bytes 1572896 | tf_op jit(solution)/shard_map/all_to_all | solution.py:127
  723.4 2.2 bitcast_convert_fusion
  725.6 6.0 gather_fusion.1
  (70 shorter events, 6.3 us)
Async XLA Ops:
  6.5 3.2 copy-start
  6.5 53.6 %all-gather.3.cloned.1.call-start = ((), (), s32[]{:S(2)}) async-start(), calls=%async_computation.4 | async-start | bytes 2506752 | tf_op jit(solution)/shard_map/all_gather | solution.py:69
  7.3 108.4 %reduce-scatter.3.cloned.1.call-start = ((), (), s32[]{:S(2)}) async-start(), calls=%async_computation.5 | async-start | bytes 1179648 | tf_op jit(solution)/shard_map/reduce_scatter | solution.py:90
  66.1 3.5 copy-start.9
  66.1 7.6 %slice-start = ((s8[8388608]{0:T(1024)(128)(4,1)}), s8[4194304]{0:T(1024)(128)(4,1)S(1)}, s32[]{:S(2)}) async-start(s8[8388608]{0:T(1024)(128)(4,1)} %bitcast.87), calls=%async_computation.8 | async-start | bytes 8388608
  69.6 3.6 copy-start.4
  69.6 4.1 slice-start.1
  73.8 2.6 copy-start.5
  73.8 41.9 %copy-start.2 = (bf16[128,512]{1,0:T(8,128)(2,1)S(1)}, bf16[128,512]{1,0:T(8,128)(2,1)}, u32[]{:S(2)}) copy-start(bf16[128,512]{1,0:T(8,128)(2,1)} %param.17) | copy-start | bytes 393220
  73.8 59.7 %copy-start.7 = (f32[512]{0:T(512)S(1)}, f32[512]{0:T(512)}, u32[]{:S(2)}) copy-start(f32[512]{0:T(512)} %param.18) | copy-start | bytes 6148
  76.1 335.5 %all-gather.5.cloned.1.call-start = ((), (), s32[]{:S(2)}) async-start(), calls=%async_computation.6 | async-start | bytes 14155776 | tf_op jit(solution)/shard_map/all_gather | solution.py:123
  169.8 523.4 %reduce-scatter.5.cloned.1.call-start = ((), (), s32[]{:S(2)}) async-start(), calls=%async_computation.7 | async-start | bytes 14155776 | tf_op jit(solution)/shard_map/reduce_scatter | solution.py:125
  411.6 13.3 %copy-start.8 = (bf16[2,256,4096]{2,1,0:T(8,128)(2,1)S(1)}, bf16[2,256,4096]{2,1,0:T(8,128)(2,1)}, u32[]{:S(2)}) copy-start(bf16[2,256,4096]{2,1,0:T(8,128)(2,1)} %param.20) | copy-start | bytes 12582916
  443.9 255.8 %copy-start.6 = (f32[128,8]{0,1:T(8,128)S(1)}, f32[128,8]{0,1:T(8,128)}, u32[]{:S(2)}) copy-start(f32[128,8]{0,1:T(8,128)} %param.22) | copy-start | bytes 12292
  693.2 30.2 %all-to-all-start.1 = ((bf16[16,96,512]{2,1,0:T(8,128)(2,1)}), bf16[16,96,512]{2,1,0:T(8,128)(2,1)S(1)}, u32[]{:S(2)}, u32[]{:S(2)}) async-start(bf16[16,96,512]{2,1,0:T(8,128)(2,1)} %reduce-scatter.5.cloned.1.call-done), calls=%async_computation.3 | async-start | bytes 3145728 | tf_op jit(solution)/shard_map/all_to_all | solution.py:127
  725.6 6.7 copy-start.3
  725.6 7.4 copy-start.1
Sparse Core Ops, SparseCore 0:
  9.6 50.4 all-gather.2
  76.2 39.3 reduce-scatter.2
  170.0 241.6 all-gather.4
  444.0 249.1 reduce-scatter.4
where the time goes:
time: 740 us
  waiting for transfers between devices  586 us (79%)
  blocking collectives  47 us (6%)
  matrix products  34.4 us (5%)
  local copies, waits for them, and re-layouts  32.6 us (4%)
  other arithmetic  19.7 us (3%)
  between operations  13.5 us (2%)
    reduce_scatter x1, waiting for transfers between devices, body(): lax.psum_scatter(partials, 'exp', scatter_dimension=2, tiled=True)  249 us
    all_gather x1, waiting for transfers between devices, body(): rows_full = lax.all_gather(arrived, 'exp', axis=2, tiled=True)  242 us
    all_gather x1, waiting for transfers between devices, body(): piece = lax.all_gather(latent, 'ctx', axis=0, tiled=True)  49.8 us
    all_to_all x1, blocking collectives, body(): lax.all_to_all(outgoing, 'ctx', split_axis=0, concat_axis=0, tiled=True)  30.3 us
    all_to_all x1, waiting for transfers between devices, body(): lax.all_to_all(summed.astype(jnp.bfloat16), 'ctx', split_axis=0, concat_a...  23.6 us
    reduce_scatter x1, waiting for transfers between devices, body(): lax.psum_scatter(lax.dot_general(w_o, head_out, (((0,), (1,)), ((), ())),...  20.4 us
    psum x1, blocking collectives, body(): squares = lax.psum(jnp.sum(hidden * hidden, axis=1), 'exp')  16.8 us
  transfers between devices with their start and end apart: 5, of which 5 were waited for; matrix products, arithmetic and copies ran while one was open for 3% of the time, Pallas kernels for 0%

commit v1 on v0

v1 whole, which is shorter than its diff:
```python
import itertools
import math

import jax
import jax.numpy as jnp
from jax import lax
from jax.sharding import PartitionSpec as P

D = 4096
NOPE = 128
ROPE = 64
LAT = 512
VDIM = 128
TOP = 8
EXPERTS = 32
GATE_COLS = 128
BOTH = ("ctx", "exp")

epsilon = 1e-06


def table(dx=0, dy=0, dz=0, dc=0):
    def at(x, y, z, c):
        return ((x // 2 * 4 + y) * 2 + c) * 8 + z * 2 + x % 2

    return [
        (at(x, y, z, c), at((x + dx) % 4, (y + dy) % 4, (z + dz) % 4, (c + dc) % 2))
        for x, y, z, c in itertools.product(range(4), range(4), range(4), range(2))
    ]


def shift(value, axis, by):
    return lax.ppermute(value, BOTH, table(**{"d" + axis: by}))


def other_core(value):
    return shift(value, "c", 1)


def ring(block, axis):
    return [block, shift(block, axis, 1), shift(block, axis, -1), shift(block, axis, 2)]


def add_up(*blocks):
    total = blocks[0].astype(jnp.float32)
    for block in blocks[1:]:
        total = total + block.astype(jnp.float32)
    return total


def ring_sum(own, before, after, far, axis):
    return add_up(own, shift(before, axis, -1), shift(after, axis, 1), shift(far, axis, 2))


def document(positions, doc_ends):
    return jnp.sum((positions[:, None] >= doc_ends[None, :]).astype(jnp.int32), axis=1)


def attention(latent, query, w_uk, w_uv, doc_lengths):
    tokens = latent.shape[0]
    heads = w_uk.shape[0]
    qk_width = NOPE + ROPE
    score_scale = 1.0 / math.sqrt(qk_width)
    doc_ends = jnp.cumsum(doc_lengths)
    ctx = lax.axis_index("ctx")
    x_hi, y, core = ctx // 8, (ctx // 2) % 4, ctx % 2
    pair = jnp.concatenate([latent, shift(latent, "x", 2)], axis=0)
    half = jnp.concatenate(ring(pair, "y"), axis=0)
    piece = jnp.concatenate([half, other_core(half)], axis=0)
    starts = [
        (((x_hi + dx) % 2 * 4 + (y + dy) % 4) * 2 + (core + dc) % 2) * tokens
        for dc in (0, 1)
        for dy in (0, 3, 1, 2)
        for dx in (0, 1)
    ]
    steps = jnp.arange(tokens, dtype=jnp.int32)
    key_pos = (jnp.stack(starts)[:, None] + steps[None, :]).reshape(-1)
    key_doc = document(key_pos, doc_ends)
    q_pos = ctx * tokens + steps
    q_doc = document(q_pos, doc_ends)
    q_rows = query.reshape(tokens, heads, qk_width)
    q_lat = jnp.einsum(
        "thn,hln->htl", q_rows[:, :, :NOPE], w_uk, preferred_element_type=jnp.float32
    ).astype(jnp.bfloat16)
    q_full = jnp.concatenate(
        [q_lat, jnp.transpose(q_rows[:, :, NOPE:], (1, 0, 2))], axis=2
    ).reshape(heads * tokens, LAT + ROPE)
    row_pos = jnp.tile(q_pos, heads)
    row_doc = jnp.tile(q_doc, heads)
    allowed = (row_doc[:, None] == key_doc[None, :]) & (row_pos[:, None] >= key_pos[None, :])
    scores = jnp.dot(q_full, piece.T, preferred_element_type=jnp.float32) * score_scale
    scores = jnp.where(allowed, scores, -1e30)
    row_max = jnp.max(scores, axis=1)
    weights = jnp.where(allowed, jnp.exp(scores - row_max[:, None]), 0.0)
    row_total = jnp.sum(weights, axis=1)
    accumulated = jnp.dot(
        weights.astype(jnp.bfloat16), piece[:, :LAT], preferred_element_type=jnp.float32
    )
    o_lat = (accumulated / row_total[:, None]).astype(jnp.bfloat16).reshape(heads, tokens, LAT)
    return (
        jnp.einsum("htl,hlv->thv", o_lat, w_uv, preferred_element_type=jnp.float32)
        .astype(jnp.bfloat16)
        .reshape(tokens, heads * VDIM)
    )


def body(
    latent,
    query,
    w_uk,
    w_uv,
    w_o,
    residual,
    norm_gain,
    w_in,
    w_out,
    routes,
    gate_weights,
    doc_lengths,
):
    tokens = latent.shape[0]
    count_exp = lax.axis_size("exp")
    local_width = residual.shape[1]
    own = tokens // count_exp
    ctx, exp = lax.axis_index("ctx"), lax.axis_index("exp")
    local_experts = w_in.shape[0]
    units = w_in.shape[3]

    sent = jnp.concatenate(
        [
            residual.astype(jnp.float32).reshape(count_exp, own, local_width),
            jnp.broadcast_to(norm_gain[None, None, :], (count_exp, 1, local_width)),
        ],
        axis=1,
    )
    got = lax.all_to_all(sent, "exp", split_axis=0, concat_axis=0)
    wide = jnp.transpose(got, (1, 0, 2)).reshape(own + 1, D)
    residual_rows, gain = wide[:own], wide[own]

    own_routes = lax.dynamic_slice_in_dim(routes, exp * own, own, axis=0)
    own_gates = lax.dynamic_slice_in_dim(gate_weights, exp * own, own, axis=0)
    named = own_routes[:, :, None] == jnp.arange(EXPERTS, dtype=jnp.int32)[None, None, :]
    dense = jnp.sum(jnp.where(named, own_gates[:, :, None], 0.0), axis=1)
    high = dense.astype(jnp.bfloat16)
    low = (dense - high.astype(jnp.float32)).astype(jnp.bfloat16)
    gate_row = jnp.concatenate(
        [high, low, jnp.zeros((own, GATE_COLS - 2 * EXPERTS), jnp.bfloat16)], axis=1
    )
    column = jnp.arange(GATE_COLS, dtype=jnp.int32)[:, None]
    mine = ctx * local_experts + jnp.arange(local_experts, dtype=jnp.int32)[None, :]
    pick = ((column == mine) | (column == mine + EXPERTS)).astype(jnp.bfloat16)

    up = jnp.transpose(w_in, (1, 0, 2, 3)).reshape(D, local_experts * 2 * units)
    down = w_out.reshape(local_experts * units, D)

    def experts(rows):
        pre = jnp.dot(rows[:, :D], up, preferred_element_type=jnp.float32)
        gates = jnp.dot(rows[:, D:], pick, preferred_element_type=jnp.float32)
        acts = []
        for e in range(local_experts):
            gate_pre = pre[:, 2 * e * units : (2 * e + 1) * units]
            up_pre = pre[:, (2 * e + 1) * units : (2 * e + 2) * units]
            acts.append(jax.nn.silu(gate_pre) * up_pre * gates[:, e : e + 1])
        activated = jnp.concatenate(acts, axis=1).astype(jnp.bfloat16)
        return jnp.dot(activated, down, preferred_element_type=jnp.float32).astype(jnp.bfloat16)

    def both_cores(rows):
        theirs = other_core(rows)
        result = experts(jnp.concatenate([theirs, rows], axis=0))
        count = rows.shape[0]
        return add_up(result[count:], other_core(result[:count])).astype(jnp.bfloat16)

    head_out = attention(latent, query, w_uk, w_uv, doc_lengths)
    partial = jnp.dot(head_out, w_o, preferred_element_type=jnp.float32).astype(jnp.bfloat16)
    parts = lax.all_to_all(
        partial.reshape(count_exp, own, D), "exp", split_axis=0, concat_axis=0
    )
    hidden = residual_rows + jnp.sum(parts.astype(jnp.float32), axis=0)
    squares = jnp.mean(hidden * hidden, axis=1, keepdims=True)
    normed = (hidden * lax.rsqrt(squares + epsilon) * gain[None, :]).astype(jnp.bfloat16)
    rows = jnp.concatenate([normed, gate_row], axis=1)

    x_own, x_before, x_after, x_far = ring(rows, "x")
    first = jnp.concatenate(ring(jnp.concatenate([x_own, x_before], axis=0), "z"), axis=0)
    second = jnp.concatenate(ring(jnp.concatenate([x_after, x_far], axis=0), "y"), axis=0)
    count = first.shape[0]
    near = count // 2
    gathered = []
    for block, axis in ((first, "y"), (second, "z")):
        before, after = shift(block, axis, 1), shift(block, axis, -1)
        far = jnp.concatenate(
            [shift(before[:near], axis, 1), shift(after[near:], axis, -1)], axis=0
        )
        gathered.append((before, after, far))
    (y_before, y_after, y_far), (z_before, z_after, z_far) = gathered

    out_own = both_cores(jnp.concatenate([first, second], axis=0))
    out_before = both_cores(jnp.concatenate([y_before, z_before], axis=0))
    out_after = both_cores(jnp.concatenate([y_after, z_after], axis=0))
    out_far = both_cores(jnp.concatenate([y_far, z_far], axis=0))

    first = ring_sum(*[o[:count] for o in (out_own, out_before, out_after, out_far)], "y")
    second = ring_sum(*[o[count:] for o in (out_own, out_before, out_after, out_far)], "z")
    first, second = first.astype(jnp.bfloat16), second.astype(jnp.bfloat16)
    pair = 2 * own
    first = ring_sum(*[first[i * pair : (i + 1) * pair] for i in range(4)], "z")
    second = ring_sum(*[second[i * pair : (i + 1) * pair] for i in range(4)], "y")
    first, second = first.astype(jnp.bfloat16), second.astype(jnp.bfloat16)
    moe_out = ring_sum(first[:own], first[own:], second[:own], second[own:], "x")
    mixed = (hidden + moe_out).astype(jnp.bfloat16)
    return lax.all_to_all(mixed, "exp", split_axis=1, concat_axis=0, tiled=True)


def solution(mesh):
    placed = (
        P("ctx", None),
        P("ctx", "exp"),
        P("exp", None, None),
        P("exp", None, None),
        P("exp", None),
        P("ctx", "exp"),
        P("exp"),
        P("ctx", None, None, "exp"),
        P("ctx", "exp", None),
        P("ctx", None),
        P("ctx", None),
        P(),
    )
    return jax.shard_map(
        body, mesh=mesh, in_specs=placed, out_specs=P("ctx", "exp"), check_vma=False
    )
```

time: 740 us -> 365 us (0.49)
  waiting for transfers between devices: 586 us -> 135 us
  starting transfers between devices: 6.82 us -> 71.4 us
  blocking collectives: 47 us -> 10.7 us
  local copies, waits for them, and re-layouts: 32.6 us -> 67.2 us
  matrix products: 34.4 us -> 55.8 us
  between operations: 13.5 us -> 0.89 us
    all_gather x2 -> x0, waiting for transfers between devices: 291 us -> none  [the longest x1 242 us: body(): rows_full = lax.all_gather(arrived, 'exp', axis=2, tiled=True)]
    reduce_scatter x2 -> x0, waiting for transfers between devices: 270 us -> none  [the longest x1 249 us: body(): lax.psum_scatter(partials, 'exp', scatter_dimension=2, tiled=True)]
    ppermute x0 -> x45, waiting for transfers between devices: none -> 120 us  [shift(): return lax.ppermute(value, BOTH, table(**{'d' + axis: by}))]
    ppermute x0 -> x45, starting transfers between devices: none -> 58.9 us  [shift(): return lax.ppermute(value, BOTH, table(**{'d' + axis: by}))]
    unnamed x28 -> x83, local copies, waits for them, and re-layouts: 1.66 us -> 55.6 us
    dot_general x7 -> x17, matrix products: 34.4 us -> 55.8 us  [the longest x4 25.4 us: experts(): pre = jnp.dot(rows[:, :D], up, preferred_element_type=jnp.float32)]
    all_to_all x1, blocking collectives: 30.3 us -> 10.7 us  [body(): return lax.all_to_all(mixed, 'exp', split_axis=1, concat_axis=0, tiled=True)]
    psum x1 -> x0, blocking collectives: 16.8 us -> none  [body(): squares = lax.psum(jnp.sum(hidden * hidden, axis=1), 'exp')]
  transfers between devices with their start and end apart: 5 -> 47, of which waited for: 5 -> 21; matrix products, arithmetic and copies ran while one was open for 3% -> 34% of each run, Pallas kernels for 0% -> 0%
where the time goes in v1:
time: 365 us; the launch traced here: 362 us
  waiting for transfers between devices  135 us (37%)
  starting transfers between devices  71.4 us (20%)
  local copies, waits for them, and re-layouts  67.2 us (18%)
  matrix products  55.8 us (15%)
  other arithmetic  20.6 us (6%)
  blocking collectives  10.7 us (3%)
    ppermute x45, waiting for transfers between devices, shift(): return lax.ppermute(value, BOTH, table(**{'d' + axis: by}))  120 us
    ppermute x45, starting transfers between devices, shift(): return lax.ppermute(value, BOTH, table(**{'d' + axis: by}))  58.9 us
    unnamed x83, local copies, waits for them, and re-layouts  55.6 us
    dot_general x4, matrix products, experts(): pre = jnp.dot(rows[:, :D], up, preferred_element_type=jnp.float32)  25.4 us
    dot_general x4, matrix products, experts(): jnp.dot(activated, down, preferred_element_type=jnp.float32)  16 us
    all_to_all x1, waiting for transfers between devices, body(): lax.all_to_all(partial.reshape(count_exp, own, D), 'exp', split_axis=0, c...  15.6 us
    all_to_all x1, blocking collectives, body(): return lax.all_to_all(mixed, 'exp', split_axis=1, concat_axis=0, tiled=True)  10.7 us
    convert_element_type x4, other arithmetic, both_cores(): add_up(result[count:], other_core(result[:count])).astype(jnp.bfloat16)  7.88 us
  transfers between devices with their start and end apart: 47, of which 21 were waited for; matrix products, arithmetic and copies ran while one was open for 34% of the time, Pallas kernels for 0%

profile of v1, /device:TPU:0, one launch (start us, length us, event | category | flops | bytes accessed | tf_op | source)
XLA Modules:
  0.0 361.8 jit_solution(7924193546569101866)
XLA Ops:
  16.0 6.2 %all-to-all-start = ((f32[8,17,512]{2,1,0:T(8,128)}), f32[8,17,512]{2,1,0:T(8,128)S(1)}, u32[]{:S(2)}, u32[]{:S(2)}) async-start(f32[8,17,512]{2,1,0:T(8,128)} %pad_maximum_fusion.4), calls=%async_computation | async-start | bytes 786432 | tf_op jit(solution)/shard_map/all_to_all | solution.py:136
  29.5 4.3 %fusion = (f32[1024]{0:T(1024)S(1)}, f32[1024,2048]{1,0:T(8,128)S(1)}) fusion(s32[2048]{0:T(1024)S(1)} %add_bitcast_fusion, s32[2048]{0:T(1024)S(1)} %convert_reduce_fusion.1, s32[1024]{0:T(1024)S(1)} %get-tuple-element.81, s32[1024]{0:T(1024)S(1)} %get-tuple-element.82, bf16[1024,576]{1,0:T(8,128)(2,1)S(1)} %bitcast.90, ...), kind=kOutput, calls=%fused_computation.3 | convolution fusion | flops 2428500992 | bytes 11956224 | tf_op jit(solution)/shard_map/dot_general | solution.py:91
  37.1 3.4 divide_convert_fusion
  43.3 6.2 %all-to-all-start.1 = ((bf16[8,16,4096]{2,1,0:T(8,128)(2,1)}), bf16[8,16,4096]{2,1,0:T(8,128)(2,1)S(1)}, u32[]{:S(2)}, u32[]{:S(2)}) async-start(bf16[8,16,4096]{2,1,0:T(8,128)(2,1)} %bitcast.29), calls=%async_computation.1 | async-start | bytes 2097152 | tf_op jit(solution)/shard_map/all_to_all | solution.py:175
  50.0 15.6 %all-to-all-done.1 = bf16[8,16,4096]{2,1,0:T(8,128)(2,1)S(1)} async-done(((bf16[8,16,4096]{2,1,0:T(8,128)(2,1)}), bf16[8,16,4096]{2,1,0:T(8,128)(2,1)S(1)}, u32[]{:S(2)}, u32[]{:S(2)}) %all-to-all-start.1) | async-done | bytes 1048608 | tf_op jit(solution)/shard_map/all_to_all | solution.py:175
  77.0 9.5 %collective-permute-done.6 = bf16[32,4224]{1,0:T(8,128)(2,1)S(1)} collective-permute-done((bf16[32,4224]{1,0:T(8,128)(2,1)S(1)}, bf16[32,4224]{1,0:T(8,128)(2,1)S(1)}, u32[]{:S(2)}, u32[]{:S(2)}) %collective-permute-start.6) | collective-permute-done | bytes 270368 | tf_op jit(solution)/shard_map/ppermute | solution.py:33
  94.6 4.5 %collective-permute-done.11 = bf16[32,4224]{1,0:T(8,128)(2,1)S(1)} collective-permute-done((bf16[32,4224]{1,0:T(8,128)(2,1)S(1)}, bf16[32,4224]{1,0:T(8,128)(2,1)S(1)}, u32[]{:S(2)}, u32[]{:S(2)}) %collective-permute-start.11) | collective-permute-done | bytes 270368 | tf_op jit(solution)/shard_map/ppermute | solution.py:33
  103.5 21.2 %copy.45 = bf16[2,4096,2,256]{1,3,2,0:T(8,128)(2,1)} copy(bf16[2,4096,2,256]{3,2,1,0:T(2,128)(2,1)} %param.19) | data formatting | bytes 16777216 | tf_op args[7]
  141.0 6.4 %fusion.9 = f32[512,1024]{1,0:T(8,128)S(1)} fusion(bf16[4096,1024]{0,1:T(8,128)(2,1)S(1)} %bitcast.82, bf16[512,4224]{1,0:T(8,128)(2,1)} %get-tuple-element.39), kind=kOutput, calls=%fused_computation.17 | convolution fusion | flops 4294967296 | bytes 14680064 | tf_op jit(solution)/shard_map/dot_general | solution.py:157
  147.3 13.5 %collective-permute-done.17 = bf16[128,4224]{1,0:T(8,128)(2,1)S(1)} collective-permute-done((bf16[128,4224]{1,0:T(8,128)(2,1)S(1)}, bf16[128,4224]{1,0:T(8,128)(2,1)S(1)}, u32[]{:S(2)}, u32[]{:S(2)}) %collective-permute-start.17) | collective-permute-done | bytes 1081376 | tf_op jit(solution)/shard_map/ppermute | solution.py:33
  173.2 3.5 collective-permute-start.27
  178.2 6.0 %collective-permute-done.28 = bf16[64,4224]{1,0:T(8,128)(2,1)S(1)} collective-permute-done((bf16[64,4224]{1,0:T(8,128)(2,1)S(1)}, bf16[64,4224]{1,0:T(8,128)(2,1)S(1)}, u32[]{:S(2)}, u32[]{:S(2)}) %collective-permute-start.28) | collective-permute-done | bytes 540704 | tf_op jit(solution)/shard_map/ppermute | solution.py:33
  193.3 6.4 %fusion.7 = f32[512,1024]{1,0:T(8,128)S(1)} fusion(bf16[4096,1024]{0,1:T(8,128)(2,1)S(1)} %bitcast.83, bf16[512,4224]{1,0:T(8,128)(2,1)} %constant_dynamic-update-slice_fusion.46), kind=kOutput, calls=%fused_computation.15 | convolution fusion | flops 4294967296 | bytes 14680064 | tf_op jit(solution)/shard_map/dot_general | solution.py:157
  200.0 4.6 %convolution_convert_fusion.2 = bf16[512,4096]{1,0:T(8,128)(2,1)S(1)} fusion(bf16[512,4096]{1,0:T(8,128)(2,1)} %bitcast.111, bf16[512,256]{1,0:T(8,128)(2,1)S(1)} %get-tuple-element.20, bf16[512,256]{1,0:T(8,128)(2,1)S(1)} %get-tuple-element.19), kind=kOutput, calls=%fused_computation.6 | convolution fusion | flops 2150629376 | bytes 8912896 | tf_op jit(solution)/shard_map/dot_general | solution.py:165
  213.0 6.4 %fusion.5 = f32[512,1024]{1,0:T(8,128)S(1)} fusion(bf16[4096,1024]{0,1:T(8,128)(2,1)S(1)} %bitcast.84, bf16[512,4224]{1,0:T(8,128)(2,1)} %constant_dynamic-update-slice_fusion.49), kind=kOutput, calls=%fused_computation.13 | convolution fusion | flops 4294967296 | bytes 14680064 | tf_op jit(solution)/shard_map/dot_general | solution.py:157
  219.7 4.6 %convolution_convert_fusion.1 = bf16[512,4096]{1,0:T(8,128)(2,1)S(1)} fusion(bf16[512,4096]{1,0:T(8,128)(2,1)} %bitcast.112, bf16[512,256]{1,0:T(8,128)(2,1)S(1)} %get-tuple-element.22, bf16[512,256]{1,0:T(8,128)(2,1)S(1)} %get-tuple-element.21), kind=kOutput, calls=%fused_computation.5 | convolution fusion | flops 2150629376 | bytes 8912896 | tf_op jit(solution)/shard_map/dot_general | solution.py:165
  230.5 6.3 %fusion.3 = f32[512,1024]{1,0:T(8,128)S(1)} fusion(bf16[4096,1024]{0,1:T(8,128)(2,1)S(1)} %bitcast.85, bf16[512,4224]{1,0:T(8,128)(2,1)} %copy-done.11), kind=kOutput, calls=%fused_computation.11 | convolution fusion | flops 4294967296 | bytes 14680064 | tf_op jit(solution)/shard_map/dot_general | solution.py:157
  237.2 4.5 %convolution_convert_fusion = bf16[512,4096]{1,0:T(8,128)(2,1)S(1)} fusion(bf16[512,4096]{1,0:T(8,128)(2,1)} %bitcast.113, bf16[512,256]{1,0:T(8,128)(2,1)S(1)} %get-tuple-element.24, bf16[512,256]{1,0:T(8,128)(2,1)S(1)} %get-tuple-element.23), kind=kOutput, calls=%fused_computation.4 | convolution fusion | flops 2150629376 | bytes 8912896 | tf_op jit(solution)/shard_map/dot_general | solution.py:165
  246.5 3.3 collective-permute-start.20
  257.2 37.9 %collective-permute-done.20 = bf16[128,4096]{1,0:T(8,128)(2,1)S(1)} collective-permute-done((bf16[128,4096]{1,0:T(8,128)(2,1)S(1)}, bf16[128,4096]{1,0:T(8,128)(2,1)S(1)}, u32[]{:S(2)}, u32[]{:S(2)}) %collective-permute-start.20) | collective-permute-done | bytes 1048608 | tf_op jit(solution)/shard_map/ppermute | solution.py:33
  301.3 19.6 %collective-permute-done.39 = bf16[128,4096]{1,0:T(8,128)(2,1)S(1)} collective-permute-done((bf16[128,4096]{1,0:T(8,128)(2,1)S(1)}, bf16[128,4096]{1,0:T(8,128)(2,1)S(1)}, u32[]{:S(2)}, u32[]{:S(2)}) %collective-permute-start.39) | collective-permute-done | bytes 1048608 | tf_op jit(solution)/shard_map/ppermute | solution.py:33
  325.0 3.9 %collective-permute-start.40 = (bf16[32,4096]{1,0:T(8,128)(2,1)S(1)}, bf16[32,4096]{1,0:T(8,128)(2,1)S(1)}, u32[]{:S(2)}, u32[]{:S(2)}) collective-permute-start(bf16[32,4096]{1,0:T(8,128)(2,1)S(1)} %get-tuple-element.28), channel_id=1, source_target_pairs={{0,48},{8,56},{2,50},{10,58},{4,52},{12,60},{6,54},{14,62},{16,0},... | collective-permute-start | bytes 786440 | tf_op jit(solution)/shard_map/ppermute | solution.py:33
  331.7 4.2 %collective-permute-done.34 = bf16[32,4096]{1,0:T(8,128)(2,1)S(1)} collective-permute-done((bf16[32,4096]{1,0:T(8,128)(2,1)S(1)}, bf16[32,4096]{1,0:T(8,128)(2,1)S(1)}, u32[]{:S(2)}, u32[]{:S(2)}) %collective-permute-start.34) | collective-permute-done | bytes 262176 | tf_op jit(solution)/shard_map/ppermute | solution.py:33
  350.3 10.7 %all_to_all.29 = bf16[16,8,512]{2,0,1:T(8,128)(2,1)S(1)} all-to-all(bf16[16,8,512]{2,0,1:T(8,128)(2,1)S(1)} %bitcast.97), channel_id=1, replica_groups=mesh['ctx'=16,'exp'=8] {'exp'}, dimensions={1} | all-to-all | bytes 262144 | tf_op jit(solution)/shard_map/all_to_all | solution.py:211
  (243 shorter events, 148.3 us)
Async XLA Ops:
  8.0 14.9 %collective-permute-start.1 = (bf16[256,576]{0,1:T(8,128)(2,1)S(1)}, bf16[256,576]{0,1:T(8,128)(2,1)S(1)}, u32[]{:S(2)}, u32[]{:S(2)}) collective-permute-start(bf16[256,576]{0,1:T(8,128)(2,1)S(1)} %get-tuple-element.55), channel_id=1, source_target_pairs={{0,16},{8,24},{2,18},{10,26},{4,20},{12,28},{6,22},{14,30},{16,32}... | collective-permute-start | bytes 884744 | tf_op jit(solution)/shard_map/ppermute | solution.py:33
  16.0 27.3 %all-to-all-start = ((f32[8,17,512]{2,1,0:T(8,128)}), f32[8,17,512]{2,1,0:T(8,128)S(1)}, u32[]{:S(2)}, u32[]{:S(2)}) async-start(f32[8,17,512]{2,1,0:T(8,128)} %pad_maximum_fusion.4), calls=%async_computation | async-start | bytes 786432 | tf_op jit(solution)/shard_map/all_to_all | solution.py:136
  43.3 22.3 %all-to-all-start.1 = ((bf16[8,16,4096]{2,1,0:T(8,128)(2,1)}), bf16[8,16,4096]{2,1,0:T(8,128)(2,1)S(1)}, u32[]{:S(2)}, u32[]{:S(2)}) async-start(bf16[8,16,4096]{2,1,0:T(8,128)(2,1)} %bitcast.29), calls=%async_computation.1 | async-start | bytes 2097152 | tf_op jit(solution)/shard_map/all_to_all | solution.py:175
  68.2 20.4 %collective-permute-start.9 = (bf16[16,4224]{1,0:T(8,128)(2,1)S(1)}, bf16[16,4224]{1,0:T(8,128)(2,1)S(1)}, u32[]{:S(2)}, u32[]{:S(2)}) collective-permute-start(bf16[16,4224]{1,0:T(8,128)(2,1)S(1)} %concatenate.84), channel_id=1, source_target_pairs={{0,65},{8,73},{2,67},{10,75},{4,69},{12,77},{6,71},{14,79},{16,81}... | collective-permute-start | bytes 405512 | tf_op jit(solution)/shard_map/ppermute | solution.py:33
  70.8 18.5 %collective-permute-start.10 = (bf16[16,4224]{1,0:T(8,128)(2,1)S(1)}, bf16[16,4224]{1,0:T(8,128)(2,1)S(1)}, u32[]{:S(2)}, u32[]{:S(2)}) collective-permute-start(bf16[16,4224]{1,0:T(8,128)(2,1)S(1)} %concatenate.84), channel_id=1, source_target_pairs={{0,64},{8,72},{2,66},{10,74},{4,68},{12,76},{6,70},{14,78},{16,80}... | collective-permute-start | bytes 405512 | tf_op jit(solution)/shard_map/ppermute | solution.py:33
  103.5 21.3 %collective-permute-start.14 = (bf16[256,4224]{1,0:T(8,128)(2,1)}, bf16[256,4224]{1,0:T(8,128)(2,1)S(1)}, u32[]{:S(2)}, u32[]{:S(2)}) collective-permute-start(bf16[256,4224]{1,0:T(8,128)(2,1)} %constant_dynamic-update-slice_fusion.15), channel_id=1, source_target_pairs={{0,8},{8,0},{2,10},{10,2},{4,12},{12,4},{6,14},{14,6},{16,24},{24,... | collective-permute-start | bytes 6488072 | tf_op jit(solution)/shard_map/ppermute | solution.py:33
  133.4 27.5 %collective-permute-start.17 = (bf16[128,4224]{1,0:T(8,128)(2,1)S(1)}, bf16[128,4224]{1,0:T(8,128)(2,1)S(1)}, u32[]{:S(2)}, u32[]{:S(2)}) collective-permute-start(bf16[128,4224]{1,0:T(8,128)(2,1)S(1)} %get-tuple-element.40), channel_id=1, source_target_pairs={{0,2},{8,10},{2,4},{10,12},{4,6},{12,14},{6,0},{14,8},{16,18},{24,... | collective-permute-start | bytes 3244040 | tf_op jit(solution)/shard_map/ppermute | solution.py:33
  133.6 36.1 %collective-permute-start.22 = (bf16[128,4224]{1,0:T(8,128)(2,1)S(1)}, bf16[128,4224]{1,0:T(8,128)(2,1)S(1)}, u32[]{:S(2)}, u32[]{:S(2)}) collective-permute-start(bf16[128,4224]{1,0:T(8,128)(2,1)S(1)} %get-tuple-element.40), channel_id=1, source_target_pairs={{0,6},{8,14},{2,0},{10,8},{4,2},{12,10},{6,4},{14,12},{16,22},{24,... | collective-permute-start | bytes 3244040 | tf_op jit(solution)/shard_map/ppermute | solution.py:33
  136.7 26.9 %collective-permute-start.16 = (bf16[128,4224]{1,0:T(8,128)(2,1)S(1)}, bf16[128,4224]{1,0:T(8,128)(2,1)S(1)}, u32[]{:S(2)}, u32[]{:S(2)}) collective-permute-start(bf16[128,4224]{1,0:T(8,128)(2,1)S(1)} %get-tuple-element.46), channel_id=1, source_target_pairs={{0,16},{8,24},{2,18},{10,26},{4,20},{12,28},{6,22},{14,30},{16,32}... | collective-permute-start | bytes 3244040 | tf_op jit(solution)/shard_map/ppermute | solution.py:33
  137.8 35.4 %collective-permute-start.21 = (bf16[128,4224]{1,0:T(8,128)(2,1)S(1)}, bf16[128,4224]{1,0:T(8,128)(2,1)S(1)}, u32[]{:S(2)}, u32[]{:S(2)}) collective-permute-start(bf16[128,4224]{1,0:T(8,128)(2,1)S(1)} %get-tuple-element.46), channel_id=1, source_target_pairs={{0,48},{8,56},{2,50},{10,58},{4,52},{12,60},{6,54},{14,62},{16,0},... | collective-permute-start | bytes 3244040 | tf_op jit(solution)/shard_map/ppermute | solution.py:33
  163.7 24.8 %collective-permute-start.18 = (bf16[256,4224]{1,0:T(8,128)(2,1)S(1)}, bf16[256,4224]{1,0:T(8,128)(2,1)S(1)}, u32[]{:S(2)}, u32[]{:S(2)}) collective-permute-start(bf16[256,4224]{1,0:T(8,128)(2,1)S(1)} %pad_maximum_fusion), channel_id=1, source_target_pairs={{0,8},{8,0},{2,10},{10,2},{4,12},{12,4},{6,14},{14,6},{16,24},{24,... | collective-permute-start | bytes 6488072 | tf_op jit(solution)/shard_map/ppermute | solution.py:33
  169.6 14.5 %collective-permute-start.28 = (bf16[64,4224]{1,0:T(8,128)(2,1)S(1)}, bf16[64,4224]{1,0:T(8,128)(2,1)S(1)}, u32[]{:S(2)}, u32[]{:S(2)}) collective-permute-start(bf16[64,4224]{1,0:T(8,128)(2,1)S(1)} %slice.321), channel_id=1, source_target_pairs={{0,2},{8,10},{2,4},{10,12},{4,6},{12,14},{6,0},{14,8},{16,18},{24,... | collective-permute-start | bytes 1622024 | tf_op jit(solution)/shard_map/ppermute | solution.py:33
  169.8 14.4 %collective-permute-start.29 = (bf16[64,4224]{1,0:T(8,128)(2,1)S(1)}, bf16[64,4224]{1,0:T(8,128)(2,1)S(1)}, u32[]{:S(2)}, u32[]{:S(2)}) collective-permute-start(bf16[64,4224]{1,0:T(8,128)(2,1)S(1)} %slice.322), channel_id=1, source_target_pairs={{0,6},{8,14},{2,0},{10,8},{4,2},{12,10},{6,4},{14,12},{16,22},{24,... | collective-permute-start | bytes 1622024 | tf_op jit(solution)/shard_map/ppermute | solution.py:33
  184.2 71.4 %collective-permute-start.15 = (bf16[256,4096]{1,0:T(8,128)(2,1)}, bf16[256,4096]{1,0:T(8,128)(2,1)}, u32[]{:S(2)}, u32[]{:S(2)}) collective-permute-start(bf16[256,4096]{1,0:T(8,128)(2,1)} %slice.295), channel_id=1, source_target_pairs={{0,8},{8,0},{2,10},{10,2},{4,12},{12,4},{6,14},{14,6},{16,24},{24,... | collective-permute-start | bytes 6291464 | tf_op jit(solution)/shard_map/ppermute | solution.py:33
  184.2 22.5 %collective-permute-start.23 = (bf16[256,4224]{1,0:T(8,128)(2,1)}, bf16[256,4224]{1,0:T(8,128)(2,1)}, u32[]{:S(2)}, u32[]{:S(2)}) collective-permute-start(bf16[256,4224]{1,0:T(8,128)(2,1)} %pad_maximum_fusion.1), channel_id=1, source_target_pairs={{0,8},{8,0},{2,10},{10,2},{4,12},{12,4},{6,14},{14,6},{16,24},{24,... | collective-permute-start | bytes 6488072 | tf_op jit(solution)/shard_map/ppermute | solution.py:33
  188.6 37.9 %collective-permute-start.30 = (bf16[256,4224]{1,0:T(8,128)(2,1)}, bf16[256,4224]{1,0:T(8,128)(2,1)}, u32[]{:S(2)}, u32[]{:S(2)}) collective-permute-start(bf16[256,4224]{1,0:T(8,128)(2,1)} %pad_maximum_fusion.2), channel_id=1, source_target_pairs={{0,8},{8,0},{2,10},{10,2},{4,12},{12,4},{6,14},{14,6},{16,24},{24,... | collective-permute-start | bytes 6488072 | tf_op jit(solution)/shard_map/ppermute | solution.py:33
  206.2 36.0 %collective-permute-start.19 = (bf16[256,4096]{1,0:T(8,128)(2,1)}, bf16[256,4096]{1,0:T(8,128)(2,1)}, u32[]{:S(2)}, u32[]{:S(2)}) collective-permute-start(bf16[256,4096]{1,0:T(8,128)(2,1)} %slice.306), channel_id=1, source_target_pairs={{0,8},{8,0},{2,10},{10,2},{4,12},{12,4},{6,14},{14,6},{16,24},{24,... | collective-permute-start | bytes 6291464 | tf_op jit(solution)/shard_map/ppermute | solution.py:33
  225.7 24.6 %collective-permute-start.24 = (bf16[256,4096]{1,0:T(8,128)(2,1)}, bf16[256,4096]{1,0:T(8,128)(2,1)}, u32[]{:S(2)}, u32[]{:S(2)}) collective-permute-start(bf16[256,4096]{1,0:T(8,128)(2,1)} %slice.317), channel_id=1, source_target_pairs={{0,8},{8,0},{2,10},{10,2},{4,12},{12,4},{6,14},{14,6},{16,24},{24,... | collective-permute-start | bytes 6291464 | tf_op jit(solution)/shard_map/ppermute | solution.py:33
  246.5 48.5 %collective-permute-start.20 = (bf16[128,4096]{1,0:T(8,128)(2,1)S(1)}, bf16[128,4096]{1,0:T(8,128)(2,1)S(1)}, u32[]{:S(2)}, u32[]{:S(2)}) collective-permute-start(bf16[128,4096]{1,0:T(8,128)(2,1)S(1)} %get-tuple-element.11), channel_id=1, source_target_pairs={{0,48},{8,56},{2,50},{10,58},{4,52},{12,60},{6,54},{14,62},{16,0},... | collective-permute-start | bytes 3145736 | tf_op jit(solution)/shard_map/ppermute | solution.py:33
  249.9 48.2 %collective-permute-start.37 = (bf16[128,4096]{1,0:T(8,128)(2,1)S(1)}, bf16[128,4096]{1,0:T(8,128)(2,1)S(1)}, u32[]{:S(2)}, u32[]{:S(2)}) collective-permute-start(bf16[128,4096]{1,0:T(8,128)(2,1)S(1)} %get-tuple-element.12), channel_id=1, source_target_pairs={{0,6},{8,14},{2,0},{10,8},{4,2},{12,10},{6,4},{14,12},{16,22},{24,... | collective-permute-start | bytes 3145736 | tf_op jit(solution)/shard_map/ppermute | solution.py:33
  252.9 48.4 %collective-permute-start.25 = (bf16[128,4096]{1,0:T(8,128)(2,1)S(1)}, bf16[128,4096]{1,0:T(8,128)(2,1)S(1)}, u32[]{:S(2)}, u32[]{:S(2)}) collective-permute-start(bf16[128,4096]{1,0:T(8,128)(2,1)S(1)} %get-tuple-element.13), channel_id=1, source_target_pairs={{0,16},{8,24},{2,18},{10,26},{4,20},{12,28},{6,22},{14,30},{16,32}... | collective-permute-start | bytes 3145736 | tf_op jit(solution)/shard_map/ppermute | solution.py:33
  253.0 48.3 %collective-permute-start.38 = (bf16[128,4096]{1,0:T(8,128)(2,1)S(1)}, bf16[128,4096]{1,0:T(8,128)(2,1)S(1)}, u32[]{:S(2)}, u32[]{:S(2)}) collective-permute-start(bf16[128,4096]{1,0:T(8,128)(2,1)S(1)} %get-tuple-element.14), channel_id=1, source_target_pairs={{0,2},{8,10},{2,4},{10,12},{4,6},{12,14},{6,0},{14,8},{16,18},{24,... | collective-permute-start | bytes 3145736 | tf_op jit(solution)/shard_map/ppermute | solution.py:33
  255.6 45.7 %collective-permute-start.32 = (bf16[128,4096]{1,0:T(8,128)(2,1)S(1)}, bf16[128,4096]{1,0:T(8,128)(2,1)S(1)}, u32[]{:S(2)}, u32[]{:S(2)}) collective-permute-start(bf16[128,4096]{1,0:T(8,128)(2,1)S(1)} %get-tuple-element.15), channel_id=1, source_target_pairs={{0,32},{8,40},{2,34},{10,42},{4,36},{12,44},{6,38},{14,46},{16,48}... | collective-permute-start | bytes 3145736 | tf_op jit(solution)/shard_map/ppermute | solution.py:33
  295.1 25.9 %collective-permute-start.39 = (bf16[128,4096]{1,0:T(8,128)(2,1)S(1)}, bf16[128,4096]{1,0:T(8,128)(2,1)S(1)}, u32[]{:S(2)}, u32[]{:S(2)}) collective-permute-start(bf16[128,4096]{1,0:T(8,128)(2,1)S(1)} %get-tuple-element.16), channel_id=1, source_target_pairs={{0,4},{8,12},{2,6},{10,14},{4,0},{12,8},{6,2},{14,10},{16,20},{24,... | collective-permute-start | bytes 3145736 | tf_op jit(solution)/shard_map/ppermute | solution.py:33
  (47 other events, 462.9 us)

commit v2 on v1

--- a/solution.py
+++ b/solution.py
@@ -1,9 +1,12 @@
+import functools
 import itertools
 import math
 
 import jax
 import jax.numpy as jnp
 from jax import lax
+from jax.experimental import pallas as pl
+from jax.experimental.pallas import tpu as pltpu
 from jax.sharding import PartitionSpec as P
 
 D = 4096
@@ -52,11 +55,169 @@
     return add_up(own, shift(before, axis, -1), shift(after, axis, 1), shift(far, axis, 2))
 
 
+VMEM_LIMIT = 56 * 1024 * 1024
+
+
+def grouped(refs, sizes):
+    found, at = [], 0
+    for size in sizes:
+        found.append(refs[at : at + size])
+        at += size
+    return found
+
+
+def stack_kernel(sizes, *refs):
+    count = sum(sizes)
+    for group, out in zip(grouped(refs[:count], sizes), refs[count:]):
+        at = 0
+        for ref in group:
+            out[at : at + ref.shape[0], :] = ref[...]
+            at += ref.shape[0]
+
+
+def stack(*groups):
+    sizes = tuple(len(group) for group in groups)
+    blocks = [block for group in groups for block in group]
+    width = blocks[0].shape[1]
+    heights = [sum(block.shape[0] for block in group) for group in groups]
+    tile = width // 3
+    return pl.pallas_call(
+        functools.partial(stack_kernel, sizes),
+        grid=(3,),
+        in_specs=[pl.BlockSpec((block.shape[0], tile), lambda i: (0, i)) for block in blocks],
+        out_specs=[pl.BlockSpec((height, tile), lambda i: (0, i)) for height in heights],
+        out_shape=[jax.ShapeDtypeStruct((height, width), jnp.bfloat16) for height in heights],
+        compiler_params=pltpu.CompilerParams(vmem_limit_bytes=VMEM_LIMIT),
+        cost_estimate=pl.CostEstimate(
+            flops=0, bytes_accessed=4 * sum(heights) * width, transcendentals=0
+        ),
+    )(*blocks)
+
+
+def sums_kernel(sizes, *refs):
+    count = sum(sizes)
+    outs = refs[count:]
+    parts = len(outs) // len(sizes)
+    for at, group in enumerate(grouped(refs[:count], sizes)):
+        total = group[0][...].astype(jnp.float32)
+        for ref in group[1:]:
+            total = total + ref[...].astype(jnp.float32)
+        total = total.astype(jnp.bfloat16)
+        rows = total.shape[0] // parts
+        for part in range(parts):
+            outs[at * parts + part][...] = total[part * rows : (part + 1) * rows]
+
+
+def sums(parts, *groups):
+    sizes = tuple(len(group) for group in groups)
+    blocks = [block for group in groups for block in group]
+    width = blocks[0].shape[1]
+    heights = [group[0].shape[0] // parts for group in groups for _ in range(parts)]
+    tile = width // 4
+    outs = pl.pallas_call(
+        functools.partial(sums_kernel, sizes),
+        grid=(4,),
+        in_specs=[pl.BlockSpec((block.shape[0], tile), lambda i: (0, i)) for block in blocks],
+        out_specs=[pl.BlockSpec((height, tile), lambda i: (0, i)) for height in heights],
+        out_shape=[jax.ShapeDtypeStruct((height, width), jnp.bfloat16) for height in heights],
+        compiler_params=pltpu.CompilerParams(vmem_limit_bytes=VMEM_LIMIT),
+        cost_estimate=pl.CostEstimate(
+            flops=0,
+            bytes_accessed=2 * width * (sum(heights) + sum(b.shape[0] for b in blocks)),
+            transcendentals=0,
+        ),
+    )(*blocks)
+    return grouped(outs, [parts] * len(groups))
+
+
+STEPS = 4
+
+
+def experts_kernel(sizes, *refs):
+    count = sum(sizes)
+    blocks, gate_refs = refs[:count], refs[count : 2 * count]
+    up, down, pick = refs[2 * count : 2 * count + 3]
+    outs = refs[2 * count + 3 : 2 * count + 3 + len(sizes)]
+    pre, act = refs[2 * count + 3 + len(sizes) :]
+    step = pl.program_id(0)
+    units = up.shape[3]
+
+    @pl.when(step < STEPS)
+    def _():
+        rows = jnp.concatenate([block[...] for block in blocks], axis=0)
+        for e in range(up.shape[0]):
+            for g in range(2):
+                columns = slice((2 * e + g) * units, (2 * e + g + 1) * units)
+                product = jnp.dot(rows, up[e, g], preferred_element_type=jnp.float32)
+
+                @pl.when(step == 0)
+                def _():
+                    pre[:, columns] = product
+
+                @pl.when(step > 0)
+                def _():
+                    pre[:, columns] += product
+
+    @pl.when(step == STEPS - 1)
+    def _():
+        gate_rows = jnp.concatenate([ref[...] for ref in gate_refs], axis=0)
+        gates = jnp.dot(gate_rows, pick[...], preferred_element_type=jnp.float32)
+        for e in range(up.shape[0]):
+            gate_pre = pre[:, 2 * e * units : (2 * e + 1) * units]
+            up_pre = pre[:, (2 * e + 1) * units : (2 * e + 2) * units]
+            value = gate_pre / (1.0 + jnp.exp(-gate_pre)) * up_pre * gates[:, e : e + 1]
+            act[:, e * units : (e + 1) * units] = value.astype(jnp.bfloat16)
+
+    @pl.when(step >= STEPS)
+    def _():
+        result = jnp.dot(act[...], down[...], preferred_element_type=jnp.float32).astype(
+            jnp.bfloat16
+        )
+        at = 0
+        for out in outs:
+            out[...] = result[at : at + out.shape[0]]
+            at += out.shape[0]
+
+
+def run_experts(groups, up, down, pick):
+    sizes = tuple(len(group) for group in groups)
+    blocks = [block for group in groups for block in group]
+    heights = [sum(block.shape[0] for block in group) for group in groups]
+    height = sum(heights)
+    experts, _, _, units = up.shape
+    tile = D // STEPS
+    early = lambda i: jnp.minimum(i, STEPS - 1)
+    late = lambda i: jnp.maximum(i - STEPS, 0)
+    return pl.pallas_call(
+        functools.partial(experts_kernel, sizes),
+        grid=(2 * STEPS,),
+        in_specs=[pl.BlockSpec((b.shape[0], tile), lambda i: (0, early(i))) for b in blocks]
+        + [pl.BlockSpec((b.shape[0], GATE_COLS), lambda i: (0, D // GATE_COLS)) for b in blocks]
+        + [
+            pl.BlockSpec((experts, 2, tile, units), lambda i: (0, 0, early(i), 0)),
+            pl.BlockSpec((experts * units, tile), lambda i: (0, late(i))),
+            pl.BlockSpec(pick.shape, lambda i: (0, 0)),
+        ],
+        out_specs=[pl.BlockSpec((h, tile), lambda i: (0, late(i))) for h in heights],
+        out_shape=[jax.ShapeDtypeStruct((h, D), jnp.bfloat16) for h in heights],
+        scratch_shapes=[
+            pltpu.VMEM((height, experts * 2 * units), jnp.float32),
+            pltpu.VMEM((height, experts * units), jnp.bfloat16),
+        ],
+        compiler_params=pltpu.CompilerParams(vmem_limit_bytes=VMEM_LIMIT),
+        cost_estimate=pl.CostEstimate(
+            flops=6 * height * D * experts * units,
+            bytes_accessed=6 * experts * units * D + 4 * height * D,
+            transcendentals=height * experts * units,
+        ),
+    )(*blocks, *blocks, up, down, pick)
+
+
 def document(positions, doc_ends):
     return jnp.sum((positions[:, None] >= doc_ends[None, :]).astype(jnp.int32), axis=1)
 
 
-def attention(latent, query, w_uk, w_uv, doc_lengths):
+def attention(latent, query, w_uk, w_uv, doc_lengths, up):
     tokens = latent.shape[0]
     heads = w_uk.shape[0]
     qk_width = NOPE + ROPE
@@ -67,6 +228,7 @@
     pair = jnp.concatenate([latent, shift(latent, "x", 2)], axis=0)
     half = jnp.concatenate(ring(pair, "y"), axis=0)
     piece = jnp.concatenate([half, other_core(half)], axis=0)
+    piece, up = lax.optimization_barrier((piece, up))
     starts = [
         (((x_hi + dx) % 2 * 4 + (y + dy) % 4) * 2 + (core + dc) % 2) * tokens
         for dc in (0, 1)
@@ -97,11 +259,12 @@
         weights.astype(jnp.bfloat16), piece[:, :LAT], preferred_element_type=jnp.float32
     )
     o_lat = (accumulated / row_total[:, None]).astype(jnp.bfloat16).reshape(heads, tokens, LAT)
-    return (
+    head_out = (
         jnp.einsum("htl,hlv->thv", o_lat, w_uv, preferred_element_type=jnp.float32)
         .astype(jnp.bfloat16)
         .reshape(tokens, heads * VDIM)
     )
+    return head_out, up
 
 
 def body(
@@ -150,27 +313,16 @@
     mine = ctx * local_experts + jnp.arange(local_experts, dtype=jnp.int32)[None, :]
     pick = ((column == mine) | (column == mine + EXPERTS)).astype(jnp.bfloat16)
 
-    up = jnp.transpose(w_in, (1, 0, 2, 3)).reshape(D, local_experts * 2 * units)
+    up = jnp.transpose(w_in, (0, 2, 1, 3))
     down = w_out.reshape(local_experts * units, D)
 
-    def experts(rows):
-        pre = jnp.dot(rows[:, :D], up, preferred_element_type=jnp.float32)
-        gates = jnp.dot(rows[:, D:], pick, preferred_element_type=jnp.float32)
-        acts = []
-        for e in range(local_experts):
-            gate_pre = pre[:, 2 * e * units : (2 * e + 1) * units]
-            up_pre = pre[:, (2 * e + 1) * units : (2 * e + 2) * units]
-            acts.append(jax.nn.silu(gate_pre) * up_pre * gates[:, e : e + 1])
-        activated = jnp.concatenate(acts, axis=1).astype(jnp.bfloat16)
-        return jnp.dot(activated, down, preferred_element_type=jnp.float32).astype(jnp.bfloat16)
-
-    def both_cores(rows):
-        theirs = other_core(rows)
-        result = experts(jnp.concatenate([theirs, rows], axis=0))
-        count = rows.shape[0]
-        return add_up(result[count:], other_core(result[:count])).astype(jnp.bfloat16)
-
-    head_out = attention(latent, query, w_uk, w_uv, doc_lengths)
+    def both_cores(groups):
+        theirs = [[other_core(block) for block in group] for group in groups]
+        result = run_experts(theirs + groups, up, down, pick)
+        back = [other_core(block) for block in result[: len(groups)]]
+        return [total for (total,) in sums(1, *zip(result[len(groups) :], back))]
+
+    head_out, up = attention(latent, query, w_uk, w_uv, doc_lengths, up)
     partial = jnp.dot(head_out, w_o, preferred_element_type=jnp.float32).astype(jnp.bfloat16)
     parts = lax.all_to_all(
         partial.reshape(count_exp, own, D), "exp", split_axis=0, concat_axis=0
@@ -181,32 +333,33 @@
     rows = jnp.concatenate([normed, gate_row], axis=1)
 
     x_own, x_before, x_after, x_far = ring(rows, "x")
-    first = jnp.concatenate(ring(jnp.concatenate([x_own, x_before], axis=0), "z"), axis=0)
-    second = jnp.concatenate(ring(jnp.concatenate([x_after, x_far], axis=0), "y"), axis=0)
-    count = first.shape[0]
-    near = count // 2
-    gathered = []
+    first, second = stack([x_own, x_before], [x_after, x_far])
+    first, second = stack(ring(first, "z"), ring(second, "y"))
+    near = first.shape[0] // 2
+    before, after, far = [], [], []
     for block, axis in ((first, "y"), (second, "z")):
-        before, after = shift(block, axis, 1), shift(block, axis, -1)
-        far = jnp.concatenate(
-            [shift(before[:near], axis, 1), shift(after[near:], axis, -1)], axis=0
+        before.append([shift(block, axis, 1)])
+        after.append([shift(block, axis, -1)])
+    for i, axis in enumerate("yz"):
+        far.append(
+            [shift(before[i][0][:near], axis, 1), shift(after[i][0][near:], axis, -1)]
         )
-        gathered.append((before, after, far))
-    (y_before, y_after, y_far), (z_before, z_after, z_far) = gathered
-
-    out_own = both_cores(jnp.concatenate([first, second], axis=0))
-    out_before = both_cores(jnp.concatenate([y_before, z_before], axis=0))
-    out_after = both_cores(jnp.concatenate([y_after, z_after], axis=0))
-    out_far = both_cores(jnp.concatenate([y_far, z_far], axis=0))
-
-    first = ring_sum(*[o[:count] for o in (out_own, out_before, out_after, out_far)], "y")
-    second = ring_sum(*[o[count:] for o in (out_own, out_before, out_after, out_far)], "z")
-    first, second = first.astype(jnp.bfloat16), second.astype(jnp.bfloat16)
-    pair = 2 * own
-    first = ring_sum(*[first[i * pair : (i + 1) * pair] for i in range(4)], "z")
-    second = ring_sum(*[second[i * pair : (i + 1) * pair] for i in range(4)], "y")
-    first, second = first.astype(jnp.bfloat16), second.astype(jnp.bfloat16)
-    moe_out = ring_sum(first[:own], first[own:], second[:own], second[own:], "x")
+
+    first_own, second_own = both_cores([[first], [second]])
+    first_before, second_before = both_cores(before)
+    first_after, second_after = both_cores(after)
+    first_far, second_far = both_cores(far)
+
+    def spread(own, before, after, far, axis):
+        return [own, shift(before, axis, -1), shift(after, axis, 1), shift(far, axis, 2)]
+
+    first, second = sums(
+        4,
+        spread(first_own, first_before, first_after, first_far, "y"),
+        spread(second_own, second_before, second_after, second_far, "z"),
+    )
+    first, second = sums(2, spread(*first, "z"), spread(*second, "y"))
+    moe_out = ring_sum(*first, *second, "x")
     mixed = (hidden + moe_out).astype(jnp.bfloat16)
     return lax.all_to_all(mixed, "exp", split_axis=1, concat_axis=0, tiled=True)
 

time: 365 us -> 377 us (1.033)
  the two profiles are of different devices: /device:TPU:0 before, /device:TPU:8 now
where the time goes in v2:
time: 377 us; the launch traced here: 372 us
  waiting for transfers between devices  134 us (36%)
  Pallas kernels  114 us (30%)
  starting transfers between devices  66.3 us (18%)
  local copies, waits for them, and re-layouts  26.2 us (7%)
  blocking collectives  11.8 us (3%)
  matrix products  10.9 us (3%)
  other arithmetic  7.69 us (2%)
    ppermute x55, waiting for transfers between devices, shift(): return lax.ppermute(value, BOTH, table(**{'d' + axis: by}))  119 us
    pallas_call x4, Pallas kernels, run_experts(): pl.pallas_call(functools.partial(experts_kernel, sizes), grid=(2 * STEPS,...  82.1 us
    ppermute x55, starting transfers between devices, shift(): return lax.ppermute(value, BOTH, table(**{'d' + axis: by}))  54.3 us
    pallas_call x6, Pallas kernels, sums(): pl.pallas_call(functools.partial(sums_kernel, sizes), grid=(4,), in_specs...  25.8 us
    unnamed x104, local copies, waits for them, and re-layouts  20.7 us
    all_to_all x1, waiting for transfers between devices, body(): lax.all_to_all(partial.reshape(count_exp, own, D), 'exp', split_axis=0, c...  15.6 us
    all_to_all x1, blocking collectives, body(): return lax.all_to_all(mixed, 'exp', split_axis=1, concat_axis=0, tiled=True)  11.8 us
  transfers between devices with their start and end apart: 57, of which 22 were waited for; matrix products, arithmetic and copies ran while one was open for 9% of the time, Pallas kernels for 27%

profile of v2, /device:TPU:8, one launch (start us, length us, event | category | flops | bytes accessed | tf_op | source)
XLA Modules:
  0.0 372.4 jit_solution(17879817436642550515)
XLA Ops:
  15.0 6.2 %all-to-all-start = ((f32[8,17,512]{2,1,0:T(8,128)}), f32[8,17,512]{2,1,0:T(8,128)S(1)}, u32[]{:S(2)}, u32[]{:S(2)}) async-start(f32[8,17,512]{2,1,0:T(8,128)} %pad_maximum_fusion.1), calls=%async_computation | async-start | bytes 786432 | tf_op jit(solution)/shard_map/all_to_all | solution.py:299
  21.9 7.8 %copy.57 = bf16[2,4096,2,256]{3,1,2,0:T(8,128)(2,1)} copy(bf16[2,4096,2,256]{3,2,1,0:T(2,128)(2,1)} %param.19) | data formatting | bytes 16777216 | tf_op args[7]
  35.8 4.3 %fusion = (f32[1024]{0:T(1024)S(1)}, f32[1024,2048]{1,0:T(8,128)S(1)}) fusion(s32[2048]{0:T(1024)S(1)} %add_bitcast_fusion, s32[2048]{0:T(1024)S(1)} %convert_reduce_fusion.1, s32[1024]{0:T(1024)S(1)} %get-tuple-element.109, s32[1024]{0:T(1024)S(1)} %get-tuple-element.110, bf16[1024,576]{1,0:T(8,128)(2,1)S(1)} %bitcast.74, ...), kind=kOutput, calls=%fused_computation.4 | convolution fusion | flops 2428500992 | bytes 11956224 | tf_op jit(solution)/shard_map/dot_general | solution.py:253
  49.6 5.7 %all-to-all-start.1 = ((bf16[8,16,4096]{2,1,0:T(8,128)(2,1)}), bf16[8,16,4096]{2,1,0:T(8,128)(2,1)S(1)}, u32[]{:S(2)}, u32[]{:S(2)}) async-start(bf16[8,16,4096]{2,1,0:T(8,128)(2,1)} %bitcast.30), calls=%async_computation.1 | async-start | bytes 2097152 | tf_op jit(solution)/shard_map/all_to_all | solution.py:327
  55.8 15.6 %all-to-all-done.1 = bf16[8,16,4096]{2,1,0:T(8,128)(2,1)S(1)} async-done(((bf16[8,16,4096]{2,1,0:T(8,128)(2,1)}), bf16[8,16,4096]{2,1,0:T(8,128)(2,1)S(1)}, u32[]{:S(2)}, u32[]{:S(2)}) %all-to-all-start.1) | async-done | bytes 1048608 | tf_op jit(solution)/shard_map/all_to_all | solution.py:327
  90.4 4.5 %collective-permute-done.8.refs_1_ = bf16[32,4224]{1,0:T(8,128)(2,1)S(1)} collective-permute-done((bf16[32,4224]{1,0:T(8,128)(2,1)}, bf16[32,4224]{1,0:T(8,128)(2,1)S(1)}, u32[]{:S(2)}, u32[]{:S(2)}) %collective-permute-start.8) | collective-permute-done | bytes 270368 | tf_op jit(solution)/shard_map/ppermute | solution.py:36
  99.1 4.0 %collective-permute-done.13.refs_7_ = bf16[32,4224]{1,0:T(8,128)(2,1)S(1)} collective-permute-done((bf16[32,4224]{1,0:T(8,128)(2,1)}, bf16[32,4224]{1,0:T(8,128)(2,1)S(1)}, u32[]{:S(2)}, u32[]{:S(2)}) %collective-permute-start.13) | collective-permute-done | bytes 270368 | tf_op jit(solution)/shard_map/ppermute | solution.py:36
  103.8 3.8 %shard_map.119 = (bf16[128,4224]{1,0:T(8,128)(2,1)}, bf16[128,4224]{1,0:T(8,128)(2,1)}) custom-call(bf16[32,4224]{1,0:T(8,128)(2,1)} %get-tuple-element.48.refs_0_, bf16[32,4224]{1,0:T(8,128)(2,1)} %copy-done.18, bf16[32,4224]{1,0:T(8,128)(2,1)} %copy-done.19, bf16[32,4224]{1,0:T(8,128)(2,1)} %copy-done.20, bf16[32,4224]{1,0:T(8,128)(2,1)} %get-tuple-element.49.refs_4_, ...), custom_call_target="tpu_custom_call" | custom-call | bytes 4325376 | tf_op jit(solution)/shard_map/pallas_call | solution.py:84
  112.9 17.0 %collective-permute-done.18.refs_2_.refs_6_ = bf16[128,4224]{1,0:T(8,128)(2,1)} collective-permute-done((bf16[128,4224]{1,0:T(8,128)(2,1)}, bf16[128,4224]{1,0:T(8,128)(2,1)}, u32[]{:S(2)}, u32[]{:S(2)}) %collective-permute-start.18) | collective-permute-done | bytes 1081376 | tf_op jit(solution)/shard_map/ppermute | solution.py:36
  140.1 7.0 %collective-permute-done.32.refs_4_.refs_12_ = bf16[64,4224]{1,0:T(8,128)(2,1)} collective-permute-done((bf16[64,4224]{1,0:T(8,128)(2,1)S(1)}, bf16[64,4224]{1,0:T(8,128)(2,1)}, u32[]{:S(2)}, u32[]{:S(2)}) %collective-permute-start.32) | collective-permute-done | bytes 540704 | tf_op jit(solution)/shard_map/ppermute | solution.py:36
  150.3 20.5 %shard_map.122 = (bf16[128,4096]{1,0:T(8,128)(2,1)}, bf16[128,4096]{1,0:T(8,128)(2,1)}, bf16[128,4096]{1,0:T(8,128)(2,1)}, bf16[128,4096]{1,0:T(8,128)(2,1)}) custom-call(bf16[128,4224]{1,0:T(8,128)(2,1)} %collective-permute-done.19.refs_0_.refs_4_, bf16[128,4224]{1,0:T(8,128)(2,1)} %collective-permute-done.21.refs_1_.refs_5_, ...), custom_call_target="tpu_custom_call" | custom-call | flops 6442450944 | bytes 20971520 | tf_op jit(solution)/shard_map/pallas_call | solution.py:191
  174.9 20.4 %shard_map.124 = (bf16[128,4096]{1,0:T(8,128)(2,1)}, bf16[128,4096]{1,0:T(8,128)(2,1)}, bf16[128,4096]{1,0:T(8,128)(2,1)}, bf16[128,4096]{1,0:T(8,128)(2,1)}) custom-call(bf16[128,4224]{1,0:T(8,128)(2,1)} %collective-permute-done.26.refs_0_.refs_4_, bf16[128,4224]{1,0:T(8,128)(2,1)} %collective-permute-done.28.refs_1_.refs_5_, bf16[128,4224]{1,0:T(8,128)(2,1)} %copy-done.24, ...), custom_call_target="tpu_custom_call" | custom-call | flops 6442450944 | bytes 20971520 | tf_op jit(solution)/shard_map/pallas_call | solution.py:191
  199.3 20.4 %shard_map.120 = (bf16[128,4096]{1,0:T(8,128)(2,1)}, bf16[128,4096]{1,0:T(8,128)(2,1)}, bf16[128,4096]{1,0:T(8,128)(2,1)}, bf16[128,4096]{1,0:T(8,128)(2,1)}) custom-call(bf16[128,4224]{1,0:T(8,128)(2,1)} %copy-done.38, bf16[128,4224]{1,0:T(8,128)(2,1)} %copy-done.39, bf16[128,4224]{1,0:T(8,128)(2,1)} %get-tuple-element.50.refs_2_.refs_6_, ...), custom_call_target="tpu_custom_call" | custom-call | flops 6442450944 | bytes 20971520 | tf_op jit(solution)/shard_map/pallas_call | solution.py:191
  220.5 20.7 %shard_map.126 = (bf16[128,4096]{1,0:T(8,128)(2,1)}, bf16[128,4096]{1,0:T(8,128)(2,1)}, bf16[128,4096]{1,0:T(8,128)(2,1)}, bf16[128,4096]{1,0:T(8,128)(2,1)}) custom-call(bf16[64,4224]{1,0:T(8,128)(2,1)} %copy-done.41, bf16[64,4224]{1,0:T(8,128)(2,1)} %copy-done.42, bf16[64,4224]{1,0:T(8,128)(2,1)} %copy-done.43, bf16[64,4224]{1,0:T(8,128)(2,1)} %copy-done.44, ...), custom_call_target="tpu_custom_call" | custom-call | flops 6442450944 | bytes 20971520 | tf_op jit(solution)/shard_map/pallas_call | solution.py:191
  243.0 4.3 %shard_map.123 = (bf16[128,4096]{1,0:T(8,128)(2,1)}, bf16[128,4096]{1,0:T(8,128)(2,1)}) custom-call(bf16[128,4096]{1,0:T(8,128)(2,1)} %get-tuple-element.58.refs_0_, bf16[128,4096]{1,0:T(8,128)(2,1)} %copy-done.6, bf16[128,4096]{1,0:T(8,128)(2,1)} %get-tuple-element.60.refs_2_, bf16[128,4096]{1,0:T(8,128)(2,1)} %copy-done.8), custom_call_target="tpu_custom_call" | custom-call | bytes 6291456 | tf_op jit(solution)/shard_map/pallas_call | solution.py:117
  248.6 4.2 %shard_map.125 = (bf16[128,4096]{1,0:T(8,128)(2,1)}, bf16[128,4096]{1,0:T(8,128)(2,1)}) custom-call(bf16[128,4096]{1,0:T(8,128)(2,1)} %get-tuple-element.63.refs_0_, bf16[128,4096]{1,0:T(8,128)(2,1)} %copy-done.4, bf16[128,4096]{1,0:T(8,128)(2,1)} %get-tuple-element.65.refs_2_, bf16[128,4096]{1,0:T(8,128)(2,1)} %copy-done.5), custom_call_target="tpu_custom_call" | custom-call | bytes 6291456 | tf_op jit(solution)/shard_map/pallas_call | solution.py:117
  254.9 4.2 %shard_map.127 = (bf16[128,4096]{1,0:T(8,128)(2,1)}, bf16[128,4096]{1,0:T(8,128)(2,1)}) custom-call(bf16[128,4096]{1,0:T(8,128)(2,1)} %get-tuple-element.68.refs_0_, bf16[128,4096]{1,0:T(8,128)(2,1)} %copy-done.9, bf16[128,4096]{1,0:T(8,128)(2,1)} %get-tuple-element.70.refs_2_, bf16[128,4096]{1,0:T(8,128)(2,1)} %copy-done.10), custom_call_target="tpu_custom_call" | custom-call | bytes 6291456 | tf_op jit(solution)/shard_map/pallas_call | solution.py:117
  263.1 32.5 %collective-permute-done.24.refs_1_ = bf16[128,4096]{1,0:T(8,128)(2,1)S(1)} collective-permute-done((bf16[128,4096]{1,0:T(8,128)(2,1)}, bf16[128,4096]{1,0:T(8,128)(2,1)S(1)}, u32[]{:S(2)}, u32[]{:S(2)}) %collective-permute-start.24) | collective-permute-done | bytes 1048608 | tf_op jit(solution)/shard_map/ppermute | solution.py:36
  297.1 4.2 %shard_map.121 = (bf16[128,4096]{1,0:T(8,128)(2,1)}, bf16[128,4096]{1,0:T(8,128)(2,1)}) custom-call(bf16[128,4096]{1,0:T(8,128)(2,1)} %get-tuple-element.53.refs_0_, bf16[128,4096]{1,0:T(8,128)(2,1)} %copy-done.3, bf16[128,4096]{1,0:T(8,128)(2,1)} %get-tuple-element.55.refs_2_, bf16[128,4096]{1,0:T(8,128)(2,1)} %copy-done.7), custom_call_target="tpu_custom_call" | custom-call | bytes 6291456 | tf_op jit(solution)/shard_map/pallas_call | solution.py:117
  301.4 20.5 %collective-permute-done.45.refs_7_ = bf16[128,4096]{1,0:T(8,128)(2,1)} collective-permute-done((bf16[128,4096]{1,0:T(8,128)(2,1)}, bf16[128,4096]{1,0:T(8,128)(2,1)}, u32[]{:S(2)}, u32[]{:S(2)}) %collective-permute-start.45) | collective-permute-done | bytes 1048608 | tf_op jit(solution)/shard_map/ppermute | solution.py:36
  321.9 5.5 %shard_map.128 = (bf16[32,4096]{1,0:T(8,128)(2,1)}, bf16[32,4096]{1,0:T(8,128)(2,1)}, bf16[32,4096]{1,0:T(8,128)(2,1)}, bf16[32,4096]{1,0:T(8,128)(2,1)}, bf16[3...) custom-call(bf16[128,4096]{1,0:T(8,128)(2,1)} %get-tuple-element.57.refs_0_,, ...), custom_call_target="tpu_custom_call" | custom-call | bytes 10485760 | tf_op jit(solution)/shard_map/pallas_call | solution.py:117
  333.1 3.9 %collective-permute-done.46.refs_1_ = bf16[32,4096]{1,0:T(8,128)(2,1)S(1)} collective-permute-done((bf16[32,4096]{1,0:T(8,128)(2,1)}, bf16[32,4096]{1,0:T(8,128)(2,1)S(1)}, u32[]{:S(2)}, u32[]{:S(2)}) %collective-permute-start.46) | collective-permute-done | bytes 262176 | tf_op jit(solution)/shard_map/ppermute | solution.py:36
  336.9 4.4 %collective-permute-done.47.refs_2_ = bf16[32,4096]{1,0:T(8,128)(2,1)S(1)} collective-permute-done((bf16[32,4096]{1,0:T(8,128)(2,1)}, bf16[32,4096]{1,0:T(8,128)(2,1)S(1)}, u32[]{:S(2)}, u32[]{:S(2)}) %collective-permute-start.47) | collective-permute-done | bytes 262176 | tf_op jit(solution)/shard_map/ppermute | solution.py:36
  359.8 11.8 %all_to_all.29 = bf16[16,8,512]{2,0,1:T(8,128)(2,1)S(1)} all-to-all(bf16[16,8,512]{2,0,1:T(8,128)(2,1)S(1)} %bitcast.81), channel_id=1, replica_groups=mesh['ctx'=16,'exp'=8] {'exp'}, dimensions={1} | all-to-all | bytes 262144 | tf_op jit(solution)/shard_map/all_to_all | solution.py:364
  (250 shorter events, 118.2 us)
Async XLA Ops:
  15.0 34.6 %all-to-all-start = ((f32[8,17,512]{2,1,0:T(8,128)}), f32[8,17,512]{2,1,0:T(8,128)S(1)}, u32[]{:S(2)}, u32[]{:S(2)}) async-start(f32[8,17,512]{2,1,0:T(8,128)} %pad_maximum_fusion.1), calls=%async_computation | async-start | bytes 786432 | tf_op jit(solution)/shard_map/all_to_all | solution.py:299
  108.5 22.7 %collective-permute-start.20 = (bf16[128,4224]{1,0:T(8,128)(2,1)}, bf16[128,4224]{1,0:T(8,128)(2,1)}, u32[]{:S(2)}, u32[]{:S(2)}) collective-permute-start(bf16[128,4224]{1,0:T(8,128)(2,1)} %get-tuple-element.51.refs_3_.refs_7_), channel_id=1, source_target_pairs={{0,2},{8,10},{2,4},{10,12},{4,6},{12,14},{6,0},{14,8},{16,18},{24,... | collective-permute-start | bytes 3244040 | tf_op jit(solution)/shard_map/ppermute | solution.py:36
  108.9 23.4 %collective-permute-start.14 = (bf16[128,4224]{1,0:T(8,128)(2,1)}, bf16[128,4224]{1,0:T(8,128)(2,1)S(1)}, u32[]{:S(2)}, u32[]{:S(2)}) collective-permute-start(bf16[128,4224]{1,0:T(8,128)(2,1)} %get-tuple-element.50.refs_2_.refs_6_), channel_id=1, source_target_pairs={{0,8},{8,0},{2,10},{10,2},{4,12},{12,4},{6,14},{14,6},{16,24},{24,... | collective-permute-start | bytes 3244040 | tf_op jit(solution)/shard_map/ppermute | solution.py:36
  108.9 27.8 %collective-permute-start.25 = (bf16[128,4224]{1,0:T(8,128)(2,1)}, bf16[128,4224]{1,0:T(8,128)(2,1)S(1)}, u32[]{:S(2)}, u32[]{:S(2)}) collective-permute-start(bf16[128,4224]{1,0:T(8,128)(2,1)} %get-tuple-element.50.refs_2_.refs_6_), channel_id=1, source_target_pairs={{0,48},{8,56},{2,50},{10,58},{4,52},{12,60},{6,54},{14,62},{16,0},... | collective-permute-start | bytes 3244040 | tf_op jit(solution)/shard_map/ppermute | solution.py:36
  110.1 26.7 %collective-permute-start.27 = (bf16[128,4224]{1,0:T(8,128)(2,1)}, bf16[128,4224]{1,0:T(8,128)(2,1)}, u32[]{:S(2)}, u32[]{:S(2)}) collective-permute-start(bf16[128,4224]{1,0:T(8,128)(2,1)} %get-tuple-element.51.refs_3_.refs_7_), channel_id=1, source_target_pairs={{0,6},{8,14},{2,0},{10,8},{4,2},{12,10},{6,4},{14,12},{16,22},{24,... | collective-permute-start | bytes 3244040 | tf_op jit(solution)/shard_map/ppermute | solution.py:36
  136.7 37.2 %collective-permute-start.26 = (bf16[128,4224]{1,0:T(8,128)(2,1)S(1)}, bf16[128,4224]{1,0:T(8,128)(2,1)}, u32[]{:S(2)}, u32[]{:S(2)}) collective-permute-start(bf16[128,4224]{1,0:T(8,128)(2,1)S(1)} %collective-permute-done.25.refs_2_.refs_6_), channel_id=1, source_target_pairs={{0,8},{8,0},{2,10},{10,2},{4,12},{12,4},{6,14},{14,6},{16,24},{24,... | collective-permute-start | bytes 3244040 | tf_op jit(solution)/shard_map/ppermute | solution.py:36
  136.8 37.7 %collective-permute-start.28 = (bf16[128,4224]{1,0:T(8,128)(2,1)}, bf16[128,4224]{1,0:T(8,128)(2,1)}, u32[]{:S(2)}, u32[]{:S(2)}) collective-permute-start(bf16[128,4224]{1,0:T(8,128)(2,1)} %collective-permute-done.27.refs_3_.refs_7_), channel_id=1, source_target_pairs={{0,8},{8,0},{2,10},{10,2},{4,12},{12,4},{6,14},{14,6},{16,24},{24,... | collective-permute-start | bytes 3244040 | tf_op jit(solution)/shard_map/ppermute | solution.py:36
  147.1 48.7 %collective-permute-start.15 = (bf16[128,4224]{1,0:T(8,128)(2,1)S(1)}, bf16[128,4224]{1,0:T(8,128)(2,1)S(1)}, u32[]{:S(2)}, u32[]{:S(2)}) collective-permute-start(bf16[128,4224]{1,0:T(8,128)(2,1)S(1)} %copy-done.37), channel_id=1, source_target_pairs={{0,8},{8,0},{2,10},{10,2},{4,12},{12,4},{6,14},{14,6},{16,24},{24,... | collective-permute-start | bytes 3244040 | tf_op jit(solution)/shard_map/ppermute | solution.py:36
  147.1 23.6 %collective-permute-start.34 = (bf16[64,4224]{1,0:T(8,128)(2,1)S(1)}, bf16[64,4224]{1,0:T(8,128)(2,1)S(1)}, u32[]{:S(2)}, u32[]{:S(2)}) collective-permute-start(bf16[64,4224]{1,0:T(8,128)(2,1)S(1)} %slice.46), channel_id=1, source_target_pairs={{0,48},{8,56},{2,50},{10,58},{4,52},{12,60},{6,54},{14,62},{16,0},... | collective-permute-start | bytes 1622024 | tf_op jit(solution)/shard_map/ppermute | solution.py:36
  150.1 23.8 %collective-permute-start.36 = (bf16[64,4224]{1,0:T(8,128)(2,1)S(1)}, bf16[64,4224]{1,0:T(8,128)(2,1)}, u32[]{:S(2)}, u32[]{:S(2)}) collective-permute-start(bf16[64,4224]{1,0:T(8,128)(2,1)S(1)} %slice.47), channel_id=1, source_target_pairs={{0,2},{8,10},{2,4},{10,12},{4,6},{12,14},{6,0},{14,8},{16,18},{24,... | collective-permute-start | bytes 1622024 | tf_op jit(solution)/shard_map/ppermute | solution.py:36
  170.8 24.6 %collective-permute-start.38 = (bf16[64,4224]{1,0:T(8,128)(2,1)S(1)}, bf16[64,4224]{1,0:T(8,128)(2,1)}, u32[]{:S(2)}, u32[]{:S(2)}) collective-permute-start(bf16[64,4224]{1,0:T(8,128)(2,1)S(1)} %slice.48), channel_id=1, source_target_pairs={{0,6},{8,14},{2,0},{10,8},{4,2},{12,10},{6,4},{14,12},{16,22},{24,... | collective-permute-start | bytes 1622024 | tf_op jit(solution)/shard_map/ppermute | solution.py:36
  173.9 23.3 %collective-permute-start.35 = (bf16[64,4224]{1,0:T(8,128)(2,1)S(1)}, bf16[64,4224]{1,0:T(8,128)(2,1)S(1)}, u32[]{:S(2)}, u32[]{:S(2)}) collective-permute-start(bf16[64,4224]{1,0:T(8,128)(2,1)S(1)} %collective-permute-done.34.refs_5_.refs_13_), channel_id=1, source_target_pairs={{0,8},{8,0},{2,10},{10,2},{4,12},{12,4},{6,14},{14,6},{16,24},{24,... | collective-permute-start | bytes 1622024 | tf_op jit(solution)/shard_map/ppermute | solution.py:36
  174.4 23.8 %collective-permute-start.37 = (bf16[64,4224]{1,0:T(8,128)(2,1)}, bf16[64,4224]{1,0:T(8,128)(2,1)S(1)}, u32[]{:S(2)}, u32[]{:S(2)}) collective-permute-start(bf16[64,4224]{1,0:T(8,128)(2,1)} %collective-permute-done.36.refs_6_.refs_14_), channel_id=1, source_target_pairs={{0,8},{8,0},{2,10},{10,2},{4,12},{12,4},{6,14},{14,6},{16,24},{24,... | collective-permute-start | bytes 1622024 | tf_op jit(solution)/shard_map/ppermute | solution.py:36
  195.4 24.3 %collective-permute-start.39 = (bf16[64,4224]{1,0:T(8,128)(2,1)}, bf16[64,4224]{1,0:T(8,128)(2,1)S(1)}, u32[]{:S(2)}, u32[]{:S(2)}) collective-permute-start(bf16[64,4224]{1,0:T(8,128)(2,1)} %collective-permute-done.38.refs_7_.refs_15_), channel_id=1, source_target_pairs={{0,8},{8,0},{2,10},{10,2},{4,12},{12,4},{6,14},{14,6},{16,24},{24,... | collective-permute-start | bytes 1622024 | tf_op jit(solution)/shard_map/ppermute | solution.py:36
  195.9 45.7 %collective-permute-start.22 = (bf16[128,4096]{1,0:T(8,128)(2,1)}, bf16[128,4096]{1,0:T(8,128)(2,1)S(1)}, u32[]{:S(2)}, u32[]{:S(2)}) collective-permute-start(bf16[128,4096]{1,0:T(8,128)(2,1)} %get-tuple-element.59), channel_id=1, source_target_pairs={{0,8},{8,0},{2,10},{10,2},{4,12},{12,4},{6,14},{14,6},{16,24},{24,... | collective-permute-start | bytes 3145736 | tf_op jit(solution)/shard_map/ppermute | solution.py:36
  196.9 45.0 %collective-permute-start.23 = (bf16[128,4096]{1,0:T(8,128)(2,1)}, bf16[128,4096]{1,0:T(8,128)(2,1)S(1)}, u32[]{:S(2)}, u32[]{:S(2)}) collective-permute-start(bf16[128,4096]{1,0:T(8,128)(2,1)} %get-tuple-element.61), channel_id=1, source_target_pairs={{0,8},{8,0},{2,10},{10,2},{4,12},{12,4},{6,14},{14,6},{16,24},{24,... | collective-permute-start | bytes 3145736 | tf_op jit(solution)/shard_map/ppermute | solution.py:36
  198.0 49.3 %collective-permute-start.29 = (bf16[128,4096]{1,0:T(8,128)(2,1)}, bf16[128,4096]{1,0:T(8,128)(2,1)S(1)}, u32[]{:S(2)}, u32[]{:S(2)}) collective-permute-start(bf16[128,4096]{1,0:T(8,128)(2,1)} %get-tuple-element.64), channel_id=1, source_target_pairs={{0,8},{8,0},{2,10},{10,2},{4,12},{12,4},{6,14},{14,6},{16,24},{24,... | collective-permute-start | bytes 3145736 | tf_op jit(solution)/shard_map/ppermute | solution.py:36
  199.0 48.6 %collective-permute-start.30 = (bf16[128,4096]{1,0:T(8,128)(2,1)}, bf16[128,4096]{1,0:T(8,128)(2,1)S(1)}, u32[]{:S(2)}, u32[]{:S(2)}) collective-permute-start(bf16[128,4096]{1,0:T(8,128)(2,1)} %get-tuple-element.66), channel_id=1, source_target_pairs={{0,8},{8,0},{2,10},{10,2},{4,12},{12,4},{6,14},{14,6},{16,24},{24,... | collective-permute-start | bytes 3145736 | tf_op jit(solution)/shard_map/ppermute | solution.py:36
  247.6 48.0 %collective-permute-start.24 = (bf16[128,4096]{1,0:T(8,128)(2,1)}, bf16[128,4096]{1,0:T(8,128)(2,1)S(1)}, u32[]{:S(2)}, u32[]{:S(2)}) collective-permute-start(bf16[128,4096]{1,0:T(8,128)(2,1)} %get-tuple-element.62), channel_id=1, source_target_pairs={{0,48},{8,56},{2,50},{10,58},{4,52},{12,60},{6,54},{14,62},{16,0},... | collective-permute-start | bytes 3145736 | tf_op jit(solution)/shard_map/ppermute | solution.py:36
  252.8 48.6 %collective-permute-start.31 = (bf16[128,4096]{1,0:T(8,128)(2,1)}, bf16[128,4096]{1,0:T(8,128)(2,1)S(1)}, u32[]{:S(2)}, u32[]{:S(2)}) collective-permute-start(bf16[128,4096]{1,0:T(8,128)(2,1)} %get-tuple-element.67), channel_id=1, source_target_pairs={{0,16},{8,24},{2,18},{10,26},{4,20},{12,28},{6,22},{14,30},{16,32}... | collective-permute-start | bytes 3145736 | tf_op jit(solution)/shard_map/ppermute | solution.py:36
  259.1 42.2 %collective-permute-start.42 = (bf16[128,4096]{1,0:T(8,128)(2,1)}, bf16[128,4096]{1,0:T(8,128)(2,1)S(1)}, u32[]{:S(2)}, u32[]{:S(2)}) collective-permute-start(bf16[128,4096]{1,0:T(8,128)(2,1)} %get-tuple-element.72), channel_id=1, source_target_pairs={{0,32},{8,40},{2,34},{10,42},{4,36},{12,44},{6,38},{14,46},{16,48}... | collective-permute-start | bytes 3145736 | tf_op jit(solution)/shard_map/ppermute | solution.py:36
  260.9 40.5 %collective-permute-start.43 = (bf16[128,4096]{1,0:T(8,128)(2,1)}, bf16[128,4096]{1,0:T(8,128)(2,1)S(1)}, u32[]{:S(2)}, u32[]{:S(2)}) collective-permute-start(bf16[128,4096]{1,0:T(8,128)(2,1)} %get-tuple-element.74), channel_id=1, source_target_pairs={{0,6},{8,14},{2,0},{10,8},{4,2},{12,10},{6,4},{14,12},{16,22},{24,... | collective-permute-start | bytes 3145736 | tf_op jit(solution)/shard_map/ppermute | solution.py:36
  261.0 40.4 %collective-permute-start.44 = (bf16[128,4096]{1,0:T(8,128)(2,1)}, bf16[128,4096]{1,0:T(8,128)(2,1)S(1)}, u32[]{:S(2)}, u32[]{:S(2)}) collective-permute-start(bf16[128,4096]{1,0:T(8,128)(2,1)} %get-tuple-element.75), channel_id=1, source_target_pairs={{0,2},{8,10},{2,4},{10,12},{4,6},{12,14},{6,0},{14,8},{16,18},{24,... | collective-permute-start | bytes 3145736 | tf_op jit(solution)/shard_map/ppermute | solution.py:36
  295.6 26.3 %collective-permute-start.45 = (bf16[128,4096]{1,0:T(8,128)(2,1)}, bf16[128,4096]{1,0:T(8,128)(2,1)}, u32[]{:S(2)}, u32[]{:S(2)}) collective-permute-start(bf16[128,4096]{1,0:T(8,128)(2,1)} %get-tuple-element.76), channel_id=1, source_target_pairs={{0,4},{8,12},{2,6},{10,14},{4,0},{12,8},{6,2},{14,10},{16,20},{24,... | collective-permute-start | bytes 3145736 | tf_op jit(solution)/shard_map/ppermute | solution.py:36
  (81 other events, 903.2 us)

commit v3 on v2

--- a/solution.py
+++ b/solution.py
@@ -55,7 +55,7 @@
     return add_up(own, shift(before, axis, -1), shift(after, axis, 1), shift(far, axis, 2))
 
 
-VMEM_LIMIT = 56 * 1024 * 1024
+MIB = 1024 * 1024
 
 
 def grouped(refs, sizes):
@@ -87,50 +87,14 @@
         in_specs=[pl.BlockSpec((block.shape[0], tile), lambda i: (0, i)) for block in blocks],
         out_specs=[pl.BlockSpec((height, tile), lambda i: (0, i)) for height in heights],
         out_shape=[jax.ShapeDtypeStruct((height, width), jnp.bfloat16) for height in heights],
-        compiler_params=pltpu.CompilerParams(vmem_limit_bytes=VMEM_LIMIT),
+        compiler_params=pltpu.CompilerParams(vmem_limit_bytes=16 * MIB),
         cost_estimate=pl.CostEstimate(
             flops=0, bytes_accessed=4 * sum(heights) * width, transcendentals=0
         ),
     )(*blocks)
 
 
-def sums_kernel(sizes, *refs):
-    count = sum(sizes)
-    outs = refs[count:]
-    parts = len(outs) // len(sizes)
-    for at, group in enumerate(grouped(refs[:count], sizes)):
-        total = group[0][...].astype(jnp.float32)
-        for ref in group[1:]:
-            total = total + ref[...].astype(jnp.float32)
-        total = total.astype(jnp.bfloat16)
-        rows = total.shape[0] // parts
-        for part in range(parts):
-            outs[at * parts + part][...] = total[part * rows : (part + 1) * rows]
-
-
-def sums(parts, *groups):
-    sizes = tuple(len(group) for group in groups)
-    blocks = [block for group in groups for block in group]
-    width = blocks[0].shape[1]
-    heights = [group[0].shape[0] // parts for group in groups for _ in range(parts)]
-    tile = width // 4
-    outs = pl.pallas_call(
-        functools.partial(sums_kernel, sizes),
-        grid=(4,),
-        in_specs=[pl.BlockSpec((block.shape[0], tile), lambda i: (0, i)) for block in blocks],
-        out_specs=[pl.BlockSpec((height, tile), lambda i: (0, i)) for height in heights],
-        out_shape=[jax.ShapeDtypeStruct((height, width), jnp.bfloat16) for height in heights],
-        compiler_params=pltpu.CompilerParams(vmem_limit_bytes=VMEM_LIMIT),
-        cost_estimate=pl.CostEstimate(
-            flops=0,
-            bytes_accessed=2 * width * (sum(heights) + sum(b.shape[0] for b in blocks)),
-            transcendentals=0,
-        ),
-    )(*blocks)
-    return grouped(outs, [parts] * len(groups))
-
-
-STEPS = 4
+STEPS = 2
 
 
 def experts_kernel(sizes, *refs):
@@ -142,21 +106,17 @@
     step = pl.program_id(0)
     units = up.shape[3]
 
+    @pl.when(step == 0)
+    def _():
+        pre[...] = jnp.zeros_like(pre)
+
     @pl.when(step < STEPS)
     def _():
         rows = jnp.concatenate([block[...] for block in blocks], axis=0)
-        for e in range(up.shape[0]):
-            for g in range(2):
-                columns = slice((2 * e + g) * units, (2 * e + g + 1) * units)
-                product = jnp.dot(rows, up[e, g], preferred_element_type=jnp.float32)
-
-                @pl.when(step == 0)
-                def _():
-                    pre[:, columns] = product
-
-                @pl.when(step > 0)
-                def _():
-                    pre[:, columns] += product
+        weights = jnp.concatenate(
+            [up[e, g] for e in range(up.shape[0]) for g in range(2)], axis=1
+        )
+        pre[...] += jnp.dot(rows, weights, preferred_element_type=jnp.float32)
 
     @pl.when(step == STEPS - 1)
     def _():
@@ -204,11 +164,9 @@
             pltpu.VMEM((height, experts * 2 * units), jnp.float32),
             pltpu.VMEM((height, experts * units), jnp.bfloat16),
         ],
-        compiler_params=pltpu.CompilerParams(vmem_limit_bytes=VMEM_LIMIT),
+        compiler_params=pltpu.CompilerParams(vmem_limit_bytes=40 * MIB),
         cost_estimate=pl.CostEstimate(
-            flops=6 * height * D * experts * units,
-            bytes_accessed=6 * experts * units * D + 4 * height * D,
-            transcendentals=height * experts * units,
+            flops=0, bytes_accessed=4096, transcendentals=0
         ),
     )(*blocks, *blocks, up, down, pick)
 
@@ -217,7 +175,7 @@
     return jnp.sum((positions[:, None] >= doc_ends[None, :]).astype(jnp.int32), axis=1)
 
 
-def attention(latent, query, w_uk, w_uv, doc_lengths, up):
+def attention(latent, query, w_uk, w_uv, doc_lengths):
     tokens = latent.shape[0]
     heads = w_uk.shape[0]
     qk_width = NOPE + ROPE
@@ -228,7 +186,6 @@
     pair = jnp.concatenate([latent, shift(latent, "x", 2)], axis=0)
     half = jnp.concatenate(ring(pair, "y"), axis=0)
     piece = jnp.concatenate([half, other_core(half)], axis=0)
-    piece, up = lax.optimization_barrier((piece, up))
     starts = [
         (((x_hi + dx) % 2 * 4 + (y + dy) % 4) * 2 + (core + dc) % 2) * tokens
         for dc in (0, 1)
@@ -264,7 +221,7 @@
         .astype(jnp.bfloat16)
         .reshape(tokens, heads * VDIM)
     )
-    return head_out, up
+    return head_out
 
 
 def body(
@@ -316,17 +273,23 @@
     up = jnp.transpose(w_in, (0, 2, 1, 3))
     down = w_out.reshape(local_experts * units, D)
 
-    def both_cores(groups):
+    def own_and_theirs(groups):
         theirs = [[other_core(block) for block in group] for group in groups]
-        result = run_experts(theirs + groups, up, down, pick)
-        back = [other_core(block) for block in result[: len(groups)]]
-        return [total for (total,) in sums(1, *zip(result[len(groups) :], back))]
-
-    head_out, up = attention(latent, query, w_uk, w_uv, doc_lengths, up)
+        return run_experts(theirs + groups, up, down, pick)
+
+    def both_cores(result):
+        half = len(result) // 2
+        return [
+            add_up(here, other_core(there)).astype(jnp.bfloat16)
+            for there, here in zip(result[:half], result[half:])
+        ]
+
+    head_out = attention(latent, query, w_uk, w_uv, doc_lengths)
     partial = jnp.dot(head_out, w_o, preferred_element_type=jnp.float32).astype(jnp.bfloat16)
     parts = lax.all_to_all(
         partial.reshape(count_exp, own, D), "exp", split_axis=0, concat_axis=0
     )
+    parts, up = lax.optimization_barrier((parts, up))
     hidden = residual_rows + jnp.sum(parts.astype(jnp.float32), axis=0)
     squares = jnp.mean(hidden * hidden, axis=1, keepdims=True)
     normed = (hidden * lax.rsqrt(squares + epsilon) * gain[None, :]).astype(jnp.bfloat16)
@@ -336,30 +299,37 @@
     first, second = stack([x_own, x_before], [x_after, x_far])
     first, second = stack(ring(first, "z"), ring(second, "y"))
     near = first.shape[0] // 2
-    before, after, far = [], [], []
+    before, after = [], []
     for block, axis in ((first, "y"), (second, "z")):
         before.append([shift(block, axis, 1)])
         after.append([shift(block, axis, -1)])
-    for i, axis in enumerate("yz"):
-        far.append(
-            [shift(before[i][0][:near], axis, 1), shift(after[i][0][near:], axis, -1)]
-        )
-
-    first_own, second_own = both_cores([[first], [second]])
-    first_before, second_before = both_cores(before)
-    first_after, second_after = both_cores(after)
-    first_far, second_far = both_cores(far)
-
-    def spread(own, before, after, far, axis):
-        return [own, shift(before, axis, -1), shift(after, axis, 1), shift(far, axis, 2)]
-
-    first, second = sums(
-        4,
-        spread(first_own, first_before, first_after, first_far, "y"),
-        spread(second_own, second_before, second_after, second_far, "z"),
-    )
-    first, second = sums(2, spread(*first, "z"), spread(*second, "y"))
-    moe_out = ring_sum(*first, *second, "x")
+    at_own = own_and_theirs([[first], [second]])
+    before, after, at_own = lax.optimization_barrier((before, after, at_own))
+    far = [
+        [shift(before[i][0][:near], axis, 1), shift(after[i][0][near:], axis, -1)]
+        for i, axis in enumerate("yz")
+    ]
+    at_before = own_and_theirs(before)
+    at_after = own_and_theirs(after)
+    far, at_before, at_after = lax.optimization_barrier((far, at_before, at_after))
+    sum_own = both_cores(at_own)
+    sum_before = both_cores(at_before)
+    sum_after = both_cores(at_after)
+    sent = [
+        (shift(sum_before[i], axis, -1), shift(sum_after[i], axis, 1))
+        for i, axis in enumerate("yz")
+    ]
+    sent, at_far = lax.optimization_barrier((sent, own_and_theirs(far)))
+    sum_far = both_cores(at_far)
+    first, second = [
+        add_up(sum_own[i], *sent[i], shift(sum_far[i], axis, 2)).astype(jnp.bfloat16)
+        for i, axis in enumerate("yz")
+    ]
+    pair = 2 * own
+    first = ring_sum(*[first[i * pair : (i + 1) * pair] for i in range(4)], "z")
+    second = ring_sum(*[second[i * pair : (i + 1) * pair] for i in range(4)], "y")
+    first, second = first.astype(jnp.bfloat16), second.astype(jnp.bfloat16)
+    moe_out = ring_sum(first[:own], first[own:], second[:own], second[own:], "x")
     mixed = (hidden + moe_out).astype(jnp.bfloat16)
     return lax.all_to_all(mixed, "exp", split_axis=1, concat_axis=0, tiled=True)
 

time: 377 us -> 277 us (0.73)
  the two profiles are of different devices: /device:TPU:8 before, /device:TPU:0 now
where the time goes in v3:
time: 277 us; the launch traced here: 274 us
  waiting for transfers between devices  91.2 us (33%)
  starting transfers between devices  72.4 us (26%)
  Pallas kernels  47.1 us (17%)
  local copies, waits for them, and re-layouts  27.5 us (10%)
  matrix products  14.3 us (5%)
  other arithmetic  11.1 us (4%)
  blocking collectives  9.36 us (3%)
    ppermute x55, waiting for transfers between devices, shift(): return lax.ppermute(value, BOTH, table(**{'d' + axis: by}))  83.5 us
    ppermute x55, starting transfers between devices, shift(): return lax.ppermute(value, BOTH, table(**{'d' + axis: by}))  59.7 us
    pallas_call x4, Pallas kernels, run_experts(): pl.pallas_call(functools.partial(experts_kernel, sizes), grid=(2 * STEPS,...  44.8 us
    unnamed x50, local copies, waits for them, and re-layouts  19.7 us
    all_to_all x1, blocking collectives, body(): return lax.all_to_all(mixed, 'exp', split_axis=1, concat_axis=0, tiled=True)  9.36 us
    all_to_all x1, waiting for transfers between devices, body(): lax.all_to_all(partial.reshape(count_exp, own, D), 'exp', split_axis=0, c...  7.7 us
    all_to_all x1, starting transfers between devices, body(): lax.all_to_all(partial.reshape(count_exp, own, D), 'exp', split_axis=0, c...  6.45 us
    all_to_all x1, starting transfers between devices, body(): got = lax.all_to_all(sent, 'exp', split_axis=0, concat_axis=0)  6.24 us
  transfers between devices with their start and end apart: 57, of which 30 were waited for; matrix products, arithmetic and copies ran while one was open for 16% of the time, Pallas kernels for 16%

profile of v3, /device:TPU:0, one launch (start us, length us, event | category | flops | bytes accessed | tf_op | source)
XLA Modules:
  0.0 273.7 jit_solution(9744204036017500961)
XLA Ops:
  0.0 3.2 %collective-permute-start = (bf16[128,576]{0,1:T(8,128)(2,1)}, bf16[128,576]{0,1:T(8,128)(2,1)S(1)}, u32[]{:S(2)}, u32[]{:S(2)}) collective-permute-start(bf16[128,576]{0,1:T(8,128)(2,1)} %param.12), channel_id=1, source_target_pairs={{0,64},{8,72},{2,66},{10,74},{4,68},{12,76},{6,70},{14,78},{16,80}... | collective-permute-start | bytes 442376 | tf_op jit(solution)/shard_map/ppermute | solution.py:36
  16.0 6.2 %all-to-all-start = ((f32[8,17,512]{2,1,0:T(8,128)}), f32[8,17,512]{2,1,0:T(8,128)S(1)}, u32[]{:S(2)}, u32[]{:S(2)}) async-start(f32[8,17,512]{2,1,0:T(8,128)} %pad_maximum_fusion.1), calls=%async_computation | async-start | bytes 786432 | tf_op jit(solution)/shard_map/all_to_all | solution.py:256
  30.4 5.9 %fusion = (f32[1024]{0:T(1024)S(1)}, f32[1024,2048]{1,0:T(8,128)S(1)}) fusion(s32[2048]{0:T(1024)S(1)} %add_bitcast_fusion, s32[2048]{0:T(1024)S(1)} %convert_reduce_fusion.1, s32[1024]{0:T(1024)S(1)} %get-tuple-element.133, s32[1024]{0:T(1024)S(1)} %get-tuple-element.134, bf16[1024,576]{1,0:T(8,128)(2,1)S(1)} %bitcast.78, ...), kind=kOutput, calls=%fused_computation.4 | convolution fusion | flops 2428500992 | bytes 11956224 | tf_op jit(solution)/shard_map/dot_general | solution.py:210
  36.3 3.2 %fusion.1 = f32[1024]{0:T(1024)S(1)} fusion(f32[1024,2048]{1,0:T(8,128)S(1)} %get-tuple-element.132, f32[1024]{0:T(1024)S(1)} %get-tuple-element.131, s32[2048]{0:T(1024)S(1)} %add_bitcast_fusion, s32[2048]{0:T(1024)S(1)} %convert_reduce_fusion.1, s32[1024]{0:T(1024)S(1)} %get-tuple-element.133, s32[1024]{0:T(1024)S(1)} %get-tuple-element.134), kind=kLoop, calls=%fused_computation.6 | loop fusion | flops 16776192 | bytes 8421376 | tf_op jit(solution)/shard_map/reduce_sum | solution.py:214
  39.6 5.1 %divide_convert_fusion = bf16[1024,512]{1,0:T(8,128)(2,1)S(1)} fusion(f32[1024]{0:T(1024)S(1)} %fusion.1, bf16[2048,576]{0,1:T(8,128)(2,1)} %constant_dynamic-update-slice_fusion.7, f32[1024,2048]{1,0:T(8,128)S(1)} %get-tuple-element.132, f32[1024]{0:T(1024)S(1)} %get-tuple-element.131, s32[2048]{0:T(1024)S(1)} %add_bitcast_fusion, ...), kind=kOutput, calls=%fused_computation.21 | convolution fusion | flops 2165309440 | bytes 11567104 | tf_op jit(solution)/shard_map/dot_general | solution.py:215
  47.5 6.4 %all-to-all-start.1 = ((bf16[8,16,4096]{2,1,0:T(8,128)(2,1)}), bf16[8,16,4096]{2,1,0:T(8,128)(2,1)S(1)}, u32[]{:S(2)}, u32[]{:S(2)}) async-start(bf16[8,16,4096]{2,1,0:T(8,128)(2,1)} %bitcast.29), calls=%async_computation.1 | async-start | bytes 2097152 | tf_op jit(solution)/shard_map/all_to_all | solution.py:289
  54.0 7.8 %copy.57 = bf16[2,4096,2,256]{3,1,2,0:T(8,128)(2,1)} copy(bf16[2,4096,2,256]{3,2,1,0:T(2,128)(2,1)} %param.19) | data formatting | bytes 16777216 | tf_op args[7]
  62.3 7.7 %all-to-all-done.1 = bf16[8,16,4096]{2,1,0:T(8,128)(2,1)S(1)} async-done(((bf16[8,16,4096]{2,1,0:T(8,128)(2,1)}), bf16[8,16,4096]{2,1,0:T(8,128)(2,1)S(1)}, u32[]{:S(2)}, u32[]{:S(2)}) %all-to-all-start.1) | async-done | bytes 1048608 | tf_op jit(solution)/shard_map/all_to_all | solution.py:289
  89.5 2.6 collective-permute-start.13
  92.0 2.7 collective-permute-done.10.refs_3_
  111.9 11.3 %shard_map.120 = (bf16[128,4096]{1,0:T(8,128)(2,1)S(1)}, bf16[128,4096]{1,0:T(8,128)(2,1)S(1)}, bf16[128,4096]{1,0:T(8,128)(2,1)S(1)}, bf16[128,4096]{1,0:T(8,128)(2,1)S(1)}) custom-call(bf16[128,4224]{1,0:T(8,128)(2,1)S(1)} %copy-done.5, bf16[128,4224]{1,0:T(8,128)(2,1)} %collective-permute-done.19.refs_1_.refs_5_, ...), custom_call_target="tpu_custom_call" | custom-call | bytes 4096 | tf_op jit(solution)/shard_map/pallas_call | solution.py:151
  123.2 4.9 %collective-permute-done.14.refs_2_.refs_6_ = bf16[128,4224]{1,0:T(8,128)(2,1)S(1)} collective-permute-done((bf16[128,4224]{1,0:T(8,128)(2,1)}, bf16[128,4224]{1,0:T(8,128)(2,1)S(1)}, u32[]{:S(2)}, u32[]{:S(2)}) %collective-permute-start.14) | collective-permute-done | bytes 1081376 | tf_op jit(solution)/shard_map/ppermute | solution.py:36
  129.1 2.9 %collective-permute-done.17.refs_3_.refs_7_ = bf16[128,4224]{1,0:T(8,128)(2,1)S(1)} collective-permute-done((bf16[128,4224]{1,0:T(8,128)(2,1)}, bf16[128,4224]{1,0:T(8,128)(2,1)S(1)}, u32[]{:S(2)}, u32[]{:S(2)}) %collective-permute-start.17) | collective-permute-done | bytes 1081376 | tf_op jit(solution)/shard_map/ppermute | solution.py:36
  144.6 11.1 %shard_map.121 = (bf16[128,4096]{1,0:T(8,128)(2,1)S(1)}, bf16[128,4096]{1,0:T(8,128)(2,1)S(1)}, bf16[128,4096]{1,0:T(8,128)(2,1)S(1)}, bf16[128,4096]{1,0:T(8,128)(2,1)S(1)}) custom-call(bf16[128,4224]{1,0:T(8,128)(2,1)S(1)} %collective-permute-done.25.refs_0_.refs_4_, bf16[128,4224]{1,0:T(8,128)(2,1)S(1)} %collective-permute-done.26.refs_1_.refs_5_, ...), custom_call_target="tpu_custom_call" | custom-call | bytes 4096 | tf_op jit(solution)/shard_map/pallas_call | solution.py:151
  157.7 11.4 %shard_map.122 = (bf16[128,4096]{1,0:T(8,128)(2,1)S(1)}, bf16[128,4096]{1,0:T(8,128)(2,1)S(1)}, bf16[128,4096]{1,0:T(8,128)(2,1)S(1)}, bf16[128,4096]{1,0:T(8,128)(2,1)S(1)}) custom-call(bf16[128,4224]{1,0:T(8,128)(2,1)S(1)} %collective-permute-done.27.refs_0_.refs_4_, bf16[128,4224]{1,0:T(8,128)(2,1)S(1)} %collective-permute-done.28.refs_1_.refs_5_, ...), custom_call_target="tpu_custom_call" | custom-call | bytes 4096 | tf_op jit(solution)/shard_map/pallas_call | solution.py:151
  181.7 11.1 %shard_map.123 = (bf16[128,4096]{1,0:T(8,128)(2,1)S(1)}, bf16[128,4096]{1,0:T(8,128)(2,1)S(1)}, bf16[128,4096]{1,0:T(8,128)(2,1)S(1)}, bf16[128,4096]{1,0:T(8,128)(2,1)S(1)}) custom-call(bf16[64,4224]{1,0:T(8,128)(2,1)S(1)} %collective-permute-done.37.refs_0_.refs_8_, bf16[64,4224]{1,0:T(8,128)(2,1)S(1)} %collective-permute-done.38.refs_1_.refs_9_, ...), custom_call_target="tpu_custom_call" | custom-call | bytes 4096 | tf_op jit(solution)/shard_map/pallas_call | solution.py:151
  192.8 7.2 %collective-permute-done.30 = bf16[128,4096]{1,0:T(8,128)(2,1)S(1)} collective-permute-done((bf16[128,4096]{1,0:T(8,128)(2,1)S(1)}, bf16[128,4096]{1,0:T(8,128)(2,1)S(1)}, u32[]{:S(2)}, u32[]{:S(2)}) %collective-permute-start.30) | collective-permute-done | bytes 1048608 | tf_op jit(solution)/shard_map/ppermute | solution.py:36
  200.1 2.9 %collective-permute-done.32 = bf16[128,4096]{1,0:T(8,128)(2,1)S(1)} collective-permute-done((bf16[128,4096]{1,0:T(8,128)(2,1)S(1)}, bf16[128,4096]{1,0:T(8,128)(2,1)S(1)}, u32[]{:S(2)}, u32[]{:S(2)}) %collective-permute-start.32) | collective-permute-done | bytes 1048608 | tf_op jit(solution)/shard_map/ppermute | solution.py:36
  211.6 23.5 %collective-permute-done.49 = bf16[128,4096]{1,0:T(8,128)(2,1)S(1)} collective-permute-done((bf16[128,4096]{1,0:T(8,128)(2,1)S(1)}, bf16[128,4096]{1,0:T(8,128)(2,1)S(1)}, u32[]{:S(2)}, u32[]{:S(2)}) %collective-permute-start.49) | collective-permute-done | bytes 1048608 | tf_op jit(solution)/shard_map/ppermute | solution.py:36
  244.7 3.7 %collective-permute-done.52 = bf16[32,4096]{1,0:T(8,128)(2,1)S(1)} collective-permute-done((bf16[32,4096]{1,0:T(8,128)(2,1)S(1)}, bf16[32,4096]{1,0:T(8,128)(2,1)S(1)}, u32[]{:S(2)}, u32[]{:S(2)}) %collective-permute-start.52) | collective-permute-done | bytes 262176 | tf_op jit(solution)/shard_map/ppermute | solution.py:36
  248.7 3.6 %collective-permute-done.51 = bf16[32,4096]{1,0:T(8,128)(2,1)S(1)} collective-permute-done((bf16[32,4096]{1,0:T(8,128)(2,1)S(1)}, bf16[32,4096]{1,0:T(8,128)(2,1)S(1)}, u32[]{:S(2)}, u32[]{:S(2)}) %collective-permute-start.51) | collective-permute-done | bytes 262176 | tf_op jit(solution)/shard_map/ppermute | solution.py:36
  252.4 4.3 %collective-permute-start.54 = (bf16[16,4096]{1,0:T(8,128)(2,1)S(1)}, bf16[16,4096]{1,0:T(8,128)(2,1)S(1)}, u32[]{:S(2)}, u32[]{:S(2)}) collective-permute-start(bf16[16,4096]{1,0:T(8,128)(2,1)S(1)} %get-tuple-element.124), channel_id=1, source_target_pairs={{0,64},{8,72},{2,66},{10,74},{4,68},{12,76},{6,70},{14,78},{16,80}... | collective-permute-start | bytes 393224 | tf_op jit(solution)/shard_map/ppermute | solution.py:36
  257.5 2.6 collective-permute-start.46
  263.5 9.4 %all_to_all.29 = bf16[16,8,512]{2,0,1:T(8,128)(2,1)S(1)} all-to-all(bf16[16,8,512]{2,0,1:T(8,128)(2,1)S(1)} %bitcast.85), channel_id=1, replica_groups=mesh['ctx'=16,'exp'=8] {'exp'}, dimensions={1} | all-to-all | bytes 262144 | tf_op jit(solution)/shard_map/all_to_all | solution.py:334
  (204 shorter events, 112.3 us)
Async XLA Ops:
  8.1 14.9 %collective-permute-start.1 = (bf16[256,576]{0,1:T(8,128)(2,1)S(1)}, bf16[256,576]{0,1:T(8,128)(2,1)S(1)}, u32[]{:S(2)}, u32[]{:S(2)}) collective-permute-start(bf16[256,576]{0,1:T(8,128)(2,1)S(1)} %get-tuple-element.127), channel_id=1, source_target_pairs={{0,16},{8,24},{2,18},{10,26},{4,20},{12,28},{6,22},{14,30},{16,32}... | collective-permute-start | bytes 884744 | tf_op jit(solution)/shard_map/ppermute | solution.py:36
  9.9 14.1 %collective-permute-start.2 = (bf16[256,576]{0,1:T(8,128)(2,1)S(1)}, bf16[256,576]{0,1:T(8,128)(2,1)S(1)}, u32[]{:S(2)}, u32[]{:S(2)}) collective-permute-start(bf16[256,576]{0,1:T(8,128)(2,1)S(1)} %get-tuple-element.127), channel_id=1, source_target_pairs={{0,48},{8,56},{2,50},{10,58},{4,52},{12,60},{6,54},{14,62},{16,0},... | collective-permute-start | bytes 884744 | tf_op jit(solution)/shard_map/ppermute | solution.py:36
  12.2 12.7 %collective-permute-start.3 = (bf16[256,576]{0,1:T(8,128)(2,1)S(1)}, bf16[256,576]{0,1:T(8,128)(2,1)S(1)}, u32[]{:S(2)}, u32[]{:S(2)}) collective-permute-start(bf16[256,576]{0,1:T(8,128)(2,1)S(1)} %get-tuple-element.127), channel_id=1, source_target_pairs={{0,32},{8,40},{2,34},{10,42},{4,36},{12,44},{6,38},{14,46},{16,48}... | collective-permute-start | bytes 884744 | tf_op jit(solution)/shard_map/ppermute | solution.py:36
  16.0 31.5 %all-to-all-start = ((f32[8,17,512]{2,1,0:T(8,128)}), f32[8,17,512]{2,1,0:T(8,128)S(1)}, u32[]{:S(2)}, u32[]{:S(2)}) async-start(f32[8,17,512]{2,1,0:T(8,128)} %pad_maximum_fusion.1), calls=%async_computation | async-start | bytes 786432 | tf_op jit(solution)/shard_map/all_to_all | solution.py:256
  47.5 22.5 %all-to-all-start.1 = ((bf16[8,16,4096]{2,1,0:T(8,128)(2,1)}), bf16[8,16,4096]{2,1,0:T(8,128)(2,1)S(1)}, u32[]{:S(2)}, u32[]{:S(2)}) async-start(bf16[8,16,4096]{2,1,0:T(8,128)(2,1)} %bitcast.29), calls=%async_computation.1 | async-start | bytes 2097152 | tf_op jit(solution)/shard_map/all_to_all | solution.py:289
  100.9 27.2 %collective-permute-start.14 = (bf16[128,4224]{1,0:T(8,128)(2,1)}, bf16[128,4224]{1,0:T(8,128)(2,1)S(1)}, u32[]{:S(2)}, u32[]{:S(2)}) collective-permute-start(bf16[128,4224]{1,0:T(8,128)(2,1)} %get-tuple-element.58.refs_2_.refs_6_), channel_id=1, source_target_pairs={{0,16},{8,24},{2,18},{10,26},{4,20},{12,28},{6,22},{14,30},{16,32}... | collective-permute-start | bytes 3244040 | tf_op jit(solution)/shard_map/ppermute | solution.py:36
  102.1 27.0 %collective-permute-start.15 = (bf16[128,4224]{1,0:T(8,128)(2,1)}, bf16[128,4224]{1,0:T(8,128)(2,1)}, u32[]{:S(2)}, u32[]{:S(2)}) collective-permute-start(bf16[128,4224]{1,0:T(8,128)(2,1)} %get-tuple-element.59.refs_3_.refs_7_), channel_id=1, source_target_pairs={{0,2},{8,10},{2,4},{10,12},{4,6},{12,14},{6,0},{14,8},{16,18},{24,... | collective-permute-start | bytes 3244040 | tf_op jit(solution)/shard_map/ppermute | solution.py:36
  103.2 25.9 %collective-permute-start.16 = (bf16[128,4224]{1,0:T(8,128)(2,1)}, bf16[128,4224]{1,0:T(8,128)(2,1)S(1)}, u32[]{:S(2)}, u32[]{:S(2)}) collective-permute-start(bf16[128,4224]{1,0:T(8,128)(2,1)} %get-tuple-element.58.refs_2_.refs_6_), channel_id=1, source_target_pairs={{0,48},{8,56},{2,50},{10,58},{4,52},{12,60},{6,54},{14,62},{16,0},... | collective-permute-start | bytes 3244040 | tf_op jit(solution)/shard_map/ppermute | solution.py:36
  106.2 25.7 %collective-permute-start.17 = (bf16[128,4224]{1,0:T(8,128)(2,1)}, bf16[128,4224]{1,0:T(8,128)(2,1)S(1)}, u32[]{:S(2)}, u32[]{:S(2)}) collective-permute-start(bf16[128,4224]{1,0:T(8,128)(2,1)} %get-tuple-element.59.refs_3_.refs_7_), channel_id=1, source_target_pairs={{0,6},{8,14},{2,0},{10,8},{4,2},{12,10},{6,4},{14,12},{16,22},{24,... | collective-permute-start | bytes 3244040 | tf_op jit(solution)/shard_map/ppermute | solution.py:36
  132.5 25.2 %collective-permute-start.28 = (bf16[128,4224]{1,0:T(8,128)(2,1)S(1)}, bf16[128,4224]{1,0:T(8,128)(2,1)S(1)}, u32[]{:S(2)}, u32[]{:S(2)}) collective-permute-start(bf16[128,4224]{1,0:T(8,128)(2,1)S(1)} %collective-permute-done.17.refs_3_.refs_7_), channel_id=1, source_target_pairs={{0,8},{8,0},{2,10},{10,2},{4,12},{12,4},{6,14},{14,6},{16,24},{24,... | collective-permute-start | bytes 3244040 | tf_op jit(solution)/shard_map/ppermute | solution.py:36
  137.5 31.6 %collective-permute-start.21 = (bf16[64,4224]{1,0:T(8,128)(2,1)}, bf16[64,4224]{1,0:T(8,128)(2,1)S(1)}, u32[]{:S(2)}, u32[]{:S(2)}) collective-permute-start(bf16[64,4224]{1,0:T(8,128)(2,1)} %slice.73), channel_id=1, source_target_pairs={{0,16},{8,24},{2,18},{10,26},{4,20},{12,28},{6,22},{14,30},{16,32}... | collective-permute-start | bytes 1622024 | tf_op jit(solution)/shard_map/ppermute | solution.py:36
  139.0 30.1 %collective-permute-start.22 = (bf16[64,4224]{1,0:T(8,128)(2,1)}, bf16[64,4224]{1,0:T(8,128)(2,1)S(1)}, u32[]{:S(2)}, u32[]{:S(2)}) collective-permute-start(bf16[64,4224]{1,0:T(8,128)(2,1)} %slice.74), channel_id=1, source_target_pairs={{0,48},{8,56},{2,50},{10,58},{4,52},{12,60},{6,54},{14,62},{16,0},... | collective-permute-start | bytes 1622024 | tf_op jit(solution)/shard_map/ppermute | solution.py:36
  141.1 28.0 %collective-permute-start.23 = (bf16[64,4224]{1,0:T(8,128)(2,1)}, bf16[64,4224]{1,0:T(8,128)(2,1)S(1)}, u32[]{:S(2)}, u32[]{:S(2)}) collective-permute-start(bf16[64,4224]{1,0:T(8,128)(2,1)} %slice.75), channel_id=1, source_target_pairs={{0,2},{8,10},{2,4},{10,12},{4,6},{12,14},{6,0},{14,8},{16,18},{24,... | collective-permute-start | bytes 1622024 | tf_op jit(solution)/shard_map/ppermute | solution.py:36
  142.1 27.0 %collective-permute-start.24 = (bf16[64,4224]{1,0:T(8,128)(2,1)}, bf16[64,4224]{1,0:T(8,128)(2,1)S(1)}, u32[]{:S(2)}, u32[]{:S(2)}) collective-permute-start(bf16[64,4224]{1,0:T(8,128)(2,1)} %slice.76), channel_id=1, source_target_pairs={{0,6},{8,14},{2,0},{10,8},{4,2},{12,10},{6,4},{14,12},{16,22},{24,... | collective-permute-start | bytes 1622024 | tf_op jit(solution)/shard_map/ppermute | solution.py:36
  174.9 25.2 %collective-permute-start.30 = (bf16[128,4096]{1,0:T(8,128)(2,1)S(1)}, bf16[128,4096]{1,0:T(8,128)(2,1)S(1)}, u32[]{:S(2)}, u32[]{:S(2)}) collective-permute-start(bf16[128,4096]{1,0:T(8,128)(2,1)S(1)} %add_convert_fusion.8), channel_id=1, source_target_pairs={{0,48},{8,56},{2,50},{10,58},{4,52},{12,60},{6,54},{14,62},{16,0},... | collective-permute-start | bytes 3145736 | tf_op jit(solution)/shard_map/ppermute | solution.py:36
  176.4 26.6 %collective-permute-start.32 = (bf16[128,4096]{1,0:T(8,128)(2,1)S(1)}, bf16[128,4096]{1,0:T(8,128)(2,1)S(1)}, u32[]{:S(2)}, u32[]{:S(2)}) collective-permute-start(bf16[128,4096]{1,0:T(8,128)(2,1)S(1)} %add_convert_fusion.7), channel_id=1, source_target_pairs={{0,16},{8,24},{2,18},{10,26},{4,20},{12,28},{6,22},{14,30},{16,32}... | collective-permute-start | bytes 3145736 | tf_op jit(solution)/shard_map/ppermute | solution.py:36
  177.7 25.3 %collective-permute-start.34 = (bf16[128,4096]{1,0:T(8,128)(2,1)S(1)}, bf16[128,4096]{1,0:T(8,128)(2,1)}, u32[]{:S(2)}, u32[]{:S(2)}) collective-permute-start(bf16[128,4096]{1,0:T(8,128)(2,1)S(1)} %add_convert_fusion.6), channel_id=1, source_target_pairs={{0,6},{8,14},{2,0},{10,8},{4,2},{12,10},{6,4},{14,12},{16,22},{24,... | collective-permute-start | bytes 3145736 | tf_op jit(solution)/shard_map/ppermute | solution.py:36
  179.7 25.7 %collective-permute-start.36 = (bf16[128,4096]{1,0:T(8,128)(2,1)S(1)}, bf16[128,4096]{1,0:T(8,128)(2,1)}, u32[]{:S(2)}, u32[]{:S(2)}) collective-permute-start(bf16[128,4096]{1,0:T(8,128)(2,1)S(1)} %add_convert_fusion.5), channel_id=1, source_target_pairs={{0,2},{8,10},{2,4},{10,12},{4,6},{12,14},{6,0},{14,8},{16,18},{24,... | collective-permute-start | bytes 3145736 | tf_op jit(solution)/shard_map/ppermute | solution.py:36
  208.3 26.8 %collective-permute-start.49 = (bf16[128,4096]{1,0:T(8,128)(2,1)S(1)}, bf16[128,4096]{1,0:T(8,128)(2,1)S(1)}, u32[]{:S(2)}, u32[]{:S(2)}) collective-permute-start(bf16[128,4096]{1,0:T(8,128)(2,1)S(1)} %add_convert_fusion.1), channel_id=1, source_target_pairs={{0,4},{8,12},{2,6},{10,14},{4,0},{12,8},{6,2},{14,10},{16,20},{24,... | collective-permute-start | bytes 3145736 | tf_op jit(solution)/shard_map/ppermute | solution.py:36
  208.4 34.2 %collective-permute-start.20 = (bf16[128,4096]{1,0:T(8,128)(2,1)S(1)}, bf16[128,4096]{1,0:T(8,128)(2,1)S(1)}, u32[]{:S(2)}, u32[]{:S(2)}) collective-permute-start(bf16[128,4096]{1,0:T(8,128)(2,1)S(1)} %copy-done.7), channel_id=1, source_target_pairs={{0,8},{8,0},{2,10},{10,2},{4,12},{12,4},{6,14},{14,6},{16,24},{24,... | collective-permute-start | bytes 3145736 | tf_op jit(solution)/shard_map/ppermute | solution.py:36
  209.8 32.8 %collective-permute-start.42 = (bf16[128,4096]{1,0:T(8,128)(2,1)S(1)}, bf16[128,4096]{1,0:T(8,128)(2,1)S(1)}, u32[]{:S(2)}, u32[]{:S(2)}) collective-permute-start(bf16[128,4096]{1,0:T(8,128)(2,1)S(1)} %add_convert_fusion.4), channel_id=1, source_target_pairs={{0,32},{8,40},{2,34},{10,42},{4,36},{12,44},{6,38},{14,46},{16,48}... | collective-permute-start | bytes 3145736 | tf_op jit(solution)/shard_map/ppermute | solution.py:36
  239.3 12.9 %collective-permute-start.51 = (bf16[32,4096]{1,0:T(8,128)(2,1)S(1)}, bf16[32,4096]{1,0:T(8,128)(2,1)S(1)}, u32[]{:S(2)}, u32[]{:S(2)}) collective-permute-start(bf16[32,4096]{1,0:T(8,128)(2,1)S(1)} %get-tuple-element.114), channel_id=1, source_target_pairs={{0,16},{8,24},{2,18},{10,26},{4,20},{12,28},{6,22},{14,30},{16,32}... | collective-permute-start | bytes 786440 | tf_op jit(solution)/shard_map/ppermute | solution.py:36
  243.5 13.2 %collective-permute-start.45 = (bf16[32,4096]{1,0:T(8,128)(2,1)S(1)}, bf16[32,4096]{1,0:T(8,128)(2,1)S(1)}, u32[]{:S(2)}, u32[]{:S(2)}) collective-permute-start(bf16[32,4096]{1,0:T(8,128)(2,1)S(1)} %get-tuple-element.110), channel_id=1, source_target_pairs={{0,4},{8,12},{2,6},{10,14},{4,0},{12,8},{6,2},{14,10},{16,20},{24,... | collective-permute-start | bytes 786440 | tf_op jit(solution)/shard_map/ppermute | solution.py:36
  243.8 13.5 %collective-permute-start.44 = (bf16[32,4096]{1,0:T(8,128)(2,1)S(1)}, bf16[32,4096]{1,0:T(8,128)(2,1)S(1)}, u32[]{:S(2)}, u32[]{:S(2)}) collective-permute-start(bf16[32,4096]{1,0:T(8,128)(2,1)S(1)} %get-tuple-element.111), channel_id=1, source_target_pairs={{0,2},{8,10},{2,4},{10,12},{4,6},{12,14},{6,0},{14,8},{16,18},{24,... | collective-permute-start | bytes 786440 | tf_op jit(solution)/shard_map/ppermute | solution.py:36
  (54 other events, 481.6 us)

commit v4 on v3

--- a/solution.py
+++ b/solution.py
@@ -18,6 +18,7 @@
 EXPERTS = 32
 GATE_COLS = 128
 BOTH = ("ctx", "exp")
+NOWHERE = 64
 
 epsilon = 1e-06
 
@@ -80,10 +81,11 @@
     blocks = [block for group in groups for block in group]
     width = blocks[0].shape[1]
     heights = [sum(block.shape[0] for block in group) for group in groups]
-    tile = width // 3
+    cuts = 3 if width % 384 == 0 else 1
+    tile = width // cuts
     return pl.pallas_call(
         functools.partial(stack_kernel, sizes),
-        grid=(3,),
+        grid=(cuts,),
         in_specs=[pl.BlockSpec((block.shape[0], tile), lambda i: (0, i)) for block in blocks],
         out_specs=[pl.BlockSpec((height, tile), lambda i: (0, i)) for height in heights],
         out_shape=[jax.ShapeDtypeStruct((height, width), jnp.bfloat16) for height in heights],
@@ -183,15 +185,26 @@
     doc_ends = jnp.cumsum(doc_lengths)
     ctx = lax.axis_index("ctx")
     x_hi, y, core = ctx // 8, (ctx // 2) % 4, ctx % 2
-    pair = jnp.concatenate([latent, shift(latent, "x", 2)], axis=0)
-    half = jnp.concatenate(ring(pair, "y"), axis=0)
-    piece = jnp.concatenate([half, other_core(half)], axis=0)
-    starts = [
-        (((x_hi + dx) % 2 * 4 + (y + dy) % 4) * 2 + (core + dc) % 2) * tokens
-        for dc in (0, 1)
-        for dy in (0, 3, 1, 2)
-        for dx in (0, 1)
-    ]
+    other = lax.ppermute(latent, BOTH, [(a, b) for a, b in table(dx=2) if a < b])
+    blocks, places = [latent, other], [ctx, jnp.where(x_hi > 0, ctx - 8, NOWHERE)]
+    for by in (1, -1, 2):
+        to, come = (y + by) % 4, (y - by) % 4
+        blocks.append(shift(jnp.where(to > y, latent, other), "y", by))
+        place = x_hi * 8 + come * 2 + core
+        places.append(
+            jnp.where(come < y, place, jnp.where(x_hi > 0, place - 8, NOWHERE))
+        )
+    last = lax.ppermute(
+        other,
+        BOTH,
+        [(a, b) for a, b in table(dy=1, dc=1) if a >= 64 and a // 8 % 2 and a // 16 % 4 < 3],
+    )
+    (half,) = stack(blocks)
+    piece = jnp.concatenate([half, other_core(half), last], axis=0)
+    starts = [place * tokens for place in places]
+    starts += [(place + 1 - 2 * core) * tokens for place in places]
+    seen = (x_hi > 0) & (core == 0) & (y > 0)
+    starts.append(jnp.where(seen, ctx - 9, NOWHERE) * tokens)
     steps = jnp.arange(tokens, dtype=jnp.int32)
     key_pos = (jnp.stack(starts)[:, None] + steps[None, :]).reshape(-1)
     key_doc = document(key_pos, doc_ends)
@@ -305,26 +318,36 @@
         after.append([shift(block, axis, -1)])
     at_own = own_and_theirs([[first], [second]])
     before, after, at_own = lax.optimization_barrier((before, after, at_own))
-    far = [
-        [shift(before[i][0][:near], axis, 1), shift(after[i][0][near:], axis, -1)]
+    far = []
+    for i, axis in enumerate("yz"):
+        far.append([shift(before[i][0][:near], axis, 1)])
+        far.append([shift(after[i][0][near:], axis, -1)])
+    at_before = own_and_theirs(before)
+    far, at_before = lax.optimization_barrier((far, at_before))
+    at_far = own_and_theirs(far)
+    after, at_far = lax.optimization_barrier((after, at_far))
+    sum_far = both_cores(at_far)
+    passing = [
+        (shift(sum_far[2 * i], axis, 1), shift(sum_far[2 * i + 1], axis, -1))
         for i, axis in enumerate("yz")
     ]
-    at_before = own_and_theirs(before)
-    at_after = own_and_theirs(after)
-    far, at_before, at_after = lax.optimization_barrier((far, at_before, at_after))
-    sum_own = both_cores(at_own)
-    sum_before = both_cores(at_before)
-    sum_after = both_cores(at_after)
-    sent = [
-        (shift(sum_before[i], axis, -1), shift(sum_after[i], axis, 1))
-        for i, axis in enumerate("yz")
+    passing, at_after = lax.optimization_barrier((passing, own_and_theirs(after)))
+    back_own, back_before, back_after = [
+        [other_core(there) for there in at[:2]] for at in (at_own, at_before, at_after)
     ]
-    sent, at_far = lax.optimization_barrier((sent, own_and_theirs(far)))
-    sum_far = both_cores(at_far)
-    first, second = [
-        add_up(sum_own[i], *sent[i], shift(sum_far[i], axis, 2)).astype(jnp.bfloat16)
-        for i, axis in enumerate("yz")
-    ]
+    totals = []
+    for i, axis in enumerate("yz"):
+        for_after, for_before = passing[i]
+        low = jnp.pad(for_before, ((near, 0), (0, 0)))
+        high = jnp.pad(for_after, ((0, near), (0, 0)))
+        sum_before = add_up(at_before[2 + i], back_before[i], low).astype(jnp.bfloat16)
+        sum_after = add_up(at_after[2 + i], back_after[i], high).astype(jnp.bfloat16)
+        totals.append(
+            add_up(
+                at_own[2 + i], back_own[i], shift(sum_before, axis, -1), shift(sum_after, axis, 1)
+            ).astype(jnp.bfloat16)
+        )
+    first, second = totals
     pair = 2 * own
     first = ring_sum(*[first[i * pair : (i + 1) * pair] for i in range(4)], "z")
     second = ring_sum(*[second[i * pair : (i + 1) * pair] for i in range(4)], "y")

time: 277 us -> 276 us (level)
  local copies, waits for them, and re-layouts: 27.5 us -> 23.5 us
  matrix products: 14.3 us -> 11 us
    ppermute x0 -> x2, starting transfers between devices: none -> 6.16 us  [the longest x1 5.02 us: attention(): lax.ppermute(latent, BOTH, [(a, b) for a, b in table(dx=2) if a < b])]
    ppermute x55 -> x58, starting transfers between devices: 59.7 us -> 54.8 us  [shift(): return lax.ppermute(value, BOTH, table(**{'d' + axis: by}))]
    unnamed x50 -> x43, local copies, waits for them, and re-layouts: 19.7 us -> 16.2 us
    slice x4, local copies, waits for them, and re-layouts: 4.43 us -> 1.47 us  [the longest x2 1.39 us: body(): far.append([shift(before[i][0][:near], axis, 1)])]
    dot_general x1, matrix products: 5.12 us -> 2.26 us  [attention(): jnp.dot(weights.astype(jnp.bfloat16), piece[:, :LAT], preferred_element_t...]
    ppermute x55 -> x58, waiting for transfers between devices: 83.5 us -> 85.2 us  [shift(): return lax.ppermute(value, BOTH, table(**{'d' + axis: by}))]
  transfers between devices with their start and end apart: 57 -> 62, of which waited for: 30 -> 33; matrix products, arithmetic and copies ran while one was open for 16% -> 14% of each run, Pallas kernels for 16% -> 12%
where the time goes in v4:
time: 276 us; the launch traced here: 272 us
  waiting for transfers between devices  92.5 us (34%)
  starting transfers between devices  71.8 us (26%)
  Pallas kernels  47.5 us (17%)
  local copies, waits for them, and re-layouts  23.5 us (9%)
  other arithmetic  13.5 us (5%)
  blocking collectives  11.3 us (4%)
  matrix products  11 us (4%)
    ppermute x58, waiting for transfers between devices, shift(): return lax.ppermute(value, BOTH, table(**{'d' + axis: by}))  85.2 us
    ppermute x58, starting transfers between devices, shift(): return lax.ppermute(value, BOTH, table(**{'d' + axis: by}))  54.8 us
    pallas_call x4, Pallas kernels, run_experts(): pl.pallas_call(functools.partial(experts_kernel, sizes), grid=(2 * STEPS,...  45.2 us
    unnamed x43, local copies, waits for them, and re-layouts  16.2 us
    all_to_all x1, blocking collectives, body(): return lax.all_to_all(mixed, 'exp', split_axis=1, concat_axis=0, tiled=True)  11.3 us
    all_to_all x1, waiting for transfers between devices, body(): lax.all_to_all(partial.reshape(count_exp, own, D), 'exp', split_axis=0, c...  7.27 us
    all_to_all x1, starting transfers between devices, body(): lax.all_to_all(partial.reshape(count_exp, own, D), 'exp', split_axis=0, c...  5.56 us
  transfers between devices with their start and end apart: 62, of which 33 were waited for; matrix products, arithmetic and copies ran while one was open for 14% of the time, Pallas kernels for 12%

profile of v4, /device:TPU:0, one launch (start us, length us, event | category | flops | bytes accessed | tf_op | source)
XLA Modules:
  0.0 272.4 jit_solution(11456768315482819001)
XLA Ops:
  1.2 5.0 %collective-permute-start = (bf16[128,576]{1,0:T(8,128)(2,1)S(1)}, bf16[128,576]{1,0:T(8,128)(2,1)S(1)}, u32[]{:S(2)}, u32[]{:S(2)}) collective-permute-start(bf16[128,576]{1,0:T(8,128)(2,1)S(1)} %copy.63.refs_0_), channel_id=1, source_target_pairs={{0,64},{8,72},{2,66},{10,74},{4,68},{12,76},{6,70},{14,78},{16,80}... | collective-permute-start | bytes 442376 | tf_op jit(solution)/shard_map/ppermute | solution.py:188
  8.6 5.3 %all-to-all-start = ((f32[8,17,512]{2,1,0:T(8,128)}), f32[8,17,512]{2,1,0:T(8,128)}, u32[]{:S(2)}, u32[]{:S(2)}) async-start(f32[8,17,512]{2,1,0:T(8,128)} %pad_maximum_fusion.1), calls=%async_computation | async-start | bytes 786432 | tf_op jit(solution)/shard_map/all_to_all | solution.py:269
  15.5 3.3 %collective-permute-start.3 = (bf16[128,576]{1,0:T(8,128)(2,1)S(1)}, bf16[128,576]{1,0:T(8,128)(2,1)S(1)}, u32[]{:S(2)}, u32[]{:S(2)}) collective-permute-start(bf16[128,576]{1,0:T(8,128)(2,1)S(1)} %get-tuple-element.137), channel_id=1, source_target_pairs={{0,32},{8,40},{2,34},{10,42},{4,36},{12,44},{6,38},{14,46},{16,48}... | collective-permute-start | bytes 442376 | tf_op jit(solution)/shard_map/ppermute | solution.py:37
  34.5 4.6 %fusion = (f32[1024]{0:T(1024)S(1)}, f32[1024,1408]{1,0:T(8,128)S(1)}) fusion(s32[1408]{0:T(1024)S(1)} %add_bitcast_fusion, s32[1408]{0:T(1024)S(1)} %convert_reduce_fusion.1, s32[1024]{0:T(1024)S(1)} %get-tuple-element.144, s32[1024]{0:T(1024)S(1)} %get-tuple-element.145, bf16[1024,576]{1,0:T(8,128)(2,1)} %bitcast.72, ...), kind=kOutput, calls=%fused_computation.4 | convolution fusion | flops 1674460160 | bytes 8592384 | tf_op jit(solution)/shard_map/dot_general | solution.py:223
  46.6 5.6 %all-to-all-start.1 = ((bf16[8,16,4096]{2,1,0:T(8,128)(2,1)}), bf16[8,16,4096]{2,1,0:T(8,128)(2,1)S(1)}, u32[]{:S(2)}, u32[]{:S(2)}) async-start(bf16[8,16,4096]{2,1,0:T(8,128)(2,1)} %bitcast.24), calls=%async_computation.1 | async-start | bytes 2097152 | tf_op jit(solution)/shard_map/all_to_all | solution.py:302
  52.5 7.8 %copy.81 = bf16[2,4096,2,256]{3,1,2,0:T(8,128)(2,1)} copy(bf16[2,4096,2,256]{3,2,1,0:T(2,128)(2,1)} %param.19) | data formatting | bytes 16777216 | tf_op args[7]
  61.3 7.3 %all-to-all-done.1 = bf16[8,16,4096]{2,1,0:T(8,128)(2,1)S(1)} async-done(((bf16[8,16,4096]{2,1,0:T(8,128)(2,1)}), bf16[8,16,4096]{2,1,0:T(8,128)(2,1)S(1)}, u32[]{:S(2)}, u32[]{:S(2)}) %all-to-all-start.1) | async-done | bytes 1048608 | tf_op jit(solution)/shard_map/all_to_all | solution.py:302
  70.1 3.5 %collective-permute-start.7 = (bf16[16,4224]{1,0:T(8,128)(2,1)S(1)}, bf16[16,4224]{1,0:T(8,128)(2,1)S(1)}, u32[]{:S(2)}, u32[]{:S(2)}) collective-permute-start(bf16[16,4224]{1,0:T(8,128)(2,1)S(1)} %concatenate.15.refs_0_), channel_id=1, source_target_pairs={{0,65},{8,73},{2,67},{10,75},{4,69},{12,77},{6,71},{14,79},{16,81}... | collective-permute-start | bytes 405512 | tf_op jit(solution)/shard_map/ppermute | solution.py:37
  73.6 4.5 %collective-permute-done.8.refs_3_ = bf16[16,4224]{1,0:T(8,128)(2,1)S(1)} collective-permute-done((bf16[16,4224]{1,0:T(8,128)(2,1)S(1)}, bf16[16,4224]{1,0:T(8,128)(2,1)S(1)}, u32[]{:S(2)}, u32[]{:S(2)}) %collective-permute-start.8) | collective-permute-done | bytes 135200 | tf_op jit(solution)/shard_map/ppermute | solution.py:37
  87.1 4.4 %collective-permute-done.11.refs_3_ = bf16[32,4224]{1,0:T(8,128)(2,1)S(1)} collective-permute-done((bf16[32,4224]{1,0:T(8,128)(2,1)S(1)}, bf16[32,4224]{1,0:T(8,128)(2,1)S(1)}, u32[]{:S(2)}, u32[]{:S(2)}) %collective-permute-start.11) | collective-permute-done | bytes 270368 | tf_op jit(solution)/shard_map/ppermute | solution.py:37
  110.4 11.3 %shard_map.121 = (bf16[128,4096]{1,0:T(8,128)(2,1)S(1)}, bf16[128,4096]{1,0:T(8,128)(2,1)S(1)}, bf16[128,4096]{1,0:T(8,128)(2,1)S(1)}, bf16[128,4096]{1,0:T(8,128)(2,1)S(1)}) custom-call(bf16[128,4224]{1,0:T(8,128)(2,1)S(1)} %copy-done.5, bf16[128,4224]{1,0:T(8,128)(2,1)} %collective-permute-done.20.refs_1_.refs_5_, ...), custom_call_target="tpu_custom_call" | custom-call | bytes 4096 | tf_op jit(solution)/shard_map/pallas_call | solution.py:153
  121.8 5.9 %collective-permute-done.17.refs_2_.refs_6_ = bf16[128,4224]{1,0:T(8,128)(2,1)S(1)} collective-permute-done((bf16[128,4224]{1,0:T(8,128)(2,1)}, bf16[128,4224]{1,0:T(8,128)(2,1)S(1)}, u32[]{:S(2)}, u32[]{:S(2)}) %collective-permute-start.17) | collective-permute-done | bytes 1081376 | tf_op jit(solution)/shard_map/ppermute | solution.py:37
  129.6 4.5 %collective-permute-done.16.refs_3_.refs_7_ = bf16[128,4224]{1,0:T(8,128)(2,1)} collective-permute-done((bf16[128,4224]{1,0:T(8,128)(2,1)}, bf16[128,4224]{1,0:T(8,128)(2,1)}, u32[]{:S(2)}, u32[]{:S(2)}) %collective-permute-start.16) | collective-permute-done | bytes 1081376 | tf_op jit(solution)/shard_map/ppermute | solution.py:37
  139.4 3.4 %collective-permute-start.23 = (bf16[64,4224]{1,0:T(8,128)(2,1)S(1)}, bf16[64,4224]{1,0:T(8,128)(2,1)S(1)}, u32[]{:S(2)}, u32[]{:S(2)}) collective-permute-start(bf16[64,4224]{1,0:T(8,128)(2,1)S(1)} %slice.74), channel_id=1, source_target_pairs={{0,48},{8,56},{2,50},{10,58},{4,52},{12,60},{6,54},{14,62},{16,0},... | collective-permute-start | bytes 1622024 | tf_op jit(solution)/shard_map/ppermute | solution.py:37
  142.8 11.7 %shard_map.122 = (bf16[128,4096]{1,0:T(8,128)(2,1)}, bf16[128,4096]{1,0:T(8,128)(2,1)S(1)}, bf16[128,4096]{1,0:T(8,128)(2,1)S(1)}, bf16[128,4096]{1,0:T(8,128)(2,1)S(1)}) custom-call(bf16[128,4224]{1,0:T(8,128)(2,1)S(1)} %collective-permute-done.26.refs_0_.refs_4_, bf16[128,4224]{1,0:T(8,128)(2,1)S(1)} %collective-permute-done.27.refs_1_.refs_5_, ...), custom_call_target="tpu_custom_call" | custom-call | bytes 4096 | tf_op jit(solution)/shard_map/pallas_call | solution.py:153
  159.9 11.2 %shard_map.123 = (bf16[64,4096]{1,0:T(8,128)(2,1)S(1)}, bf16[64,4096]{1,0:T(8,128)(2,1)S(1)}, bf16[64,4096]{1,0:T(8,128)(2,1)S(1)}, bf16[64,4096]{1,0:T(8,128)(2...) custom-call(bf16[64,4224]{1,0:T(8,128)(2,1)S(1)} %collective-permute, ...), custom_call_target="tpu_custom_call" | custom-call | bytes 4096 | tf_op jit(solution)/shard_map/pallas_call | solution.py:153
  184.8 11.0 %shard_map.124 = (bf16[128,4096]{1,0:T(8,128)(2,1)S(1)}, bf16[128,4096]{1,0:T(8,128)(2,1)S(1)}, bf16[128,4096]{1,0:T(8,128)(2,1)S(1)}, bf16[128,4096]{1,0:T(8,128)(2,1)S(1)}) custom-call(bf16[128,4224]{1,0:T(8,128)(2,1)S(1)} %collective-permute-done.41.refs_0_.refs_4_, bf16[128,4224]{1,0:T(8,128)(2,1)S(1)} %collective-permute-done.42.refs_1_.refs_5_, ...), custom_call_target="tpu_custom_call" | custom-call | bytes 4096 | tf_op jit(solution)/shard_map/pallas_call | solution.py:153
  199.5 4.0 %collective-permute-done.51 = bf16[128,4096]{1,0:T(8,128)(2,1)S(1)} collective-permute-done((bf16[128,4096]{1,0:T(8,128)(2,1)S(1)}, bf16[128,4096]{1,0:T(8,128)(2,1)S(1)}, u32[]{:S(2)}, u32[]{:S(2)}) %collective-permute-start.51) | collective-permute-done | bytes 1048608 | tf_op jit(solution)/shard_map/ppermute | solution.py:37
  208.4 15.6 %collective-permute-done.43 = bf16[128,4096]{1,0:T(8,128)(2,1)S(1)} collective-permute-done((bf16[128,4096]{1,0:T(8,128)(2,1)S(1)}, bf16[128,4096]{1,0:T(8,128)(2,1)S(1)}, u32[]{:S(2)}, u32[]{:S(2)}) %collective-permute-start.43) | collective-permute-done | bytes 1048608 | tf_op jit(solution)/shard_map/ppermute | solution.py:37
  224.0 5.9 %collective-permute-done.45 = bf16[128,4096]{1,0:T(8,128)(2,1)S(1)} collective-permute-done((bf16[128,4096]{1,0:T(8,128)(2,1)S(1)}, bf16[128,4096]{1,0:T(8,128)(2,1)S(1)}, u32[]{:S(2)}, u32[]{:S(2)}) %collective-permute-start.45) | collective-permute-done | bytes 1048608 | tf_op jit(solution)/shard_map/ppermute | solution.py:37
  235.4 6.0 %collective-permute-start.55 = (bf16[32,4096]{1,0:T(8,128)(2,1)S(1)}, bf16[32,4096]{1,0:T(8,128)(2,1)S(1)}, u32[]{:S(2)}, u32[]{:S(2)}) collective-permute-start(bf16[32,4096]{1,0:T(8,128)(2,1)S(1)} %get-tuple-element.132), channel_id=1, source_target_pairs={{0,48},{8,56},{2,50},{10,58},{4,52},{12,60},{6,54},{14,62},{16,0},... | collective-permute-start | bytes 786440 | tf_op jit(solution)/shard_map/ppermute | solution.py:37
  244.4 3.3 %collective-permute-done.47 = bf16[32,4096]{1,0:T(8,128)(2,1)S(1)} collective-permute-done((bf16[32,4096]{1,0:T(8,128)(2,1)S(1)}, bf16[32,4096]{1,0:T(8,128)(2,1)S(1)}, u32[]{:S(2)}, u32[]{:S(2)}) %collective-permute-start.47) | collective-permute-done | bytes 262176 | tf_op jit(solution)/shard_map/ppermute | solution.py:37
  254.4 5.4 %collective-permute-done.58 = bf16[16,4096]{1,0:T(8,128)(2,1)S(1)} collective-permute-done((bf16[16,4096]{1,0:T(8,128)(2,1)S(1)}, bf16[16,4096]{1,0:T(8,128)(2,1)S(1)}, u32[]{:S(2)}, u32[]{:S(2)}) %collective-permute-start.58) | collective-permute-done | bytes 131104 | tf_op jit(solution)/shard_map/ppermute | solution.py:37
  260.0 11.3 %all_to_all.29 = bf16[16,8,512]{2,0,1:T(8,128)(2,1)S(1)} all-to-all(bf16[16,8,512]{2,0,1:T(8,128)(2,1)S(1)} %bitcast.77), channel_id=1, replica_groups=mesh['ctx'=16,'exp'=8] {'exp'}, dimensions={1} | all-to-all | bytes 262144 | tf_op jit(solution)/shard_map/all_to_all | solution.py:357
  (211 shorter events, 109.4 us)
Async XLA Ops:
  1.2 14.3 %collective-permute-start = (bf16[128,576]{1,0:T(8,128)(2,1)S(1)}, bf16[128,576]{1,0:T(8,128)(2,1)S(1)}, u32[]{:S(2)}, u32[]{:S(2)}) collective-permute-start(bf16[128,576]{1,0:T(8,128)(2,1)S(1)} %copy.63.refs_0_), channel_id=1, source_target_pairs={{0,64},{8,72},{2,66},{10,74},{4,68},{12,76},{6,70},{14,78},{16,80}... | collective-permute-start | bytes 442376 | tf_op jit(solution)/shard_map/ppermute | solution.py:188
  8.6 38.0 %all-to-all-start = ((f32[8,17,512]{2,1,0:T(8,128)}), f32[8,17,512]{2,1,0:T(8,128)}, u32[]{:S(2)}, u32[]{:S(2)}) async-start(f32[8,17,512]{2,1,0:T(8,128)} %pad_maximum_fusion.1), calls=%async_computation | async-start | bytes 786432 | tf_op jit(solution)/shard_map/all_to_all | solution.py:269
  46.6 22.0 %all-to-all-start.1 = ((bf16[8,16,4096]{2,1,0:T(8,128)(2,1)}), bf16[8,16,4096]{2,1,0:T(8,128)(2,1)S(1)}, u32[]{:S(2)}, u32[]{:S(2)}) async-start(bf16[8,16,4096]{2,1,0:T(8,128)(2,1)} %bitcast.24), calls=%async_computation.1 | async-start | bytes 2097152 | tf_op jit(solution)/shard_map/all_to_all | solution.py:302
  101.7 26.0 %collective-permute-start.17 = (bf16[128,4224]{1,0:T(8,128)(2,1)}, bf16[128,4224]{1,0:T(8,128)(2,1)S(1)}, u32[]{:S(2)}, u32[]{:S(2)}) collective-permute-start(bf16[128,4224]{1,0:T(8,128)(2,1)} %get-tuple-element.68.refs_2_.refs_6_), channel_id=1, source_target_pairs={{0,48},{8,56},{2,50},{10,58},{4,52},{12,60},{6,54},{14,62},{16,0},... | collective-permute-start | bytes 3244040 | tf_op jit(solution)/shard_map/ppermute | solution.py:37
  102.7 26.9 %collective-permute-start.15 = (bf16[128,4224]{1,0:T(8,128)(2,1)}, bf16[128,4224]{1,0:T(8,128)(2,1)S(1)}, u32[]{:S(2)}, u32[]{:S(2)}) collective-permute-start(bf16[128,4224]{1,0:T(8,128)(2,1)} %get-tuple-element.68.refs_2_.refs_6_), channel_id=1, source_target_pairs={{0,16},{8,24},{2,18},{10,26},{4,20},{12,28},{6,22},{14,30},{16,32}... | collective-permute-start | bytes 3244040 | tf_op jit(solution)/shard_map/ppermute | solution.py:37
  103.7 25.9 %collective-permute-start.18 = (bf16[128,4224]{1,0:T(8,128)(2,1)}, bf16[128,4224]{1,0:T(8,128)(2,1)S(1)}, u32[]{:S(2)}, u32[]{:S(2)}) collective-permute-start(bf16[128,4224]{1,0:T(8,128)(2,1)} %get-tuple-element.69.refs_3_.refs_7_), channel_id=1, source_target_pairs={{0,6},{8,14},{2,0},{10,8},{4,2},{12,10},{6,4},{14,12},{16,22},{24,... | collective-permute-start | bytes 3244040 | tf_op jit(solution)/shard_map/ppermute | solution.py:37
  106.6 27.4 %collective-permute-start.16 = (bf16[128,4224]{1,0:T(8,128)(2,1)}, bf16[128,4224]{1,0:T(8,128)(2,1)}, u32[]{:S(2)}, u32[]{:S(2)}) collective-permute-start(bf16[128,4224]{1,0:T(8,128)(2,1)} %get-tuple-element.69.refs_3_.refs_7_), channel_id=1, source_target_pairs={{0,2},{8,10},{2,4},{10,12},{4,6},{12,14},{6,0},{14,8},{16,18},{24,... | collective-permute-start | bytes 3244040 | tf_op jit(solution)/shard_map/ppermute | solution.py:37
  136.1 19.4 %collective-permute-start.24 = (bf16[64,4224]{1,0:T(8,128)(2,1)S(1)}, bf16[64,4224]{1,0:T(8,128)(2,1)S(1)}, u32[]{:S(2)}, u32[]{:S(2)}) collective-permute-start(bf16[64,4224]{1,0:T(8,128)(2,1)S(1)} %slice.75), channel_id=1, source_target_pairs={{0,2},{8,10},{2,4},{10,12},{4,6},{12,14},{6,0},{14,8},{16,18},{24,... | collective-permute-start | bytes 1622024 | tf_op jit(solution)/shard_map/ppermute | solution.py:37
  136.2 19.3 %collective-permute-start.22 = (bf16[64,4224]{1,0:T(8,128)(2,1)S(1)}, bf16[64,4224]{1,0:T(8,128)(2,1)S(1)}, u32[]{:S(2)}, u32[]{:S(2)}) collective-permute-start(bf16[64,4224]{1,0:T(8,128)(2,1)S(1)} %slice.73), channel_id=1, source_target_pairs={{0,16},{8,24},{2,18},{10,26},{4,20},{12,28},{6,22},{14,30},{16,32}... | collective-permute-start | bytes 1622024 | tf_op jit(solution)/shard_map/ppermute | solution.py:37
  136.3 19.3 %collective-permute-start.25 = (bf16[64,4224]{1,0:T(8,128)(2,1)S(1)}, bf16[64,4224]{1,0:T(8,128)(2,1)S(1)}, u32[]{:S(2)}, u32[]{:S(2)}) collective-permute-start(bf16[64,4224]{1,0:T(8,128)(2,1)S(1)} %slice.76), channel_id=1, source_target_pairs={{0,6},{8,14},{2,0},{10,8},{4,2},{12,10},{6,4},{14,12},{16,22},{24,... | collective-permute-start | bytes 1622024 | tf_op jit(solution)/shard_map/ppermute | solution.py:37
  139.4 16.1 %collective-permute-start.23 = (bf16[64,4224]{1,0:T(8,128)(2,1)S(1)}, bf16[64,4224]{1,0:T(8,128)(2,1)S(1)}, u32[]{:S(2)}, u32[]{:S(2)}) collective-permute-start(bf16[64,4224]{1,0:T(8,128)(2,1)S(1)} %slice.74), channel_id=1, source_target_pairs={{0,48},{8,56},{2,50},{10,58},{4,52},{12,60},{6,54},{14,62},{16,0},... | collective-permute-start | bytes 1622024 | tf_op jit(solution)/shard_map/ppermute | solution.py:37
  171.3 26.0 %collective-permute-start.28 = (bf16[128,4096]{1,0:T(8,128)(2,1)}, bf16[128,4096]{1,0:T(8,128)(2,1)S(1)}, u32[]{:S(2)}, u32[]{:S(2)}) collective-permute-start(bf16[128,4096]{1,0:T(8,128)(2,1)} %get-tuple-element.86), channel_id=1, source_target_pairs={{0,8},{8,0},{2,10},{10,2},{4,12},{12,4},{6,14},{14,6},{16,24},{24,... | collective-permute-start | bytes 3145736 | tf_op jit(solution)/shard_map/ppermute | solution.py:37
  176.1 19.6 %collective-permute-start.34 = (bf16[64,4096]{1,0:T(8,128)(2,1)S(1)}, bf16[64,4096]{1,0:T(8,128)(2,1)S(1)}, u32[]{:S(2)}, u32[]{:S(2)}) collective-permute-start(bf16[64,4096]{1,0:T(8,128)(2,1)S(1)} %add_convert_fusion.9), channel_id=1, source_target_pairs={{0,16},{8,24},{2,18},{10,26},{4,20},{12,28},{6,22},{14,30},{16,32}... | collective-permute-start | bytes 1572872 | tf_op jit(solution)/shard_map/ppermute | solution.py:37
  177.0 18.7 %collective-permute-start.36 = (bf16[64,4096]{1,0:T(8,128)(2,1)S(1)}, bf16[64,4096]{1,0:T(8,128)(2,1)}, u32[]{:S(2)}, u32[]{:S(2)}) collective-permute-start(bf16[64,4096]{1,0:T(8,128)(2,1)S(1)} %add_convert_fusion.8), channel_id=1, source_target_pairs={{0,48},{8,56},{2,50},{10,58},{4,52},{12,60},{6,54},{14,62},{16,0},... | collective-permute-start | bytes 1572872 | tf_op jit(solution)/shard_map/ppermute | solution.py:37
  181.2 15.1 %collective-permute-start.38 = (bf16[64,4096]{1,0:T(8,128)(2,1)}, bf16[64,4096]{1,0:T(8,128)(2,1)S(1)}, u32[]{:S(2)}, u32[]{:S(2)}) collective-permute-start(bf16[64,4096]{1,0:T(8,128)(2,1)} %add_convert_fusion.7), channel_id=1, source_target_pairs={{0,2},{8,10},{2,4},{10,12},{4,6},{12,14},{6,0},{14,8},{16,18},{24,... | collective-permute-start | bytes 1572872 | tf_op jit(solution)/shard_map/ppermute | solution.py:37
  181.5 14.8 %collective-permute-start.40 = (bf16[64,4096]{1,0:T(8,128)(2,1)}, bf16[64,4096]{1,0:T(8,128)(2,1)S(1)}, u32[]{:S(2)}, u32[]{:S(2)}) collective-permute-start(bf16[64,4096]{1,0:T(8,128)(2,1)} %add_convert_fusion.6), channel_id=1, source_target_pairs={{0,6},{8,14},{2,0},{10,8},{4,2},{12,10},{6,4},{14,12},{16,22},{24,... | collective-permute-start | bytes 1572872 | tf_op jit(solution)/shard_map/ppermute | solution.py:37
  196.9 36.8 %collective-permute-start.50 = (bf16[128,4096]{1,0:T(8,128)(2,1)S(1)}, bf16[128,4096]{1,0:T(8,128)(2,1)S(1)}, u32[]{:S(2)}, u32[]{:S(2)}) collective-permute-start(bf16[128,4096]{1,0:T(8,128)(2,1)S(1)} %copy-done.7), channel_id=1, source_target_pairs={{0,8},{8,0},{2,10},{10,2},{4,12},{12,4},{6,14},{14,6},{16,24},{24,... | collective-permute-start | bytes 3145736 | tf_op jit(solution)/shard_map/ppermute | solution.py:37
  198.8 25.2 %collective-permute-start.43 = (bf16[128,4096]{1,0:T(8,128)(2,1)S(1)}, bf16[128,4096]{1,0:T(8,128)(2,1)S(1)}, u32[]{:S(2)}, u32[]{:S(2)}) collective-permute-start(bf16[128,4096]{1,0:T(8,128)(2,1)S(1)} %add_convert_fusion.5), channel_id=1, source_target_pairs={{0,48},{8,56},{2,50},{10,58},{4,52},{12,60},{6,54},{14,62},{16,0},... | collective-permute-start | bytes 3145736 | tf_op jit(solution)/shard_map/ppermute | solution.py:37
  203.5 26.4 %collective-permute-start.45 = (bf16[128,4096]{1,0:T(8,128)(2,1)S(1)}, bf16[128,4096]{1,0:T(8,128)(2,1)S(1)}, u32[]{:S(2)}, u32[]{:S(2)}) collective-permute-start(bf16[128,4096]{1,0:T(8,128)(2,1)S(1)} %add_convert_fusion.4), channel_id=1, source_target_pairs={{0,16},{8,24},{2,18},{10,26},{4,20},{12,28},{6,22},{14,30},{16,32}... | collective-permute-start | bytes 3145736 | tf_op jit(solution)/shard_map/ppermute | solution.py:37
  205.0 29.6 %collective-permute-start.52 = (bf16[128,4096]{1,0:T(8,128)(2,1)S(1)}, bf16[128,4096]{1,0:T(8,128)(2,1)S(1)}, u32[]{:S(2)}, u32[]{:S(2)}) collective-permute-start(bf16[128,4096]{1,0:T(8,128)(2,1)S(1)} %add_convert_fusion.2), channel_id=1, source_target_pairs={{0,6},{8,14},{2,0},{10,8},{4,2},{12,10},{6,4},{14,12},{16,22},{24,... | collective-permute-start | bytes 3145736 | tf_op jit(solution)/shard_map/ppermute | solution.py:37
  208.3 26.3 %collective-permute-start.54 = (bf16[128,4096]{1,0:T(8,128)(2,1)S(1)}, bf16[128,4096]{1,0:T(8,128)(2,1)S(1)}, u32[]{:S(2)}, u32[]{:S(2)}) collective-permute-start(bf16[128,4096]{1,0:T(8,128)(2,1)S(1)} %add_convert_fusion.1), channel_id=1, source_target_pairs={{0,2},{8,10},{2,4},{10,12},{4,6},{12,14},{6,0},{14,8},{16,18},{24,... | collective-permute-start | bytes 3145736 | tf_op jit(solution)/shard_map/ppermute | solution.py:37
  230.7 13.7 %collective-permute-start.46 = (bf16[32,4096]{1,0:T(8,128)(2,1)S(1)}, bf16[32,4096]{1,0:T(8,128)(2,1)S(1)}, u32[]{:S(2)}, u32[]{:S(2)}) collective-permute-start(bf16[32,4096]{1,0:T(8,128)(2,1)S(1)} %get-tuple-element.129), channel_id=1, source_target_pairs={{0,6},{8,14},{2,0},{10,8},{4,2},{12,10},{6,4},{14,12},{16,22},{24,... | collective-permute-start | bytes 786440 | tf_op jit(solution)/shard_map/ppermute | solution.py:37
  233.7 14.1 %collective-permute-start.47 = (bf16[32,4096]{1,0:T(8,128)(2,1)S(1)}, bf16[32,4096]{1,0:T(8,128)(2,1)S(1)}, u32[]{:S(2)}, u32[]{:S(2)}) collective-permute-start(bf16[32,4096]{1,0:T(8,128)(2,1)S(1)} %get-tuple-element.131), channel_id=1, source_target_pairs={{0,2},{8,10},{2,4},{10,12},{4,6},{12,14},{6,0},{14,8},{16,18},{24,... | collective-permute-start | bytes 786440 | tf_op jit(solution)/shard_map/ppermute | solution.py:37
  235.4 14.0 %collective-permute-start.55 = (bf16[32,4096]{1,0:T(8,128)(2,1)S(1)}, bf16[32,4096]{1,0:T(8,128)(2,1)S(1)}, u32[]{:S(2)}, u32[]{:S(2)}) collective-permute-start(bf16[32,4096]{1,0:T(8,128)(2,1)S(1)} %get-tuple-element.132), channel_id=1, source_target_pairs={{0,48},{8,56},{2,50},{10,58},{4,52},{12,60},{6,54},{14,62},{16,0},... | collective-permute-start | bytes 786440 | tf_op jit(solution)/shard_map/ppermute | solution.py:37
  (57 other events, 453.1 us)

commit v5 on v4

--- a/solution.py
+++ b/solution.py
@@ -177,7 +177,7 @@
     return jnp.sum((positions[:, None] >= doc_ends[None, :]).astype(jnp.int32), axis=1)
 
 
-def attention(latent, query, w_uk, w_uv, doc_lengths):
+def attention(latent, query, w_uk, w_uv, doc_lengths, sent):
     tokens = latent.shape[0]
     heads = w_uk.shape[0]
     qk_width = NOPE + ROPE
@@ -200,7 +200,8 @@
         [(a, b) for a, b in table(dy=1, dc=1) if a >= 64 and a // 8 % 2 and a // 16 % 4 < 3],
     )
     (half,) = stack(blocks)
-    piece = jnp.concatenate([half, other_core(half), last], axis=0)
+    half, sent = lax.optimization_barrier((half, sent))
+    (piece,) = stack([half, other_core(half), last])
     starts = [place * tokens for place in places]
     starts += [(place + 1 - 2 * core) * tokens for place in places]
     seen = (x_hi > 0) & (core == 0) & (y > 0)
@@ -234,7 +235,7 @@
         .astype(jnp.bfloat16)
         .reshape(tokens, heads * VDIM)
     )
-    return head_out
+    return head_out, sent
 
 
 def body(
@@ -266,10 +267,6 @@
         ],
         axis=1,
     )
-    got = lax.all_to_all(sent, "exp", split_axis=0, concat_axis=0)
-    wide = jnp.transpose(got, (1, 0, 2)).reshape(own + 1, D)
-    residual_rows, gain = wide[:own], wide[own]
-
     own_routes = lax.dynamic_slice_in_dim(routes, exp * own, own, axis=0)
     own_gates = lax.dynamic_slice_in_dim(gate_weights, exp * own, own, axis=0)
     named = own_routes[:, :, None] == jnp.arange(EXPERTS, dtype=jnp.int32)[None, None, :]
@@ -286,18 +283,28 @@
     up = jnp.transpose(w_in, (0, 2, 1, 3))
     down = w_out.reshape(local_experts * units, D)
 
-    def own_and_theirs(groups):
-        theirs = [[other_core(block) for block in group] for group in groups]
-        return run_experts(theirs + groups, up, down, pick)
-
-    def both_cores(result):
-        half = len(result) // 2
+    def both_cores(blocks):
+        theirs = [other_core(block) for block in blocks]
+        result = run_experts([theirs] + [[block] for block in blocks], up, down, pick)
+        return result[1:], result[0]
+
+    def summed(result, extra=None):
+        here, there = result
+        back = other_core(there)
+        rows = here[0].shape[0]
         return [
-            add_up(here, other_core(there)).astype(jnp.bfloat16)
-            for there, here in zip(result[:half], result[half:])
+            add_up(
+                block,
+                back[i * rows : (i + 1) * rows],
+                *(() if extra is None else (extra[i],)),
+            ).astype(jnp.bfloat16)
+            for i, block in enumerate(here)
         ]
 
-    head_out = attention(latent, query, w_uk, w_uv, doc_lengths)
+    head_out, sent = attention(latent, query, w_uk, w_uv, doc_lengths, sent)
+    got = lax.all_to_all(sent, "exp", split_axis=0, concat_axis=0)
+    wide = jnp.transpose(got, (1, 0, 2)).reshape(own + 1, D)
+    residual_rows, gain = wide[:own], wide[own]
     partial = jnp.dot(head_out, w_o, preferred_element_type=jnp.float32).astype(jnp.bfloat16)
     parts = lax.all_to_all(
         partial.reshape(count_exp, own, D), "exp", split_axis=0, concat_axis=0
@@ -310,48 +317,51 @@
 
     x_own, x_before, x_after, x_far = ring(rows, "x")
     first, second = stack([x_own, x_before], [x_after, x_far])
-    first, second = stack(ring(first, "z"), ring(second, "y"))
-    near = first.shape[0] // 2
-    before, after = [], []
-    for block, axis in ((first, "y"), (second, "z")):
-        before.append([shift(block, axis, 1)])
-        after.append([shift(block, axis, -1)])
-    at_own = own_and_theirs([[first], [second]])
-    before, after, at_own = lax.optimization_barrier((before, after, at_own))
-    far = []
-    for i, axis in enumerate("yz"):
-        far.append([shift(before[i][0][:near], axis, 1)])
-        far.append([shift(after[i][0][near:], axis, -1)])
-    at_before = own_and_theirs(before)
-    far, at_before = lax.optimization_barrier((far, at_before))
-    at_far = own_and_theirs(far)
-    after, at_far = lax.optimization_barrier((after, at_far))
-    sum_far = both_cores(at_far)
-    passing = [
-        (shift(sum_far[2 * i], axis, 1), shift(sum_far[2 * i + 1], axis, -1))
-        for i, axis in enumerate("yz")
-    ]
-    passing, at_after = lax.optimization_barrier((passing, own_and_theirs(after)))
-    back_own, back_before, back_after = [
-        [other_core(there) for there in at[:2]] for at in (at_own, at_before, at_after)
-    ]
-    totals = []
-    for i, axis in enumerate("yz"):
-        for_after, for_before = passing[i]
-        low = jnp.pad(for_before, ((near, 0), (0, 0)))
-        high = jnp.pad(for_after, ((0, near), (0, 0)))
-        sum_before = add_up(at_before[2 + i], back_before[i], low).astype(jnp.bfloat16)
-        sum_after = add_up(at_after[2 + i], back_after[i], high).astype(jnp.bfloat16)
-        totals.append(
-            add_up(
-                at_own[2 + i], back_own[i], shift(sum_before, axis, -1), shift(sum_after, axis, 1)
-            ).astype(jnp.bfloat16)
-        )
-    first, second = totals
+    by_z, by_y = ring(first, "z"), ring(second, "y")
+    halves = stack(by_z[:2], by_z[2:], by_y[:2], by_y[2:])
+    y_low, y_high, z_low, z_high = halves
+
+    def near(low, high, axis):
+        return [shift(low, axis, 1), shift(high, axis, -1)]
+
+    near_a = near(y_low, y_high, "y") + near(z_low, z_high, "z")
+    near_a, at_own = lax.optimization_barrier((near_a, both_cores(halves)))
+    far = near(*near_a[:2], "y") + near(*near_a[2:], "z")
+    far, at_a = lax.optimization_barrier((far, both_cores(near_a)))
+    halves, far = lax.optimization_barrier((halves, far))
+    y_low, y_high, z_low, z_high = halves
+    near_b = near(y_high, y_low, "y") + near(z_high, z_low, "z")
+    near_b, at_far = lax.optimization_barrier((near_b, both_cores(far)))
+    sum_far = summed(at_far)
+    passing = near(*sum_far[:2], "y") + near(*sum_far[2:], "z")
+    passing, at_b = lax.optimization_barrier((passing, both_cores(near_b)))
+    sum_a = summed(at_a)
+    back_a = near(sum_a[1], sum_a[0], "y") + near(sum_a[3], sum_a[2], "z")
+    sum_b = summed(at_b, [passing[1], passing[0], passing[3], passing[2]])
+    back_b = near(sum_b[1], sum_b[0], "y") + near(sum_b[3], sum_b[2], "z")
+    own_here, own_there = at_own
+    own_back = other_core(own_there)
+    rows = 4 * own
     pair = 2 * own
-    first = ring_sum(*[first[i * pair : (i + 1) * pair] for i in range(4)], "z")
-    second = ring_sum(*[second[i * pair : (i + 1) * pair] for i in range(4)], "y")
-    first, second = first.astype(jnp.bfloat16), second.astype(jnp.bfloat16)
+
+    def final(i, k, *arrived):
+        part = slice(k * pair, (k + 1) * pair)
+        return add_up(
+            own_here[i][part],
+            own_back[i * rows : (i + 1) * rows][part],
+            *[block[part] for block in arrived],
+        ).astype(jnp.bfloat16)
+
+    sums = []
+    for i in range(4):
+        at = i // 2 * 2
+        if i % 2 == 0:
+            arrived = (back_a[at + 1], back_b[at])
+        else:
+            arrived = (back_a[at], back_b[at + 1])
+        sums += [final(i, k, *arrived) for k in range(2)]
+    first = ring_sum(*sums[:4], "z").astype(jnp.bfloat16)
+    second = ring_sum(*sums[4:], "y").astype(jnp.bfloat16)
     moe_out = ring_sum(first[:own], first[own:], second[:own], second[own:], "x")
     mixed = (hidden + moe_out).astype(jnp.bfloat16)
     return lax.all_to_all(mixed, "exp", split_axis=1, concat_axis=0, tiled=True)

time: 276 us -> 284 us (1.029)
  starting transfers between devices: 71.8 us -> 99.7 us
  waiting for transfers between devices: 92.5 us -> 74.2 us
  local copies, waits for them, and re-layouts: 23.5 us -> 27.5 us
    ppermute x58 -> x66, starting transfers between devices: 54.8 us -> 82.3 us  [shift(): return lax.ppermute(value, BOTH, table(**{'d' + axis: by}))]
    ppermute x58 -> x66, waiting for transfers between devices: 85.2 us -> 65.2 us  [shift(): return lax.ppermute(value, BOTH, table(**{'d' + axis: by}))]
    unnamed x43 -> x47, local copies, waits for them, and re-layouts: 16.2 us -> 21.8 us
    convert_element_type x12 -> x6, other arithmetic: 6.04 us -> 5.65 us  [the longest x3 4.15 us: summed(): return [add_up(block, back[i * rows:(i + 1) * rows], *(() if extra is Non...]
  transfers between devices with their start and end apart: 62 -> 70, of which waited for: 33 -> 25; matrix products, arithmetic and copies ran while one was open for 14% -> 13% of each run, Pallas kernels for 12% -> 16%
where the time goes in v5:
time: 284 us; the launch traced here: 280 us
  starting transfers between devices  99.7 us (35%)
  waiting for transfers between devices  74.2 us (26%)
  Pallas kernels  45.7 us (16%)
  local copies, waits for them, and re-layouts  27.5 us (10%)
  other arithmetic  13.7 us (5%)
  matrix products  9.51 us (3%)
  blocking collectives  9.08 us (3%)
    ppermute x66, starting transfers between devices, shift(): return lax.ppermute(value, BOTH, table(**{'d' + axis: by}))  82.3 us
    ppermute x66, waiting for transfers between devices, shift(): return lax.ppermute(value, BOTH, table(**{'d' + axis: by}))  65.2 us
    pallas_call x4, Pallas kernels, run_experts(): pl.pallas_call(functools.partial(experts_kernel, sizes), grid=(2 * STEPS,...  44.7 us
    unnamed x47, local copies, waits for them, and re-layouts  21.8 us
    all_to_all x1, blocking collectives, body(): return lax.all_to_all(mixed, 'exp', split_axis=1, concat_axis=0, tiled=True)  9.08 us
    all_to_all x1, waiting for transfers between devices, body(): lax.all_to_all(partial.reshape(count_exp, own, D), 'exp', split_axis=0, c...  6.66 us
    all_to_all x1, starting transfers between devices, body(): got = lax.all_to_all(sent, 'exp', split_axis=0, concat_axis=0)  6.05 us
    all_to_all x1, starting transfers between devices, body(): lax.all_to_all(partial.reshape(count_exp, own, D), 'exp', split_axis=0, c...  5.71 us
  transfers between devices with their start and end apart: 70, of which 25 were waited for; matrix products, arithmetic and copies ran while one was open for 13% of the time, Pallas kernels for 16%

profile of v5, /device:TPU:0, one launch (start us, length us, event | category | flops | bytes accessed | tf_op | source)
XLA Modules:
  0.0 280.4 jit_solution(4550600926689622371)
XLA Ops:
  1.2 5.0 %collective-permute-start = (bf16[128,576]{1,0:T(8,128)(2,1)S(1)}, bf16[128,576]{1,0:T(8,128)(2,1)S(1)}, u32[]{:S(2)}, u32[]{:S(2)}) collective-permute-start(bf16[128,576]{1,0:T(8,128)(2,1)S(1)} %copy.59.refs_0_), channel_id=1, source_target_pairs={{0,64},{8,72},{2,66},{10,74},{4,68},{12,76},{6,70},{14,78},{16,80}... | collective-permute-start | bytes 442376 | tf_op jit(solution)/shard_map/ppermute | solution.py:188
  26.7 6.1 %all-to-all-start = ((f32[8,17,512]{2,1,0:T(8,128)}), f32[8,17,512]{2,1,0:T(8,128)}, u32[]{:S(2)}, u32[]{:S(2)}) async-start(f32[8,17,512]{2,1,0:T(8,128)} %pad_maximum_fusion.1), calls=%async_computation | async-start | bytes 786432 | tf_op jit(solution)/shard_map/all_to_all | solution.py:305
  34.5 3.2 %fusion = (f32[1024]{0:T(1024)S(1)}, f32[1024,1408]{1,0:T(8,128)S(1)}) fusion(s32[1408]{0:T(1024)S(1)} %add_bitcast_fusion, s32[1408]{0:T(1024)S(1)} %convert_reduce_fusion.1, s32[1024]{0:T(1024)S(1)} %get-tuple-element.187, s32[1024]{0:T(1024)S(1)} %get-tuple-element.188, bf16[1024,576]{1,0:T(8,128)(2,1)S(1)} %bitcast.73, bf16[1408,576]{1,0:T(8,128)(2,1)S(1)} %shard_map.119), kind=kOutput, calls=%fused_computation.4 | convolution fusion | flops 1669594112 | bytes 8592384 | tf_op jit(solution)/shard_map/dot_general | solution.py:224
  45.0 5.7 %all-to-all-start.1 = ((bf16[8,16,4096]{2,1,0:T(8,128)(2,1)}), bf16[8,16,4096]{2,1,0:T(8,128)(2,1)S(1)}, u32[]{:S(2)}, u32[]{:S(2)}) async-start(bf16[8,16,4096]{2,1,0:T(8,128)(2,1)} %bitcast.24), calls=%async_computation.1 | async-start | bytes 2097152 | tf_op jit(solution)/shard_map/all_to_all | solution.py:309
  50.8 7.8 %copy.81 = bf16[2,4096,2,256]{3,1,2,0:T(8,128)(2,1)} copy(bf16[2,4096,2,256]{3,2,1,0:T(2,128)(2,1)} %param.19) | data formatting | bytes 16777216 | tf_op args[7]
  60.0 6.7 %all-to-all-done.1 = bf16[8,16,4096]{2,1,0:T(8,128)(2,1)S(1)} async-done(((bf16[8,16,4096]{2,1,0:T(8,128)(2,1)}), bf16[8,16,4096]{2,1,0:T(8,128)(2,1)S(1)}, u32[]{:S(2)}, u32[]{:S(2)}) %all-to-all-start.1) | async-done | bytes 1048608 | tf_op jit(solution)/shard_map/all_to_all | solution.py:309
  68.9 4.0 %collective-permute-start.7 = (bf16[16,4224]{1,0:T(8,128)(2,1)S(1)}, bf16[16,4224]{1,0:T(8,128)(2,1)S(1)}, u32[]{:S(2)}, u32[]{:S(2)}) collective-permute-start(bf16[16,4224]{1,0:T(8,128)(2,1)S(1)} %concatenate.11.refs_0_), channel_id=1, source_target_pairs={{0,65},{8,73},{2,67},{10,75},{4,69},{12,77},{6,71},{14,79},{16,81}... | collective-permute-start | bytes 405512 | tf_op jit(solution)/shard_map/ppermute | solution.py:37
  77.8 3.2 %collective-permute-done.8.refs_3_ = bf16[16,4224]{1,0:T(8,128)(2,1)S(1)} collective-permute-done((bf16[16,4224]{1,0:T(8,128)(2,1)S(1)}, bf16[16,4224]{1,0:T(8,128)(2,1)S(1)}, u32[]{:S(2)}, u32[]{:S(2)}) %collective-permute-start.8) | collective-permute-done | bytes 135200 | tf_op jit(solution)/shard_map/ppermute | solution.py:37
  90.9 4.8 %collective-permute-start.9 = (bf16[32,4224]{1,0:T(8,128)(2,1)S(1)}, bf16[32,4224]{1,0:T(8,128)(2,1)S(1)}, u32[]{:S(2)}, u32[]{:S(2)}) collective-permute-start(bf16[32,4224]{1,0:T(8,128)(2,1)S(1)} %get-tuple-element.82.refs_0_), channel_id=1, source_target_pairs={{0,2},{8,10},{2,4},{10,12},{4,6},{12,14},{6,0},{14,8},{16,18},{24,... | collective-permute-start | bytes 811016 | tf_op jit(solution)/shard_map/ppermute | solution.py:37
  115.7 11.1 %shard_map.122 = (bf16[256,4096]{1,0:T(8,128)(2,1)S(1)}, bf16[64,4096]{1,0:T(8,128)(2,1)S(1)}, bf16[64,4096]{1,0:T(8,128)(2,1)S(1)}, bf16[64,4096]{1,0:T(8,128)(2,1)S(1)}, bf16[64,4096]{1,0:T(8,128)(2,1)S(1)}) custom-call(bf16[64,4224]{1,0:T(8,128)(2,1)S(1)} %copy-done.5, bf16[64,4224]{1,0:T(8,128)(2,1)S(1)} %copy-done.7, bf16[64,4224]{1,0:T(8,128)(2,1)S(1)} %copy-done.9, ...), custom_call_target="tpu_custom_call" | custom-call | bytes 4096 | tf_op jit(solution)/shard_map/pallas_call | solution.py:153
  136.7 11.3 %shard_map.123 = (bf16[256,4096]{1,0:T(8,128)(2,1)S(1)}, bf16[64,4096]{1,0:T(8,128)(2,1)S(1)}, bf16[64,4096]{1,0:T(8,128)(2,1)S(1)}, bf16[64,4096]{1,0:T(8,128)(2,1)S(1)}, bf16[64,4096]{1,0:T(8,128)(2,1)S(1)}) custom-call(bf16[64,4224]{1,0:T(8,128)(2,1)S(1)} %collective-permute-done.28.refs_0_.refs_8_, ...), custom_call_target="tpu_custom_call" | custom-call | bytes 4096 | tf_op jit(solution)/shard_map/pallas_call | solution.py:153
  156.4 11.1 %shard_map.124 = (bf16[256,4096]{1,0:T(8,128)(2,1)S(1)}, bf16[64,4096]{1,0:T(8,128)(2,1)S(1)}, bf16[64,4096]{1,0:T(8,128)(2,1)S(1)}, bf16[64,4096]{1,0:T(8,128)(2,1)S(1)}, bf16[64,4096]{1,0:T(8,128)(2,1)S(1)}) custom-call(bf16[64,4224]{1,0:T(8,128)(2,1)S(1)} %collective-permute-done.38.refs_0_.refs_8_, ...), custom_call_target="tpu_custom_call" | custom-call | bytes 4096 | tf_op jit(solution)/shard_map/pallas_call | solution.py:153
  169.2 6.1 %collective-permute-done.42 = bf16[256,4096]{1,0:T(8,128)(2,1)S(1)} collective-permute-done((bf16[256,4096]{1,0:T(8,128)(2,1)S(1)}, bf16[256,4096]{1,0:T(8,128)(2,1)S(1)}, u32[]{:S(2)}, u32[]{:S(2)}) %collective-permute-start.42) | collective-permute-done | bytes 2097184 | tf_op jit(solution)/shard_map/ppermute | solution.py:37
  176.9 3.0 %collective-permute-start.44 = (bf16[64,4096]{1,0:T(8,128)(2,1)S(1)}, bf16[64,4096]{1,0:T(8,128)(2,1)S(1)}, u32[]{:S(2)}, u32[]{:S(2)}) collective-permute-start(bf16[64,4096]{1,0:T(8,128)(2,1)S(1)} %get-tuple-element.176), channel_id=1, source_target_pairs={{0,48},{8,56},{2,50},{10,58},{4,52},{12,60},{6,54},{14,62},{16,0},... | collective-permute-start | bytes 1572872 | tf_op jit(solution)/shard_map/ppermute | solution.py:37
  183.2 11.1 %shard_map.125 = (bf16[256,4096]{1,0:T(8,128)(2,1)S(1)}, bf16[64,4096]{1,0:T(8,128)(2,1)S(1)}, bf16[64,4096]{1,0:T(8,128)(2,1)S(1)}, bf16[64,4096]{1,0:T(8,128)(2,1)S(1)}, bf16[64,4096]{1,0:T(8,128)(2,1)S(1)}) custom-call(bf16[64,4224]{1,0:T(8,128)(2,1)S(1)} %collective-permute-done.47.refs_0_.refs_8_, ...), custom_call_target="tpu_custom_call" | custom-call | bytes 4096 | tf_op jit(solution)/shard_map/pallas_call | solution.py:153
  204.0 3.2 %collective-permute-start.55 = (bf16[64,4096]{1,0:T(8,128)(2,1)S(1)}, bf16[64,4096]{1,0:T(8,128)(2,1)S(1)}, u32[]{:S(2)}, u32[]{:S(2)}) collective-permute-start(bf16[64,4096]{1,0:T(8,128)(2,1)S(1)} %get-tuple-element.173), channel_id=1, source_target_pairs={{0,48},{8,56},{2,50},{10,58},{4,52},{12,60},{6,54},{14,62},{16,0},... | collective-permute-start | bytes 1572872 | tf_op jit(solution)/shard_map/ppermute | solution.py:37
  207.2 5.3 %collective-permute-done.33 = bf16[64,4096]{1,0:T(8,128)(2,1)S(1)} collective-permute-done((bf16[64,4096]{1,0:T(8,128)(2,1)S(1)}, bf16[64,4096]{1,0:T(8,128)(2,1)S(1)}, u32[]{:S(2)}, u32[]{:S(2)}) %collective-permute-start.33) | collective-permute-done | bytes 524320 | tf_op jit(solution)/shard_map/ppermute | solution.py:37
  217.5 6.7 %collective-permute-done.52 = bf16[64,4096]{1,0:T(8,128)(2,1)S(1)} collective-permute-done((bf16[64,4096]{1,0:T(8,128)(2,1)S(1)}, bf16[64,4096]{1,0:T(8,128)(2,1)S(1)}, u32[]{:S(2)}, u32[]{:S(2)}) %collective-permute-start.52) | collective-permute-done | bytes 524320 | tf_op jit(solution)/shard_map/ppermute | solution.py:37
  224.2 4.4 %collective-permute-done.60 = bf16[64,4096]{1,0:T(8,128)(2,1)S(1)} collective-permute-done((bf16[64,4096]{1,0:T(8,128)(2,1)S(1)}, bf16[64,4096]{1,0:T(8,128)(2,1)S(1)}, u32[]{:S(2)}, u32[]{:S(2)}) %collective-permute-start.60) | collective-permute-done | bytes 524320 | tf_op jit(solution)/shard_map/ppermute | solution.py:37
  233.1 6.7 %collective-permute-done.62 = bf16[64,4096]{1,0:T(8,128)(2,1)S(1)} collective-permute-done((bf16[64,4096]{1,0:T(8,128)(2,1)S(1)}, bf16[64,4096]{1,0:T(8,128)(2,1)S(1)}, u32[]{:S(2)}, u32[]{:S(2)}) %collective-permute-start.62) | collective-permute-done | bytes 524320 | tf_op jit(solution)/shard_map/ppermute | solution.py:37
  241.4 3.1 %collective-permute-done.56 = bf16[32,4096]{1,0:T(8,128)(2,1)S(1)} collective-permute-done((bf16[32,4096]{1,0:T(8,128)(2,1)S(1)}, bf16[32,4096]{1,0:T(8,128)(2,1)S(1)}, u32[]{:S(2)}, u32[]{:S(2)}) %collective-permute-start.56) | collective-permute-done | bytes 262176 | tf_op jit(solution)/shard_map/ppermute | solution.py:37
  244.5 5.0 %collective-permute-done.57 = bf16[32,4096]{1,0:T(8,128)(2,1)S(1)} collective-permute-done((bf16[32,4096]{1,0:T(8,128)(2,1)S(1)}, bf16[32,4096]{1,0:T(8,128)(2,1)S(1)}, u32[]{:S(2)}, u32[]{:S(2)}) %collective-permute-start.57) | collective-permute-done | bytes 262176 | tf_op jit(solution)/shard_map/ppermute | solution.py:37
  255.3 7.0 %collective-permute-done.64 = bf16[32,4096]{1,0:T(8,128)(2,1)S(1)} collective-permute-done((bf16[32,4096]{1,0:T(8,128)(2,1)S(1)}, bf16[32,4096]{1,0:T(8,128)(2,1)S(1)}, u32[]{:S(2)}, u32[]{:S(2)}) %collective-permute-start.64) | collective-permute-done | bytes 262176 | tf_op jit(solution)/shard_map/ppermute | solution.py:37
  270.4 9.1 %all_to_all.29 = bf16[16,8,512]{2,0,1:T(8,128)(2,1)S(1)} all-to-all(bf16[16,8,512]{2,0,1:T(8,128)(2,1)S(1)} %bitcast.78), channel_id=1, replica_groups=mesh['ctx'=16,'exp'=8] {'exp'}, dimensions={1} | all-to-all | bytes 262144 | tf_op jit(solution)/shard_map/all_to_all | solution.py:367
  (220 shorter events, 128.8 us)
Async XLA Ops:
  26.7 18.3 %all-to-all-start = ((f32[8,17,512]{2,1,0:T(8,128)}), f32[8,17,512]{2,1,0:T(8,128)}, u32[]{:S(2)}, u32[]{:S(2)}) async-start(f32[8,17,512]{2,1,0:T(8,128)} %pad_maximum_fusion.1), calls=%async_computation | async-start | bytes 786432 | tf_op jit(solution)/shard_map/all_to_all | solution.py:305
  45.0 21.6 %all-to-all-start.1 = ((bf16[8,16,4096]{2,1,0:T(8,128)(2,1)}), bf16[8,16,4096]{2,1,0:T(8,128)(2,1)S(1)}, u32[]{:S(2)}, u32[]{:S(2)}) async-start(bf16[8,16,4096]{2,1,0:T(8,128)(2,1)} %bitcast.24), calls=%async_computation.1 | async-start | bytes 2097152 | tf_op jit(solution)/shard_map/all_to_all | solution.py:309
  101.4 27.7 %collective-permute-start.15 = (bf16[64,4224]{1,0:T(8,128)(2,1)S(1)}, bf16[64,4224]{1,0:T(8,128)(2,1)S(1)}, u32[]{:S(2)}, u32[]{:S(2)}) collective-permute-start(bf16[64,4224]{1,0:T(8,128)(2,1)S(1)} %get-tuple-element.112.refs_4_.refs_12_), channel_id=1, source_target_pairs={{0,16},{8,24},{2,18},{10,26},{4,20},{12,28},{6,22},{14,30},{16,32}... | collective-permute-start | bytes 1622024 | tf_op jit(solution)/shard_map/ppermute | solution.py:37
  104.8 24.4 %collective-permute-start.16 = (bf16[64,4224]{1,0:T(8,128)(2,1)S(1)}, bf16[64,4224]{1,0:T(8,128)(2,1)S(1)}, u32[]{:S(2)}, u32[]{:S(2)}) collective-permute-start(bf16[64,4224]{1,0:T(8,128)(2,1)S(1)} %get-tuple-element.111.refs_5_.refs_13_), channel_id=1, source_target_pairs={{0,48},{8,56},{2,50},{10,58},{4,52},{12,60},{6,54},{14,62},{16,0},... | collective-permute-start | bytes 1622024 | tf_op jit(solution)/shard_map/ppermute | solution.py:37
  106.3 22.8 %collective-permute-start.17 = (bf16[64,4224]{1,0:T(8,128)(2,1)S(1)}, bf16[64,4224]{1,0:T(8,128)(2,1)}, u32[]{:S(2)}, u32[]{:S(2)}) collective-permute-start(bf16[64,4224]{1,0:T(8,128)(2,1)S(1)} %get-tuple-element.114.refs_6_.refs_14_), channel_id=1, source_target_pairs={{0,2},{8,10},{2,4},{10,12},{4,6},{12,14},{6,0},{14,8},{16,18},{24,... | collective-permute-start | bytes 1622024 | tf_op jit(solution)/shard_map/ppermute | solution.py:37
  109.6 19.6 %collective-permute-start.18 = (bf16[64,4224]{1,0:T(8,128)(2,1)S(1)}, bf16[64,4224]{1,0:T(8,128)(2,1)}, u32[]{:S(2)}, u32[]{:S(2)}) collective-permute-start(bf16[64,4224]{1,0:T(8,128)(2,1)S(1)} %get-tuple-element.113.refs_7_.refs_15_), channel_id=1, source_target_pairs={{0,6},{8,14},{2,0},{10,8},{4,2},{12,10},{6,4},{14,12},{16,22},{24,... | collective-permute-start | bytes 1622024 | tf_op jit(solution)/shard_map/ppermute | solution.py:37
  129.8 18.2 %collective-permute-start.24 = (bf16[64,4224]{1,0:T(8,128)(2,1)S(1)}, bf16[64,4224]{1,0:T(8,128)(2,1)S(1)}, u32[]{:S(2)}, u32[]{:S(2)}) collective-permute-start(bf16[64,4224]{1,0:T(8,128)(2,1)S(1)} %collective-permute-done.15.refs_4_.refs_12_), channel_id=1, source_target_pairs={{0,16},{8,24},{2,18},{10,26},{4,20},{12,28},{6,22},{14,30},{16,32}... | collective-permute-start | bytes 1622024 | tf_op jit(solution)/shard_map/ppermute | solution.py:37
  131.3 16.7 %collective-permute-start.25 = (bf16[64,4224]{1,0:T(8,128)(2,1)S(1)}, bf16[64,4224]{1,0:T(8,128)(2,1)S(1)}, u32[]{:S(2)}, u32[]{:S(2)}) collective-permute-start(bf16[64,4224]{1,0:T(8,128)(2,1)S(1)} %collective-permute-done.16.refs_5_.refs_13_), channel_id=1, source_target_pairs={{0,48},{8,56},{2,50},{10,58},{4,52},{12,60},{6,54},{14,62},{16,0},... | collective-permute-start | bytes 1622024 | tf_op jit(solution)/shard_map/ppermute | solution.py:37
  133.2 15.7 %collective-permute-start.26 = (bf16[64,4224]{1,0:T(8,128)(2,1)}, bf16[64,4224]{1,0:T(8,128)(2,1)S(1)}, u32[]{:S(2)}, u32[]{:S(2)}) collective-permute-start(bf16[64,4224]{1,0:T(8,128)(2,1)} %collective-permute-done.17.refs_6_.refs_14_), channel_id=1, source_target_pairs={{0,2},{8,10},{2,4},{10,12},{4,6},{12,14},{6,0},{14,8},{16,18},{24,... | collective-permute-start | bytes 1622024 | tf_op jit(solution)/shard_map/ppermute | solution.py:37
  149.9 17.6 %collective-permute-start.34 = (bf16[64,4224]{1,0:T(8,128)(2,1)S(1)}, bf16[64,4224]{1,0:T(8,128)(2,1)S(1)}, u32[]{:S(2)}, u32[]{:S(2)}) collective-permute-start(bf16[64,4224]{1,0:T(8,128)(2,1)S(1)} %get-tuple-element.111.refs_5_.refs_13_), channel_id=1, source_target_pairs={{0,16},{8,24},{2,18},{10,26},{4,20},{12,28},{6,22},{14,30},{16,32}... | collective-permute-start | bytes 1622024 | tf_op jit(solution)/shard_map/ppermute | solution.py:37
  150.8 16.7 %collective-permute-start.35 = (bf16[64,4224]{1,0:T(8,128)(2,1)S(1)}, bf16[64,4224]{1,0:T(8,128)(2,1)S(1)}, u32[]{:S(2)}, u32[]{:S(2)}) collective-permute-start(bf16[64,4224]{1,0:T(8,128)(2,1)S(1)} %get-tuple-element.112.refs_4_.refs_12_), channel_id=1, source_target_pairs={{0,48},{8,56},{2,50},{10,58},{4,52},{12,60},{6,54},{14,62},{16,0},... | collective-permute-start | bytes 1622024 | tf_op jit(solution)/shard_map/ppermute | solution.py:37
  153.2 15.0 %collective-permute-start.36 = (bf16[64,4224]{1,0:T(8,128)(2,1)S(1)}, bf16[64,4224]{1,0:T(8,128)(2,1)S(1)}, u32[]{:S(2)}, u32[]{:S(2)}) collective-permute-start(bf16[64,4224]{1,0:T(8,128)(2,1)S(1)} %get-tuple-element.113.refs_7_.refs_15_), channel_id=1, source_target_pairs={{0,2},{8,10},{2,4},{10,12},{4,6},{12,14},{6,0},{14,8},{16,18},{24,... | collective-permute-start | bytes 1622024 | tf_op jit(solution)/shard_map/ppermute | solution.py:37
  168.2 27.2 %collective-permute-start.32 = (bf16[256,4096]{1,0:T(8,128)(2,1)}, bf16[256,4096]{1,0:T(8,128)(2,1)}, u32[]{:S(2)}, u32[]{:S(2)}) collective-permute-start(bf16[256,4096]{1,0:T(8,128)(2,1)} %copy-done.14), channel_id=1, source_target_pairs={{0,8},{8,0},{2,10},{10,2},{4,12},{12,4},{6,14},{14,6},{16,24},{24,... | collective-permute-start | bytes 6291464 | tf_op jit(solution)/shard_map/ppermute | solution.py:37
  176.6 17.7 %collective-permute-start.43 = (bf16[64,4096]{1,0:T(8,128)(2,1)S(1)}, bf16[64,4096]{1,0:T(8,128)(2,1)S(1)}, u32[]{:S(2)}, u32[]{:S(2)}) collective-permute-start(bf16[64,4096]{1,0:T(8,128)(2,1)S(1)} %get-tuple-element.177), channel_id=1, source_target_pairs={{0,16},{8,24},{2,18},{10,26},{4,20},{12,28},{6,22},{14,30},{16,32}... | collective-permute-start | bytes 1572872 | tf_op jit(solution)/shard_map/ppermute | solution.py:37
  176.9 17.4 %collective-permute-start.44 = (bf16[64,4096]{1,0:T(8,128)(2,1)S(1)}, bf16[64,4096]{1,0:T(8,128)(2,1)S(1)}, u32[]{:S(2)}, u32[]{:S(2)}) collective-permute-start(bf16[64,4096]{1,0:T(8,128)(2,1)S(1)} %get-tuple-element.176), channel_id=1, source_target_pairs={{0,48},{8,56},{2,50},{10,58},{4,52},{12,60},{6,54},{14,62},{16,0},... | collective-permute-start | bytes 1572872 | tf_op jit(solution)/shard_map/ppermute | solution.py:37
  198.1 16.0 %collective-permute-start.54 = (bf16[64,4096]{1,0:T(8,128)(2,1)S(1)}, bf16[64,4096]{1,0:T(8,128)(2,1)S(1)}, u32[]{:S(2)}, u32[]{:S(2)}) collective-permute-start(bf16[64,4096]{1,0:T(8,128)(2,1)S(1)} %get-tuple-element.169), channel_id=1, source_target_pairs={{0,16},{8,24},{2,18},{10,26},{4,20},{12,28},{6,22},{14,30},{16,32}... | collective-permute-start | bytes 1572872 | tf_op jit(solution)/shard_map/ppermute | solution.py:37
  199.8 15.7 %collective-permute-start.59 = (bf16[64,4096]{1,0:T(8,128)(2,1)S(1)}, bf16[64,4096]{1,0:T(8,128)(2,1)S(1)}, u32[]{:S(2)}, u32[]{:S(2)}) collective-permute-start(bf16[64,4096]{1,0:T(8,128)(2,1)S(1)} %get-tuple-element.168), channel_id=1, source_target_pairs={{0,6},{8,14},{2,0},{10,8},{4,2},{12,10},{6,4},{14,12},{16,22},{24,... | collective-permute-start | bytes 1572872 | tf_op jit(solution)/shard_map/ppermute | solution.py:37
  203.9 20.3 %collective-permute-start.52 = (bf16[64,4096]{1,0:T(8,128)(2,1)S(1)}, bf16[64,4096]{1,0:T(8,128)(2,1)S(1)}, u32[]{:S(2)}, u32[]{:S(2)}) collective-permute-start(bf16[64,4096]{1,0:T(8,128)(2,1)S(1)} %get-tuple-element.170), channel_id=1, source_target_pairs={{0,16},{8,24},{2,18},{10,26},{4,20},{12,28},{6,22},{14,30},{16,32}... | collective-permute-start | bytes 1572872 | tf_op jit(solution)/shard_map/ppermute | solution.py:37
  204.0 20.2 %collective-permute-start.55 = (bf16[64,4096]{1,0:T(8,128)(2,1)S(1)}, bf16[64,4096]{1,0:T(8,128)(2,1)S(1)}, u32[]{:S(2)}, u32[]{:S(2)}) collective-permute-start(bf16[64,4096]{1,0:T(8,128)(2,1)S(1)} %get-tuple-element.173), channel_id=1, source_target_pairs={{0,48},{8,56},{2,50},{10,58},{4,52},{12,60},{6,54},{14,62},{16,0},... | collective-permute-start | bytes 1572872 | tf_op jit(solution)/shard_map/ppermute | solution.py:37
  212.5 16.1 %collective-permute-start.60 = (bf16[64,4096]{1,0:T(8,128)(2,1)S(1)}, bf16[64,4096]{1,0:T(8,128)(2,1)S(1)}, u32[]{:S(2)}, u32[]{:S(2)}) collective-permute-start(bf16[64,4096]{1,0:T(8,128)(2,1)S(1)} %get-tuple-element.172), channel_id=1, source_target_pairs={{0,2},{8,10},{2,4},{10,12},{4,6},{12,14},{6,0},{14,8},{16,18},{24,... | collective-permute-start | bytes 1572872 | tf_op jit(solution)/shard_map/ppermute | solution.py:37
  214.1 25.7 %collective-permute-start.62 = (bf16[64,4096]{1,0:T(8,128)(2,1)S(1)}, bf16[64,4096]{1,0:T(8,128)(2,1)S(1)}, u32[]{:S(2)}, u32[]{:S(2)}) collective-permute-start(bf16[64,4096]{1,0:T(8,128)(2,1)S(1)} %get-tuple-element.167), channel_id=1, source_target_pairs={{0,2},{8,10},{2,4},{10,12},{4,6},{12,14},{6,0},{14,8},{16,18},{24,... | collective-permute-start | bytes 1572872 | tf_op jit(solution)/shard_map/ppermute | solution.py:37
  215.5 25.9 %collective-permute-start.63 = (bf16[64,4096]{1,0:T(8,128)(2,1)S(1)}, bf16[64,4096]{1,0:T(8,128)(2,1)S(1)}, u32[]{:S(2)}, u32[]{:S(2)}) collective-permute-start(bf16[64,4096]{1,0:T(8,128)(2,1)S(1)} %get-tuple-element.171), channel_id=1, source_target_pairs={{0,6},{8,14},{2,0},{10,8},{4,2},{12,10},{6,4},{14,12},{16,22},{24,... | collective-permute-start | bytes 1572872 | tf_op jit(solution)/shard_map/ppermute | solution.py:37
  231.4 18.2 %collective-permute-start.57 = (bf16[32,4096]{1,0:T(8,128)(2,1)S(1)}, bf16[32,4096]{1,0:T(8,128)(2,1)S(1)}, u32[]{:S(2)}, u32[]{:S(2)}) collective-permute-start(bf16[32,4096]{1,0:T(8,128)(2,1)S(1)} %get-tuple-element.164), channel_id=1, source_target_pairs={{0,4},{8,12},{2,6},{10,14},{4,0},{12,8},{6,2},{14,10},{16,20},{24,... | collective-permute-start | bytes 786440 | tf_op jit(solution)/shard_map/ppermute | solution.py:37
  239.8 15.4 %collective-permute-start.61 = (bf16[32,4096]{1,0:T(8,128)(2,1)S(1)}, bf16[32,4096]{1,0:T(8,128)(2,1)S(1)}, u32[]{:S(2)}, u32[]{:S(2)}) collective-permute-start(bf16[32,4096]{1,0:T(8,128)(2,1)S(1)} %get-tuple-element.163), channel_id=1, source_target_pairs={{0,48},{8,56},{2,50},{10,58},{4,52},{12,60},{6,54},{14,62},{16,0},... | collective-permute-start | bytes 786440 | tf_op jit(solution)/shard_map/ppermute | solution.py:37
  (67 other events, 584.4 us)
